TPU v7x, 256 devices: a whole 4x4x8 slice. The times are simulated.
256 devices in a mesh: seq: 64 (over y, z_lo, x), fsdp: 4 (over z_hi, core).
Axes of the slice: x: 4, y: 4, z: 8 (z_hi: 2, z_lo: 4; z = z_hi * 4 + z_lo), core: 2. Of those that a mesh axis runs over, the one named last changes fastest.
Arguments:
- queries: bfloat16 [4, 128, 256, 1152], P('fsdp', 'seq'), may hold values from -36 to 36
- keys: bfloat16 [4, 128, 256, 1152], P('fsdp', 'seq'), may hold values from -5 to 5
- values: bfloat16 [4, 128, 256, 1152], P('fsdp', 'seq'), may hold values from -6 to 6
- cotangent: bfloat16 [4, 128, 256, 1152], P('fsdp', 'seq'), may hold values from -16 to 16
- out_weight: bfloat16 [1152, 1152], P('fsdp'), may hold values from -0.1875 to 0.1875
Outputs:
- output: bfloat16 [4, 128, 256, 1152], P('fsdp', 'seq')
- query_grad: bfloat16 [4, 128, 256, 1152], P('fsdp', 'seq')
- key_grad: bfloat16 [4, 128, 256, 1152], P('fsdp', 'seq')
- value_grad: bfloat16 [4, 128, 256, 1152], P('fsdp', 'seq')
- weight_grad: float32 [1152, 1152], P('fsdp', 'seq')
All inputs are finite; a program needn't handle non-finite values.
Results may differ from a plain program's by a relative error of at most 0.0058.
Values may be sent and summed in bfloat16 or wider, within the bound.
No kernel may reach another device: no remote copies, remote signals or barrier semaphores. Data moves between devices by JAX's collectives and lax.ppermute only.
A program may use at most 128 MiB of HBM per device.

v0:
```python
import functools

import jax
import jax.numpy as jnp
import numpy as np
from jax import lax
from jax.experimental import pallas as pl
from jax.experimental.pallas import tpu as pltpu
from jax.sharding import Mesh
from jax.sharding import PartitionSpec as P

HEADS = 16
HEAD_DIM = 72
D = 1152
SCALE = HEAD_DIM ** (-0.5)
LOG2E = 1.4426950408889634
MIB = 1024 * 1024
F32 = jnp.float32
BF16 = jnp.bfloat16
SEQ = ("y", "zl", "x")
ROWS = ("zh", "c")


def order_to_slabs(np_):
    size = 128 * np_
    out = np.zeros((size, size), np.float32)
    for s in range(16):
        for a in range(4):
            for f in range(2):
                for p in range(np_):
                    out[((s * 4 + a) * 2 + f) * np_ + p, ((a * 2 + f) * 16 + s) * np_ + p] = 1
    return out


def order_to_patches(np_):
    size = 128 * np_
    out = np.zeros((size, size), np.float32)
    for s in range(16):
        for a in range(4):
            for f in range(2):
                for p in range(np_):
                    out[((a * np_ + p) * 16 + s) * 2 + f, ((s * 4 + a) * 2 + f) * np_ + p] = 1
    return out


def const(matrix):
    return jnp.asarray(matrix, BF16)


def move(order, rows):
    return jnp.dot(order, rows, preferred_element_type=F32).astype(BF16)


def whole(shape):
    return pl.BlockSpec(shape, lambda i: (0,) * len(shape))


def params(mib):
    return pltpu.CompilerParams(vmem_limit_bytes=mib * MIB)


def in_vmem(count):
    return [pl.BlockSpec(memory_space=pltpu.VMEM)] * count


def pack_kernel(order_ref, q_ref, k_ref, v_ref, c_ref, out_ref):
    rows = [ref[0, f] for ref in (q_ref, k_ref, v_ref, c_ref) for f in range(2)]
    out_ref[...] = move(order_ref[...], jnp.concatenate(rows, axis=0)).reshape(16, 16, D)


def pack(arrays):
    return pl.pallas_call(
        pack_kernel,
        grid=(2, 4),
        in_specs=[pl.BlockSpec((256, 256), lambda i, g: (0, 0))]
        + [pl.BlockSpec((1, 2, 32, D), lambda i, g: (0, 0, 4 * i + g, 0))] * 4,
        out_specs=pl.BlockSpec((16, 16, D), lambda i, g: (g, i, 0)),
        out_shape=jax.ShapeDtypeStruct((64, 32, D), BF16),
        compiler_params=params(60),
        cost_estimate=pl.CostEstimate(
            flops=2 * 2048 * 256 * D, bytes_accessed=8192 * D, transcendentals=0
        ),
        name="pack",
    )(const(order_to_slabs(2)), *arrays)


def attend_part(part, order_ref, back_ref, r_ref, w_ref, s_ref, att_ref, cot_ref, x_ref, u_ref, y_ref):
    slots = pl.ds(pl.multiple_of(part * 16, 16), 16)
    mine = pl.ds(pl.multiple_of(part * 256, 256), 256)
    for b in range(4):
        t = r_ref[pl.ds(b * 16, 16), slots, :].reshape(256, D)
        t = move(order_ref[...], t)
        for a in range(4):
            for p in range(2):
                x_ref[a, pl.ds(p * 128 + b * 32, 32), :] = t[(a * 2 + p) * 32 : (a * 2 + p + 1) * 32]
    cot = x_ref[3]
    cot_ref[mine, :] = cot
    u_ref[...] = lax.dot_general(
        cot, w_ref[...], (((1,), (1,)), ((), ())), preferred_element_type=F32
    ).astype(BF16)
    y_ref[...] = jnp.zeros_like(y_ref)
    lane = lax.broadcasted_iota(jnp.int32, (1, 256), 1)
    for j in range(8):
        first = (lane >= 16 * j) & (lane < 16 * j + 72)
        second = (lane >= 16 * j + 72) & (lane < 16 * j + 144)
        keep_first = first.astype(F32).astype(BF16)
        keep_second = second.astype(F32).astype(BF16)
        win = pl.ds(128 * j, 256)

        def both(t):
            return jnp.concatenate([t * keep_first, t * keep_second], axis=0)

        def split(t):
            return jnp.where(first, t[:128], jnp.where(second, t[128:], 0.0)).astype(BF16)

        for p in range(2):
            rows = pl.ds(p * 128, 128)
            q = x_ref[0, rows, win]
            u = u_ref[rows, win]
            kk = both(x_ref[1, rows, win])
            vv = both(x_ref[2, rows, win])
            scores = lax.dot_general(kk, q, (((1,), (1,)), ((), ())), preferred_element_type=F32)
            scores = scores.reshape(2, 128, 128)
            top = jnp.max(scores, axis=1, keepdims=True)
            raised = jnp.exp2((scores - top) * (SCALE * LOG2E))
            prob = raised * (1.0 / jnp.sum(raised, axis=1, keepdims=True))
            low = prob.astype(BF16).reshape(256, 128)
            grad = lax.dot_general(vv, u, (((1,), (1,)), ((), ())), preferred_element_type=F32)
            grad = grad.reshape(2, 128, 128)
            centre = jnp.sum(prob * grad, axis=1, keepdims=True)
            sg = (prob * (grad - centre) * SCALE).astype(BF16).reshape(256, 128)
            y_ref[0, rows, win] += lax.dot_general(
                low, vv, (((0,), (0,)), ((), ())), preferred_element_type=F32
            ).astype(BF16)
            y_ref[1, rows, win] += lax.dot_general(
                sg, kk, (((0,), (0,)), ((), ())), preferred_element_type=F32
            ).astype(BF16)
            y_ref[2, rows, win] += split(jnp.dot(sg, q, preferred_element_type=F32))
            y_ref[3, rows, win] += split(jnp.dot(low, u, preferred_element_type=F32))
    att = y_ref[0]
    att_ref[mine, :] = att
    y_ref[0] = jnp.dot(att, w_ref[...], preferred_element_type=F32).astype(BF16)
    for b in range(4):
        t = jnp.concatenate(
            [y_ref[a, pl.ds(p * 128 + b * 32, 32), :] for a in range(4) for p in range(2)], axis=0
        )
        s_ref[pl.ds(b * 16, 16), slots, :] = move(back_ref[...], t).reshape(16, 16, D)


def attend_kernel(*refs):
    @pl.loop(0, 2)
    def _(part):
        attend_part(part, *refs)


def attend(received, weight):
    order = order_to_patches(2)
    return pl.pallas_call(
        attend_kernel,
        in_specs=in_vmem(4),
        out_specs=in_vmem(3),
        out_shape=[
            jax.ShapeDtypeStruct((64, 32, D), BF16),
            jax.ShapeDtypeStruct((512, D), BF16),
            jax.ShapeDtypeStruct((512, D), BF16),
        ],
        scratch_shapes=[
            pltpu.VMEM((4, 256, D), BF16),
            pltpu.VMEM((256, D), BF16),
            pltpu.VMEM((4, 256, D), BF16),
        ],
        compiler_params=params(24),
        cost_estimate=pl.CostEstimate(
            flops=12_000_000_000, bytes_accessed=40 * 256 * D + 2 * D * D, transcendentals=1048576
        ),
        name="attend",
    )(const(order), const(order.T.copy()), received, weight)


def unpack_kernel(order_ref, slabs_ref, *outs):
    t = move(order_ref[...], slabs_ref[...].reshape(256, D))
    for a in range(4):
        for f in range(2):
            at = (a * 2 + f) * 32
            outs[a][0, f] = t[at : at + 32]


def unpack(slabs):
    return pl.pallas_call(
        unpack_kernel,
        grid=(2, 4),
        in_specs=[
            pl.BlockSpec((256, 256), lambda i, g: (0, 0)),
            pl.BlockSpec((16, 16, D), lambda i, g: (g, i, 0)),
        ],
        out_specs=[pl.BlockSpec((1, 2, 32, D), lambda i, g: (0, 0, 4 * i + g, 0))] * 4,
        out_shape=[jax.ShapeDtypeStruct((1, 2, 256, D), BF16)] * 4,
        compiler_params=params(60),
        cost_estimate=pl.CostEstimate(
            flops=2 * 2048 * 256 * D, bytes_accessed=8192 * D, transcendentals=0
        ),
        name="unpack",
    )(const(order_to_slabs(2).T.copy()), slabs)


def outer_kernel(att_ref, cot_ref, mine_ref, theirs_ref):
    att = att_ref[...]
    cot = cot_ref[...]
    parts = [att[:, 288 * b : 288 * b + 288] for b in range(4)]
    even = jnp.concatenate([parts[0], parts[2]], axis=1)
    odd = jnp.concatenate([parts[1], parts[3]], axis=1)
    core = lax.axis_index("c")

    def product(t):
        return lax.dot_general(cot, t, (((0,), (0,)), ((), ())), preferred_element_type=F32)

    mine_ref[...] = product(jnp.where(core == 0, even, odd))
    theirs_ref[...] = product(jnp.where(core == 0, odd, even)).astype(theirs_ref.dtype)


def outer(att, cot):
    return pl.pallas_call(
        outer_kernel,
        in_specs=in_vmem(2),
        out_specs=in_vmem(2),
        out_shape=[jax.ShapeDtypeStruct((D, 576), F32), jax.ShapeDtypeStruct((D, 576), BF16)],
        compiler_params=params(24),
        cost_estimate=pl.CostEstimate(
            flops=2 * 512 * D * D, bytes_accessed=4 * 512 * D + 6 * D * 576, transcendentals=0
        ),
        name="outer",
    )(att, cot)


def halves_kernel(mine_ref, other_ref, own_ref, *out_refs):
    y = lax.axis_index("y")
    for k in range(4):
        rows = pl.ds(pl.multiple_of((y ^ k) * 288, 32), 288)
        total = mine_ref[rows, :] + other_ref[rows, :].astype(F32)
        if k == 0:
            own_ref[...] = total
        else:
            out_refs[k - 1][...] = total.astype(BF16)


def halves(mine, other):
    return pl.pallas_call(
        halves_kernel,
        in_specs=in_vmem(2),
        out_specs=in_vmem(4),
        out_shape=[jax.ShapeDtypeStruct((288, 576), F32)] + [jax.ShapeDtypeStruct((288, 576), BF16)] * 3,
        compiler_params=params(24),
        cost_estimate=pl.CostEstimate(flops=D * 576, bytes_accessed=10 * D * 576, transcendentals=0),
        name="halves",
    )(mine, other)


def swap(value, axis, k):
    size = 2 if axis in ("zh", "c") else 4
    return lax.ppermute(value, axis, [(i, i ^ k) for i in range(size)])


def sum_over(blocks, axis, size):
    at = lax.axis_index(axis)
    total = lax.dynamic_index_in_dim(blocks, at, 0, keepdims=False)
    for k in range(1, size):
        total = total + swap(lax.dynamic_index_in_dim(blocks, at ^ k, 0, keepdims=False), axis, k)
    return total


def weight_total(att, cot):
    mine, theirs = outer(att, cot)
    own, *sent = halves(mine, swap(theirs, "c", 1))
    total = own
    for k in range(1, 4):
        total = total + swap(sent[k - 1], "y", k).astype(F32)
    blocks = total.reshape(4, 4, 18, 576).transpose(1, 0, 2, 3)
    blocks = sum_over(blocks, "x", 4)
    blocks = sum_over(blocks, "zl", 4)
    blocks = blocks.reshape(18, 2, 288).transpose(1, 0, 2)
    return sum_over(blocks, "zh", 2).T


def by_rank(axis, own, other):
    first = lax.axis_index(axis) == 0
    return jnp.stack([jnp.where(first, own, other), jnp.where(first, other, own)])


def whole_weight(out_weight):
    place = lax.axis_index("y") * 4 + lax.axis_index("x")
    piece = lax.dynamic_index_in_dim(out_weight.reshape(16, 18, D), place, 0, keepdims=False)
    pair = by_rank("zh", piece, swap(piece, "zh", 1))
    rows = lax.all_gather(pair, ("y", "x"), axis=0, tiled=False)
    rows = rows.transpose(1, 0, 2, 3).reshape(2, 288, D)
    both = by_rank("c", rows, swap(rows, "c", 1))
    return both.transpose(1, 0, 2, 3).reshape(D, D)


def exchange(t):
    return lax.all_to_all(t, SEQ, split_axis=0, concat_axis=0, tiled=True)


def on_device(queries, keys, values, cotangent, out_weight):
    weight = whole_weight(out_weight)
    received = exchange(pack((queries, keys, values, cotangent)))
    sent, att, cot = attend(received, weight)
    weight_grad = weight_total(att, cot)
    return (*unpack(exchange(sent)), weight_grad)


def solution(mesh):
    fine = Mesh(mesh.devices.reshape(4, 4, 4, 2, 2), ("y", "zl", "x", "zh", "c"))
    frames = P(ROWS, SEQ, None, None)
    return jax.shard_map(
        on_device,
        mesh=fine,
        in_specs=(frames, frames, frames, frames, P(ROWS, None)),
        out_specs=(frames, frames, frames, frames, P(ROWS, SEQ)),
        check_vma=False,
    )
```

profile of v0, /device:TPU:2, one launch (start us, length us, event | category | flops | bytes accessed | tf_op | source)
XLA Modules:
  0.0 340.9 jit_solution(2091060277538201097)
XLA Ops:
  7.2 8.6 %pack.1 = bf16[64,32,1152]{2,1,0:T(8,128)(2,1)} custom-call(bf16[256,256]{1,0:T(8,128)(2,1)} %constant.68.clone.order_ref, bf16[1,2,256,1152]{3,2,1,0:T(8,128)(2,1)} %q_ref.1, bf16[1,2,256,1152]{3,2,1,0:T(8,128)(2,1)} %k_ref.1, bf16[1,2,256,1152]{3,2,1,0:T(8,128)(2,1)} %v_ref.1, bf16[1,2,256,1152]{3,2,1,0:T(8,128)(2,1)} %c_ref.1), custom_call_target="tpu_custom_call" | custom-call | flops 1207959552 | bytes 9437184 | tf_op jit(solution)/shard_map/pack/pallas_call | solution.py:72
  15.8 12.4 %all-to-all-start = ((bf16[64,32,1152]{2,1,0:T(8,128)(2,1)}), bf16[64,32,1152]{2,1,0:T(8,128)(2,1)}, u32[]{:S(2)}, u32[]{:S(2)}) async-start(bf16[64,32,1152]{2,1,0:T(8,128)(2,1)} %pack.1), calls=%async_computation | async-start | bytes 9437184 | tf_op jit(solution)/shard_map/all_to_all | solution.py:300
  28.5 4.6 %collective-permute-start = (bf16[18,1152]{1,0:T(8,128)(2,1)S(1)}, bf16[18,1152]{1,0:T(8,128)(2,1)S(1)}, u32[]{:S(2)}, u32[]{:S(2)}) collective-permute-start(bf16[18,1152]{1,0:T(8,128)(2,1)S(1)} %dynamic-slice_bitcast_fusion.6), channel_id=1, source_target_pairs={{0,2},{2,0},{1,3},{3,1},{4,6},{6,4},{5,7},{7,5},{8,10},{10,8},{9,1... | collective-permute-start | bytes 124424 | tf_op jit(solution)/shard_map/ppermute | solution.py:260
  33.1 77.9 %collective-permute-done = bf16[18,1152]{1,0:T(8,128)(2,1)S(1)} collective-permute-done((bf16[18,1152]{1,0:T(8,128)(2,1)S(1)}, bf16[18,1152]{1,0:T(8,128)(2,1)S(1)}, u32[]{:S(2)}, u32[]{:S(2)}) %collective-permute-start) | collective-permute-done | bytes 41504 | tf_op jit(solution)/shard_map/ppermute | solution.py:260
  111.6 48.7 %all-gather.3.cloned.1.call-done = bf16[32,18,1152]{2,1,0:T(8,128)(2,1)} async-done(((bf16[2,18,1152]{2,1,0:T(8,128)(2,1)}), bf16[32,18,1152]{2,1,0:T(8,128)(2,1)}) %all-gather.3.cloned.1.call-update) | async-done | bytes 1327120 | tf_op jit(solution)/shard_map/all_gather | solution.py:293
  160.3 2.5 copy.27
  163.0 3.0 collective-permute-done.1
  166.0 2.4 fusion
  168.4 3.8 %maximum_bitcast_fusion = bf16[2,2,288,1152]{3,0,2,1:T(2,128)(2,1)S(1)} fusion(bf16[1,2,288,1152]{3,1,2,0:T(2,128)(2,1)S(1)} %get-tuple-element.32, bf16[1,2,288,1152]{3,1,2,0:T(2,128)(2,1)S(1)} %get-tuple-element.31), kind=kLoop, calls=%fused_computation | loop fusion | flops 1327104 | bytes 5308416 | tf_op jit(solution)/shard_map/transpose | solution.py:296
  173.1 21.7 %attend.1 = (bf16[64,32,1152]{2,1,0:T(8,128)(2,1)S(1)}, bf16[512,1152]{1,0:T(8,128)(2,1)S(1)}, bf16[512,1152]{1,0:T(8,128)(2,1)S(1)}) custom-call(bf16[256,256]{1,0:T(8,128)(2,1)S(1)} %copy-done.3, bf16[256,256]{1,0:T(8,128)(2,1)S(1)} %copy-done.4, bf16[64,32,1152]{2,1,0:T(8,128)(2,1)} %all-to-all-done.refs_2_, bf16[1152,1152]{1,0:T(8,128)(2,1)S(1)} %bitcast.55), custom_call_target="tpu_custom_call" | custom-call | flops 12000000000 | bytes 14450688 | tf_op jit(solution)/shard_map/attend/pallas_call | solution.py:158
  199.1 9.8 %all-to-all-start.1 = ((bf16[64,32,1152]{2,1,0:T(8,128)(2,1)}), bf16[64,32,1152]{2,1,0:T(8,128)(2,1)}, u32[]{:S(2)}, u32[]{:S(2)}) async-start(bf16[64,32,1152]{2,1,0:T(8,128)(2,1)} %copy-done), calls=%async_computation.1 | async-start | bytes 9437184 | tf_op jit(solution)/shard_map/all_to_all | solution.py:300
  210.2 2.2 outer.1
  215.8 3.3 collective-permute-done.2
  223.9 2.9 collective-permute-start.4
  227.1 28.9 %collective-permute-done.3 = bf16[288,576]{1,0:T(8,128)(2,1)S(1)} collective-permute-done((bf16[288,576]{1,0:T(8,128)(2,1)S(1)}, bf16[288,576]{1,0:T(8,128)(2,1)S(1)}, u32[]{:S(2)}, u32[]{:S(2)}) %collective-permute-start.3) | collective-permute-done | bytes 331808 | tf_op jit(solution)/shard_map/ppermute | solution.py:260
  256.0 15.4 %collective-permute-done.4 = bf16[288,576]{1,0:T(8,128)(2,1)S(1)} collective-permute-done((bf16[288,576]{1,0:T(8,128)(2,1)S(1)}, bf16[288,576]{1,0:T(8,128)(2,1)S(1)}, u32[]{:S(2)}, u32[]{:S(2)}) %collective-permute-start.4) | collective-permute-done | bytes 331808 | tf_op jit(solution)/shard_map/ppermute | solution.py:260
  271.7 3.4 %collective-permute-start.6 = (f32[4,18,576]{2,1,0:T(8,128)S(1)}, f32[4,18,576]{2,1,0:T(8,128)S(1)}, u32[]{:S(2)}, u32[]{:S(2)}) collective-permute-start(f32[4,18,576]{2,1,0:T(8,128)S(1)} %get-tuple-element.33), channel_id=1, source_target_pairs={{0,4},{4,0},{8,12},{12,8},{1,5},{5,1},{9,13},{13,9},{2,6},{6,2},{1... | collective-permute-start | bytes 497672 | tf_op jit(solution)/shard_map/ppermute | solution.py:260
  276.7 8.3 %collective-permute-done.6 = f32[4,18,576]{2,1,0:T(8,128)S(1)} collective-permute-done((f32[4,18,576]{2,1,0:T(8,128)S(1)}, f32[4,18,576]{2,1,0:T(8,128)S(1)}, u32[]{:S(2)}, u32[]{:S(2)}) %collective-permute-start.6) | collective-permute-done | bytes 165920 | tf_op jit(solution)/shard_map/ppermute | solution.py:260
  285.0 8.3 %collective-permute-done.7 = f32[4,18,576]{2,1,0:T(8,128)S(1)} collective-permute-done((f32[4,18,576]{2,1,0:T(8,128)S(1)}, f32[4,18,576]{2,1,0:T(8,128)S(1)}, u32[]{:S(2)}, u32[]{:S(2)}) %collective-permute-start.7) | collective-permute-done | bytes 165920 | tf_op jit(solution)/shard_map/ppermute | solution.py:260
  294.8 9.4 %collective-permute-start.10 = (f32[18,576]{1,0:T(8,128)S(1)}, f32[18,576]{1,0:T(8,128)S(1)}, u32[]{:S(2)}, u32[]{:S(2)}) collective-permute-start(f32[18,576]{1,0:T(8,128)S(1)} %get-tuple-element.38), channel_id=1, source_target_pairs={{0,32},{16,48},{32,0},{48,16},{1,33},{17,49},{33,1},{49,17},{2,34}... | collective-permute-start | bytes 124424 | tf_op jit(solution)/shard_map/ppermute | solution.py:260
  304.8 12.6 %collective-permute-done.10 = f32[18,576]{1,0:T(8,128)S(1)} collective-permute-done((f32[18,576]{1,0:T(8,128)S(1)}, f32[18,576]{1,0:T(8,128)S(1)}, u32[]{:S(2)}, u32[]{:S(2)}) %collective-permute-start.10) | collective-permute-done | bytes 41504 | tf_op jit(solution)/shard_map/ppermute | solution.py:260
  317.6 3.1 collective-permute-start.12
  320.7 4.9 %collective-permute-done.12 = f32[18,288]{1,0:T(8,128)S(1)} collective-permute-done((f32[18,288]{1,0:T(8,128)S(1)}, f32[18,288]{1,0:T(8,128)S(1)}, u32[]{:S(2)}, u32[]{:S(2)}) %collective-permute-start.12) | collective-permute-done | bytes 20768 | tf_op jit(solution)/shard_map/ppermute | solution.py:260
  326.2 7.9 %unpack.1 = (bf16[1,2,256,1152]{3,2,1,0:T(8,128)(2,1)}, bf16[1,2,256,1152]{3,2,1,0:T(8,128)(2,1)}, bf16[1,2,256,1152]{3,2,1,0:T(8,128)(2,1)}, bf16[1,2,256,1152]{3,2,1,0:T(8,128)(2,1)}) custom-call(bf16[256,256]{1,0:T(8,128)(2,1)} %constant.71.clone.order_ref, bf16[64,32,1152]{2,1,0:T(8,128)(2,1)} %all-to-all-done.1.slabs_ref), custom_call_target="tpu_custom_call" | custom-call | flops 1207959552 | bytes 9437184 | tf_op jit(solution)/shard_map/unpack/pallas_call | solution.py:189
  (54 shorter events, 20.8 us)
Async XLA Ops:
  15.8 12.4 %copy-start.9 = (bf16[288,1152]{1,0:T(8,128)(2,1)S(1)}, bf16[288,1152]{1,0:T(8,128)(2,1)}, u32[]{:S(2)}) copy-start(bf16[288,1152]{1,0:T(8,128)(2,1)} %param.13) | copy-start | bytes 1990660
  15.8 156.7 %all-to-all-start = ((bf16[64,32,1152]{2,1,0:T(8,128)(2,1)}), bf16[64,32,1152]{2,1,0:T(8,128)(2,1)}, u32[]{:S(2)}, u32[]{:S(2)}) async-start(bf16[64,32,1152]{2,1,0:T(8,128)(2,1)} %pack.1), calls=%async_computation | async-start | bytes 9437184 | tf_op jit(solution)/shard_map/all_to_all | solution.py:300
  28.2 132.1 %all-gather.3.cloned.1.call-start = ((), (), s32[]{:S(2)}) async-start(), calls=%async_computation.2 | async-start | bytes 1880064 | tf_op jit(solution)/shard_map/all_gather | solution.py:293
  28.5 82.4 %collective-permute-start = (bf16[18,1152]{1,0:T(8,128)(2,1)S(1)}, bf16[18,1152]{1,0:T(8,128)(2,1)S(1)}, u32[]{:S(2)}, u32[]{:S(2)}) collective-permute-start(bf16[18,1152]{1,0:T(8,128)(2,1)S(1)} %dynamic-slice_bitcast_fusion.6), channel_id=1, source_target_pairs={{0,2},{2,0},{1,3},{3,1},{4,6},{6,4},{5,7},{7,5},{8,10},{10,8},{9,1... | collective-permute-start | bytes 124424 | tf_op jit(solution)/shard_map/ppermute | solution.py:260
  162.8 3.1 collective-permute-start.1
  194.9 2.2 copy-start
  197.0 1.0 copy-start.5
  198.1 1.0 copy-start.7
  199.1 9.8 %copy-start.6 = (bf16[512,1152]{1,0:T(8,128)(2,1)S(1)}, bf16[512,1152]{1,0:T(8,128)(2,1)}, u32[]{:S(2)}) copy-start(bf16[512,1152]{1,0:T(8,128)(2,1)} %copy-done.5) | copy-start | bytes 3538948
  199.1 127.2 %all-to-all-start.1 = ((bf16[64,32,1152]{2,1,0:T(8,128)(2,1)}), bf16[64,32,1152]{2,1,0:T(8,128)(2,1)}, u32[]{:S(2)}, u32[]{:S(2)}) async-start(bf16[64,32,1152]{2,1,0:T(8,128)(2,1)} %copy-done), calls=%async_computation.1 | async-start | bytes 9437184 | tf_op jit(solution)/shard_map/all_to_all | solution.py:300
  208.9 1.3 copy-start.8
  212.4 1.6 copy-start.1
  215.8 3.3 collective-permute-start.2
  220.2 1.8 copy-start.2
  222.3 33.7 %collective-permute-start.3 = (bf16[288,576]{1,0:T(8,128)(2,1)S(1)}, bf16[288,576]{1,0:T(8,128)(2,1)S(1)}, u32[]{:S(2)}, u32[]{:S(2)}) collective-permute-start(bf16[288,576]{1,0:T(8,128)(2,1)S(1)} %get-tuple-element.28), channel_id=1, source_target_pairs={{0,64},{64,0},{128,192},{192,128},{1,65},{65,1},{129,193},{193,129... | collective-permute-start | bytes 995336 | tf_op jit(solution)/shard_map/ppermute | solution.py:260
  223.9 47.5 %collective-permute-start.4 = (bf16[288,576]{1,0:T(8,128)(2,1)S(1)}, bf16[288,576]{1,0:T(8,128)(2,1)S(1)}, u32[]{:S(2)}, u32[]{:S(2)}) collective-permute-start(bf16[288,576]{1,0:T(8,128)(2,1)S(1)} %get-tuple-element.29), channel_id=1, source_target_pairs={{0,128},{64,192},{128,0},{192,64},{1,129},{65,193},{129,1},{193,65... | collective-permute-start | bytes 995336 | tf_op jit(solution)/shard_map/ppermute | solution.py:260
  226.7 44.7 %collective-permute-start.5 = (bf16[288,576]{1,0:T(8,128)(2,1)S(1)}, bf16[288,576]{1,0:T(8,128)(2,1)S(1)}, u32[]{:S(2)}, u32[]{:S(2)}) collective-permute-start(bf16[288,576]{1,0:T(8,128)(2,1)S(1)} %get-tuple-element.30), channel_id=1, source_target_pairs={{0,192},{64,128},{128,64},{192,0},{1,193},{65,129},{129,65},{193,1... | collective-permute-start | bytes 995336 | tf_op jit(solution)/shard_map/ppermute | solution.py:260
  271.7 13.3 %collective-permute-start.6 = (f32[4,18,576]{2,1,0:T(8,128)S(1)}, f32[4,18,576]{2,1,0:T(8,128)S(1)}, u32[]{:S(2)}, u32[]{:S(2)}) collective-permute-start(f32[4,18,576]{2,1,0:T(8,128)S(1)} %get-tuple-element.33), channel_id=1, source_target_pairs={{0,4},{4,0},{8,12},{12,8},{1,5},{5,1},{9,13},{13,9},{2,6},{6,2},{1... | collective-permute-start | bytes 497672 | tf_op jit(solution)/shard_map/ppermute | solution.py:260
  275.2 18.2 %collective-permute-start.7 = (f32[4,18,576]{2,1,0:T(8,128)S(1)}, f32[4,18,576]{2,1,0:T(8,128)S(1)}, u32[]{:S(2)}, u32[]{:S(2)}) collective-permute-start(f32[4,18,576]{2,1,0:T(8,128)S(1)} %get-tuple-element.35), channel_id=1, source_target_pairs={{0,8},{4,12},{8,0},{12,4},{1,9},{5,13},{9,1},{13,5},{2,10},{6,14},... | collective-permute-start | bytes 497672 | tf_op jit(solution)/shard_map/ppermute | solution.py:260
  275.9 18.7 %collective-permute-start.8 = (f32[4,18,576]{2,1,0:T(8,128)S(1)}, f32[4,18,576]{2,1,0:T(8,128)S(1)}, u32[]{:S(2)}, u32[]{:S(2)}) collective-permute-start(f32[4,18,576]{2,1,0:T(8,128)S(1)} %get-tuple-element.34), channel_id=1, source_target_pairs={{0,12},{4,8},{8,4},{12,0},{1,13},{5,9},{9,5},{13,1},{2,14},{6,10},... | collective-permute-start | bytes 497672 | tf_op jit(solution)/shard_map/ppermute | solution.py:260
  294.8 22.7 %collective-permute-start.10 = (f32[18,576]{1,0:T(8,128)S(1)}, f32[18,576]{1,0:T(8,128)S(1)}, u32[]{:S(2)}, u32[]{:S(2)}) collective-permute-start(f32[18,576]{1,0:T(8,128)S(1)} %get-tuple-element.38), channel_id=1, source_target_pairs={{0,32},{16,48},{32,0},{48,16},{1,33},{17,49},{33,1},{49,17},{2,34}... | collective-permute-start | bytes 124424 | tf_op jit(solution)/shard_map/ppermute | solution.py:260
  304.2 13.3 %collective-permute-start.11 = (f32[18,576]{1,0:T(8,128)S(1)}, f32[18,576]{1,0:T(8,128)S(1)}, u32[]{:S(2)}, u32[]{:S(2)}) collective-permute-start(f32[18,576]{1,0:T(8,128)S(1)} %get-tuple-element.37), channel_id=1, source_target_pairs={{0,48},{16,32},{32,16},{48,0},{1,49},{17,33},{33,17},{49,1},{2,50}... | collective-permute-start | bytes 124424 | tf_op jit(solution)/shard_map/ppermute | solution.py:260
  304.2 13.3 %collective-permute-start.9 = (f32[18,576]{1,0:T(8,128)S(1)}, f32[18,576]{1,0:T(8,128)S(1)}, u32[]{:S(2)}, u32[]{:S(2)}) collective-permute-start(f32[18,576]{1,0:T(8,128)S(1)} %get-tuple-element.36), channel_id=1, source_target_pairs={{0,16},{16,0},{32,48},{48,32},{1,17},{17,1},{33,49},{49,33},{2,18}... | collective-permute-start | bytes 124424 | tf_op jit(solution)/shard_map/ppermute | solution.py:260
  317.6 8.0 %collective-permute-start.12 = (f32[18,288]{1,0:T(8,128)S(1)}, f32[18,288]{1,0:T(8,128)S(1)}, u32[]{:S(2)}, u32[]{:S(2)}) collective-permute-start(f32[18,288]{1,0:T(8,128)S(1)} %bitcast.58), channel_id=1, source_target_pairs={{0,2},{2,0},{1,3},{3,1},{4,6},{6,4},{5,7},{7,5},{8,10},{10,8},{9,1... | collective-permute-start | bytes 62216 | tf_op jit(solution)/shard_map/ppermute | solution.py:260
  (2 other events, 1.9 us)
Sparse Core Ops, SparseCore 0:
  111.8 48.5 all-gather.2
where the time goes:
time: 342 us; the launch traced here: 341 us
  waiting for transfers between devices  213 us (62%)
  starting transfers between devices  49.9 us (15%)
  Pallas kernels  40.7 us (12%)
  local copies, waits for them, and re-layouts  15.8 us (5%)
  between operations  14.3 us (4%)
  other arithmetic  7.7 us (2%)
    ppermute x13, waiting for transfers between devices, swap(): return lax.ppermute(value, axis, [(i, i ^ k) for i in range(size)])  164 us
    all_gather x1, waiting for transfers between devices, whole_weight(): rows = lax.all_gather(pair, ('y', 'x'), axis=0, tiled=False)  48.7 us
    ppermute x13, starting transfers between devices, swap(): return lax.ppermute(value, axis, [(i, i ^ k) for i in range(size)])  27.6 us
    all_to_all x2, starting transfers between devices, exchange(): return lax.all_to_all(t, SEQ, split_axis=0, concat_axis=0, tiled=True)  22.2 us
    pallas_call x1, Pallas kernels, attend(): pl.pallas_call(attend_kernel, in_specs=in_vmem(4), out_specs=in_vmem(3),...  21.7 us
    unnamed x21, local copies, waits for them, and re-layouts  9.52 us
    pallas_call x1, Pallas kernels, pack(): pl.pallas_call(pack_kernel, grid=(2, 4), in_specs=[pl.BlockSpec((256, 256...  8.65 us
    pallas_call x1, Pallas kernels, unpack(): pl.pallas_call(unpack_kernel, grid=(2, 4), in_specs=[pl.BlockSpec((256, 2...  7.87 us
  transfers between devices with their start and end apart: 16, of which 11 were waited for; matrix products, arithmetic and copies ran while one was open for 4% of the time, Pallas kernels for 1%

commit v1 on v0

--- a/solution.py
+++ b/solution.py
@@ -59,42 +59,77 @@
     return pltpu.CompilerParams(vmem_limit_bytes=mib * MIB)
 
 
+def anywhere(count):
+    return [pl.BlockSpec(memory_space=pl.ANY)] * count
+
+
 def in_vmem(count):
     return [pl.BlockSpec(memory_space=pltpu.VMEM)] * count
 
 
-def pack_kernel(order_ref, q_ref, k_ref, v_ref, c_ref, out_ref):
-    rows = [ref[0, f] for ref in (q_ref, k_ref, v_ref, c_ref) for f in range(2)]
-    out_ref[...] = move(order_ref[...], jnp.concatenate(rows, axis=0)).reshape(16, 16, D)
-
-
-def pack(arrays):
+def pack_kernel(part, order_ref, q_ref, k_ref, v_ref, c_ref, *refs):
+    out_ref, rows_ref, slabs_ref, in_sem, out_sem = refs[-5:]
+    arrays = (q_ref, k_ref, v_ref, c_ref)
+    coming, going = [], []
+    for a in range(4):
+        coming.append(
+            pltpu.make_async_copy(
+                arrays[a].at[0, :, pl.ds(part * 128, 128), :], rows_ref.at[a], in_sem.at[a]
+            )
+        )
+        coming[-1].start()
+    for copy in coming:
+        copy.wait()
+    for g in range(4):
+        rows = [rows_ref[a, f, pl.ds(g * 32, 32), :] for a in range(4) for f in range(2)]
+        slabs_ref[g] = move(order_ref[...], jnp.concatenate(rows, axis=0)).reshape(16, 16, D)
+        going.append(
+            pltpu.make_async_copy(
+                slabs_ref.at[g],
+                out_ref.at[pl.ds(g * 16, 16), pl.ds(part * 16, 16), :],
+                out_sem.at[g],
+            )
+        )
+        going[-1].start()
+    for copy in going:
+        copy.wait()
+
+
+def pack(part, arrays, before):
     return pl.pallas_call(
-        pack_kernel,
-        grid=(2, 4),
-        in_specs=[pl.BlockSpec((256, 256), lambda i, g: (0, 0))]
-        + [pl.BlockSpec((1, 2, 32, D), lambda i, g: (0, 0, 4 * i + g, 0))] * 4,
-        out_specs=pl.BlockSpec((16, 16, D), lambda i, g: (g, i, 0)),
+        functools.partial(pack_kernel, part),
+        in_specs=in_vmem(1) + anywhere(4 + len(before)),
+        out_specs=pl.BlockSpec(memory_space=pl.ANY),
         out_shape=jax.ShapeDtypeStruct((64, 32, D), BF16),
+        scratch_shapes=[
+            pltpu.VMEM((4, 2, 128, D), BF16),
+            pltpu.VMEM((4, 16, 16, D), BF16),
+            pltpu.SemaphoreType.DMA((4,)),
+            pltpu.SemaphoreType.DMA((4,)),
+        ],
+        input_output_aliases={5: 0} if before else {},
         compiler_params=params(60),
         cost_estimate=pl.CostEstimate(
-            flops=2 * 2048 * 256 * D, bytes_accessed=8192 * D, transcendentals=0
+            flops=2 * 1024 * 256 * D, bytes_accessed=4096 * D, transcendentals=0
         ),
         name="pack",
-    )(const(order_to_slabs(2)), *arrays)
-
-
-def attend_part(part, order_ref, back_ref, r_ref, w_ref, s_ref, att_ref, cot_ref, x_ref, u_ref, y_ref):
+    )(const(order_to_slabs(2)), *arrays, *before)
+
+
+def attend_part(part, order_ref, back_ref, r_ref, w_ref, s_ref, att_ref, cot_ref, *refs):
+    in_ref, x_ref, u_ref, y_ref, out_ref, kept_ref, in_sem, out_sem, kept_sem = refs
     slots = pl.ds(pl.multiple_of(part * 16, 16), 16)
     mine = pl.ds(pl.multiple_of(part * 256, 256), 256)
     for b in range(4):
-        t = r_ref[pl.ds(b * 16, 16), slots, :].reshape(256, D)
-        t = move(order_ref[...], t)
+        n = part * 4 + b
+        pltpu.make_async_copy(r_ref.at[pl.ds(b * 16, 16), slots, :], in_ref.at[n], in_sem.at[n]).wait()
+        t = move(order_ref[...], in_ref[n].reshape(256, D))
         for a in range(4):
             for p in range(2):
                 x_ref[a, pl.ds(p * 128 + b * 32, 32), :] = t[(a * 2 + p) * 32 : (a * 2 + p + 1) * 32]
     cot = x_ref[3]
-    cot_ref[mine, :] = cot
+    kept_ref[part, 1] = cot
+    pltpu.make_async_copy(kept_ref.at[part, 1], cot_ref.at[mine, :], kept_sem.at[part, 1]).start()
     u_ref[...] = lax.dot_general(
         cot, w_ref[...], (((1,), (1,)), ((), ())), preferred_element_type=F32
     ).astype(BF16)
@@ -110,8 +145,8 @@
         def both(t):
             return jnp.concatenate([t * keep_first, t * keep_second], axis=0)
 
-        def split(t):
-            return jnp.where(first, t[:128], jnp.where(second, t[128:], 0.0)).astype(BF16)
+        def beside(t):
+            return jnp.concatenate([t[:128], t[128:]], axis=1)
 
         for p in range(2):
             rows = pl.ds(p * 128, 128)
@@ -135,41 +170,73 @@
             y_ref[1, rows, win] += lax.dot_general(
                 sg, kk, (((0,), (0,)), ((), ())), preferred_element_type=F32
             ).astype(BF16)
-            y_ref[2, rows, win] += split(jnp.dot(sg, q, preferred_element_type=F32))
-            y_ref[3, rows, win] += split(jnp.dot(low, u, preferred_element_type=F32))
+            y_ref[2, rows, win] += jnp.dot(
+                beside(sg), both(q), preferred_element_type=F32
+            ).astype(BF16)
+            y_ref[3, rows, win] += jnp.dot(
+                beside(low), both(u), preferred_element_type=F32
+            ).astype(BF16)
     att = y_ref[0]
-    att_ref[mine, :] = att
+    kept_ref[part, 0] = att
+    pltpu.make_async_copy(kept_ref.at[part, 0], att_ref.at[mine, :], kept_sem.at[part, 0]).start()
     y_ref[0] = jnp.dot(att, w_ref[...], preferred_element_type=F32).astype(BF16)
     for b in range(4):
+        n = part * 4 + b
         t = jnp.concatenate(
             [y_ref[a, pl.ds(p * 128 + b * 32, 32), :] for a in range(4) for p in range(2)], axis=0
         )
-        s_ref[pl.ds(b * 16, 16), slots, :] = move(back_ref[...], t).reshape(16, 16, D)
+        out_ref[n] = move(back_ref[...], t).reshape(16, 16, D)
+        pltpu.make_async_copy(out_ref.at[n], s_ref.at[pl.ds(b * 16, 16), slots, :], out_sem.at[n]).start()
 
 
 def attend_kernel(*refs):
+    r_ref, s_ref, att_ref, cot_ref = refs[2], refs[4], refs[5], refs[6]
+    in_ref, out_ref, kept_ref, in_sem, out_sem, kept_sem = refs[7], *refs[11:]
+    for n in range(8):
+        part, b = divmod(n, 4)
+        pltpu.make_async_copy(
+            r_ref.at[pl.ds(b * 16, 16), pl.ds(part * 16, 16), :], in_ref.at[n], in_sem.at[n]
+        ).start()
+
     @pl.loop(0, 2)
     def _(part):
         attend_part(part, *refs)
+
+    for part in range(2):
+        for i, ref in enumerate((att_ref, cot_ref)):
+            pltpu.make_async_copy(
+                kept_ref.at[part, i], ref.at[pl.ds(part * 256, 256), :], kept_sem.at[part, i]
+            ).wait()
+        for b in range(4):
+            n = part * 4 + b
+            pltpu.make_async_copy(
+                out_ref.at[n], s_ref.at[pl.ds(b * 16, 16), pl.ds(part * 16, 16), :], out_sem.at[n]
+            ).wait()
 
 
 def attend(received, weight):
     order = order_to_patches(2)
     return pl.pallas_call(
         attend_kernel,
-        in_specs=in_vmem(4),
-        out_specs=in_vmem(3),
+        in_specs=in_vmem(2) + anywhere(1) + in_vmem(1),
+        out_specs=anywhere(3),
         out_shape=[
             jax.ShapeDtypeStruct((64, 32, D), BF16),
             jax.ShapeDtypeStruct((512, D), BF16),
             jax.ShapeDtypeStruct((512, D), BF16),
         ],
         scratch_shapes=[
+            pltpu.VMEM((8, 16, 16, D), BF16),
             pltpu.VMEM((4, 256, D), BF16),
             pltpu.VMEM((256, D), BF16),
             pltpu.VMEM((4, 256, D), BF16),
+            pltpu.VMEM((8, 16, 16, D), BF16),
+            pltpu.VMEM((2, 2, 256, D), BF16),
+            pltpu.SemaphoreType.DMA((8,)),
+            pltpu.SemaphoreType.DMA((8,)),
+            pltpu.SemaphoreType.DMA((2, 2)),
         ],
-        compiler_params=params(24),
+        compiler_params=params(40),
         cost_estimate=pl.CostEstimate(
             flops=12_000_000_000, bytes_accessed=40 * 256 * D + 2 * D * D, transcendentals=1048576
         ),
@@ -177,24 +244,52 @@
     )(const(order), const(order.T.copy()), received, weight)
 
 
-def unpack_kernel(order_ref, slabs_ref, *outs):
-    t = move(order_ref[...], slabs_ref[...].reshape(256, D))
-    for a in range(4):
-        for f in range(2):
-            at = (a * 2 + f) * 32
-            outs[a][0, f] = t[at : at + 32]
+def unpack_kernel(order_ref, slabs_ref, *refs):
+    outs = refs[:4]
+    in_ref, rows_ref, in_sem, out_sem = refs[4:]
+    coming, going = [], []
+    for n in range(8):
+        part, g = divmod(n, 4)
+        coming.append(
+            pltpu.make_async_copy(
+                slabs_ref.at[pl.ds(g * 16, 16), pl.ds(part * 16, 16), :], in_ref.at[n], in_sem.at[n]
+            )
+        )
+        coming[-1].start()
+    for n in range(8):
+        part, g = divmod(n, 4)
+        coming[n].wait()
+        t = move(order_ref[...], in_ref[n].reshape(256, D))
+        for a in range(4):
+            for f in range(2):
+                at = (a * 2 + f) * 32
+                rows_ref[part, a, f, pl.ds(g * 32, 32), :] = t[at : at + 32]
+            if g % 2 == 1:
+                begin = (g - 1) * 32
+                going.append(
+                    pltpu.make_async_copy(
+                        rows_ref.at[part, a, :, pl.ds(begin, 64), :],
+                        outs[a].at[0, :, pl.ds(part * 128 + begin, 64), :],
+                        out_sem.at[n, a],
+                    )
+                )
+                going[-1].start()
+    for copy in going:
+        copy.wait()
 
 
 def unpack(slabs):
     return pl.pallas_call(
         unpack_kernel,
-        grid=(2, 4),
-        in_specs=[
-            pl.BlockSpec((256, 256), lambda i, g: (0, 0)),
-            pl.BlockSpec((16, 16, D), lambda i, g: (g, i, 0)),
+        in_specs=in_vmem(1) + anywhere(1),
+        out_specs=anywhere(4),
+        out_shape=[jax.ShapeDtypeStruct((1, 2, 256, D), BF16)] * 4,
+        scratch_shapes=[
+            pltpu.VMEM((8, 16, 16, D), BF16),
+            pltpu.VMEM((2, 4, 2, 128, D), BF16),
+            pltpu.SemaphoreType.DMA((8,)),
+            pltpu.SemaphoreType.DMA((8, 4)),
         ],
-        out_specs=[pl.BlockSpec((1, 2, 32, D), lambda i, g: (0, 0, 4 * i + g, 0))] * 4,
-        out_shape=[jax.ShapeDtypeStruct((1, 2, 256, D), BF16)] * 4,
         compiler_params=params(60),
         cost_estimate=pl.CostEstimate(
             flops=2 * 2048 * 256 * D, bytes_accessed=8192 * D, transcendentals=0
@@ -286,10 +381,13 @@
     return jnp.stack([jnp.where(first, own, other), jnp.where(first, other, own)])
 
 
-def whole_weight(out_weight):
+def weight_piece(out_weight):
     place = lax.axis_index("y") * 4 + lax.axis_index("x")
-    piece = lax.dynamic_index_in_dim(out_weight.reshape(16, 18, D), place, 0, keepdims=False)
-    pair = by_rank("zh", piece, swap(piece, "zh", 1))
+    piece = lax.dynamic_slice_in_dim(out_weight, place * 18, 18, 0)
+    return by_rank("zh", piece, swap(piece, "zh", 1))
+
+
+def whole_weight(pair):
     rows = lax.all_gather(pair, ("y", "x"), axis=0, tiled=False)
     rows = rows.transpose(1, 0, 2, 3).reshape(2, 288, D)
     both = by_rank("c", rows, swap(rows, "c", 1))
@@ -301,9 +399,12 @@
 
 
 def on_device(queries, keys, values, cotangent, out_weight):
-    weight = whole_weight(out_weight)
-    received = exchange(pack((queries, keys, values, cotangent)))
-    sent, att, cot = attend(received, weight)
+    arrays = (queries, keys, values, cotangent)
+    pair = weight_piece(out_weight)
+    packed = pack(0, arrays, ())
+    packed = pack(1, arrays, (packed, pair))
+    received = exchange(packed)
+    sent, att, cot = attend(received, whole_weight(pair))
     weight_grad = weight_total(att, cot)
     return (*unpack(exchange(sent)), weight_grad)
 

time: 342 us -> 309 us (0.904)
  waiting for transfers between devices: 213 us -> 177 us
    ppermute x13, waiting for transfers between devices: 164 us -> 84.7 us  [swap(): return lax.ppermute(value, axis, [(i, i ^ k) for i in range(size)])]
    all_gather x1, waiting for transfers between devices: 48.7 us -> 83.7 us  [whole_weight(): rows = lax.all_gather(pair, ('y', 'x'), axis=0, tiled=False)]
    all_to_all x2, waiting for transfers between devices: 0.01 us -> 8.23 us  [exchange(): return lax.all_to_all(t, SEQ, split_axis=0, concat_axis=0, tiled=True)]
    ppermute x13, starting transfers between devices: 27.6 us -> 32 us  [swap(): return lax.ppermute(value, axis, [(i, i ^ k) for i in range(size)])]
    pallas_call x3 -> x4, Pallas kernels: 38.2 us -> 39.1 us  [the longest x1 24.1 us: attend(): pl.pallas_call(attend_kernel, in_specs=in_vmem(2) + anywhere(1) + in_vmem...]
    unnamed x21 -> x19, local copies, waits for them, and re-layouts: 9.52 us -> 8.91 us
  transfers between devices with their start and end apart: 16 -> 16, of which waited for: 11 -> 11; matrix products, arithmetic and copies ran while one was open for 4% -> 4% of each run, Pallas kernels for 1% -> 2%
where the time goes in v1:
time: 309 us
  waiting for transfers between devices  177 us (57%)
  starting transfers between devices  51 us (17%)
  Pallas kernels  41.6 us (13%)
  local copies, waits for them, and re-layouts  15.9 us (5%)
  between operations  14.3 us (5%)
  other arithmetic  8.61 us (3%)
    ppermute x13, waiting for transfers between devices, swap(): return lax.ppermute(value, axis, [(i, i ^ k) for i in range(size)])  84.7 us
    all_gather x1, waiting for transfers between devices, whole_weight(): rows = lax.all_gather(pair, ('y', 'x'), axis=0, tiled=False)  83.7 us
    ppermute x13, starting transfers between devices, swap(): return lax.ppermute(value, axis, [(i, i ^ k) for i in range(size)])  32 us
    pallas_call x1, Pallas kernels, attend(): pl.pallas_call(attend_kernel, in_specs=in_vmem(2) + anywhere(1) + in_vmem...  24.1 us
    all_to_all x2, starting transfers between devices, exchange(): return lax.all_to_all(t, SEQ, split_axis=0, concat_axis=0, tiled=True)  18.9 us
    unnamed x19, local copies, waits for them, and re-layouts  8.91 us
    pallas_call x2, Pallas kernels, pack(): pl.pallas_call(functools.partial(pack_kernel, part), in_specs=in_vmem(1)...  8.79 us
    all_to_all x2, waiting for transfers between devices, exchange(): return lax.all_to_all(t, SEQ, split_axis=0, concat_axis=0, tiled=True)  8.23 us
  transfers between devices with their start and end apart: 16, of which 11 were waited for; matrix products, arithmetic and copies ran while one was open for 4% of the time, Pallas kernels for 2%

profile of v1, /device:TPU:2, one launch (start us, length us, event | category | flops | bytes accessed | tf_op | source)
XLA Modules:
  0.0 308.8 jit_solution(12772632117969893188)
XLA Ops:
  8.1 7.3 %collective-permute-start = (bf16[18,1152]{1,0:T(8,128)(2,1)S(1)}, bf16[18,1152]{1,0:T(8,128)(2,1)S(1)}, u32[]{:S(2)}, u32[]{:S(2)}) collective-permute-start(bf16[18,1152]{1,0:T(8,128)(2,1)S(1)} %constant_dynamic-slice_fusion.2), channel_id=1, source_target_pairs={{0,2},{2,0},{1,3},{3,1},{4,6},{6,4},{5,7},{7,5},{8,10},{10,8},{9,1... | collective-permute-start | bytes 124424 | tf_op jit(solution)/shard_map/ppermute | solution.py:355
  15.4 4.4 %pack.2.refs_0_ = bf16[64,32,1152]{2,1,0:T(8,128)(2,1)} custom-call(bf16[256,256]{1,0:T(8,128)(2,1)} %constant.67.clone.order_ref, bf16[1,2,256,1152]{3,2,1,0:T(8,128)(2,1)} %q_ref.3, bf16[1,2,256,1152]{3,2,1,0:T(8,128)(2,1)} %k_ref.3, bf16[1,2,256,1152]{3,2,1,0:T(8,128)(2,1)} %v_ref.3, bf16[1,2,256,1152]{3,2,1,0:T(8,128)(2,1)} %c_ref.3), custom_call_target="tpu_custom_call" | custom-call | flops 603979776 | bytes 4718592 | tf_op jit(solution)/shard_map/pack/pallas_call | solution.py:99
  21.4 4.4 %pack.3 = bf16[64,32,1152]{2,1,0:T(8,128)(2,1)} custom-call(bf16[256,256]{1,0:T(8,128)(2,1)} %constant.67.clone.order_ref, bf16[1,2,256,1152]{3,2,1,0:T(8,128)(2,1)} %q_ref.3, bf16[1,2,256,1152]{3,2,1,0:T(8,128)(2,1)} %k_ref.3, bf16[1,2,256,1152]{3,2,1,0:T(8,128)(2,1)} %v_ref.3, bf16[1,2,256,1152]{3,2,1,0:T(8,128)(2,1)} %c_ref.3, ...), custom_call_target="tpu_custom_call", output_to_operand_aliasing={{}: (5, {})} | custom-call | flops 603979776 | bytes 4718592 | tf_op jit(solution)/shard_map/pack/pallas_call | solution.py:99
  25.8 9.6 %all-to-all-start = ((bf16[64,32,1152]{2,1,0:T(8,128)(2,1)}), bf16[64,32,1152]{2,1,0:T(8,128)(2,1)}, u32[]{:S(2)}, u32[]{:S(2)}) async-start(bf16[64,32,1152]{2,1,0:T(8,128)(2,1)} %pack.3), calls=%async_computation | async-start | bytes 9437184 | tf_op jit(solution)/shard_map/all_to_all | solution.py:398
  36.1 83.7 %all-gather.3.cloned.1.call-done = bf16[32,18,1152]{2,1,0:T(8,128)(2,1)} async-done(((bf16[2,18,1152]{2,1,0:T(8,128)(2,1)}), bf16[32,18,1152]{2,1,0:T(8,128)(2,1)}) %all-gather.3.cloned.1.call-update) | async-done | bytes 1327120 | tf_op jit(solution)/shard_map/all_gather | solution.py:391
  119.8 2.5 copy.20
  122.6 3.0 collective-permute-done.1
  125.6 2.4 fusion
  128.0 3.8 %maximum_bitcast_fusion = bf16[2,2,288,1152]{3,0,2,1:T(2,128)(2,1)S(1)} fusion(bf16[1,2,288,1152]{3,1,2,0:T(2,128)(2,1)S(1)} %get-tuple-element.32, bf16[1,2,288,1152]{3,1,2,0:T(2,128)(2,1)S(1)} %get-tuple-element.31), kind=kLoop, calls=%fused_computation | loop fusion | flops 1327104 | bytes 5308416 | tf_op jit(solution)/shard_map/transpose | solution.py:394
  132.1 8.2 %all-to-all-done.refs_2_ = bf16[64,32,1152]{2,1,0:T(8,128)(2,1)} async-done(((bf16[64,32,1152]{2,1,0:T(8,128)(2,1)}), bf16[64,32,1152]{2,1,0:T(8,128)(2,1)}, u32[]{:S(2)}, u32[]{:S(2)}) %all-to-all-start) | async-done | bytes 4718624 | tf_op jit(solution)/shard_map/all_to_all | solution.py:398
  140.4 24.1 %attend.1 = (bf16[64,32,1152]{2,1,0:T(8,128)(2,1)S(1)}, bf16[512,1152]{1,0:T(8,128)(2,1)S(1)}, bf16[512,1152]{1,0:T(8,128)(2,1)S(1)}) custom-call(bf16[256,256]{1,0:T(8,128)(2,1)S(1)} %copy-done.3, bf16[256,256]{1,0:T(8,128)(2,1)S(1)} %copy-done.4, bf16[64,32,1152]{2,1,0:T(8,128)(2,1)} %all-to-all-done.refs_2_, bf16[1152,1152]{1,0:T(8,128)(2,1)S(1)} %bitcast.50), custom_call_target="tpu_custom_call" | custom-call | flops 12000000000 | bytes 14450688 | tf_op jit(solution)/shard_map/attend/pallas_call | solution.py:219
  168.7 9.4 %all-to-all-start.1 = ((bf16[64,32,1152]{2,1,0:T(8,128)(2,1)}), bf16[64,32,1152]{2,1,0:T(8,128)(2,1)}, u32[]{:S(2)}, u32[]{:S(2)}) async-start(bf16[64,32,1152]{2,1,0:T(8,128)(2,1)} %copy-done), calls=%async_computation.1 | async-start | bytes 9437184 | tf_op jit(solution)/shard_map/all_to_all | solution.py:398
  185.0 3.3 %collective-permute-done.2 = bf16[1152,576]{0,1:T(8,128)(2,1)S(1)} collective-permute-done((bf16[1152,576]{0,1:T(8,128)(2,1)}, bf16[1152,576]{0,1:T(8,128)(2,1)S(1)}, u32[]{:S(2)}, u32[]{:S(2)}) %collective-permute-start.2) | collective-permute-done | bytes 1327136 | tf_op jit(solution)/shard_map/ppermute | solution.py:355
  193.0 2.9 collective-permute-start.4
  196.3 28.9 %collective-permute-done.3 = bf16[288,576]{1,0:T(8,128)(2,1)S(1)} collective-permute-done((bf16[288,576]{1,0:T(8,128)(2,1)S(1)}, bf16[288,576]{1,0:T(8,128)(2,1)S(1)}, u32[]{:S(2)}, u32[]{:S(2)}) %collective-permute-start.3) | collective-permute-done | bytes 331808 | tf_op jit(solution)/shard_map/ppermute | solution.py:355
  225.1 15.4 %collective-permute-done.4 = bf16[288,576]{1,0:T(8,128)(2,1)S(1)} collective-permute-done((bf16[288,576]{1,0:T(8,128)(2,1)S(1)}, bf16[288,576]{1,0:T(8,128)(2,1)S(1)}, u32[]{:S(2)}, u32[]{:S(2)}) %collective-permute-start.4) | collective-permute-done | bytes 331808 | tf_op jit(solution)/shard_map/ppermute | solution.py:355
  240.9 3.4 %collective-permute-start.6 = (f32[4,18,576]{2,1,0:T(8,128)S(1)}, f32[4,18,576]{2,1,0:T(8,128)S(1)}, u32[]{:S(2)}, u32[]{:S(2)}) collective-permute-start(f32[4,18,576]{2,1,0:T(8,128)S(1)} %get-tuple-element.33), channel_id=1, source_target_pairs={{0,4},{4,0},{8,12},{12,8},{1,5},{5,1},{9,13},{13,9},{2,6},{6,2},{1... | collective-permute-start | bytes 497672 | tf_op jit(solution)/shard_map/ppermute | solution.py:355
  245.9 8.3 %collective-permute-done.6 = f32[4,18,576]{2,1,0:T(8,128)S(1)} collective-permute-done((f32[4,18,576]{2,1,0:T(8,128)S(1)}, f32[4,18,576]{2,1,0:T(8,128)S(1)}, u32[]{:S(2)}, u32[]{:S(2)}) %collective-permute-start.6) | collective-permute-done | bytes 165920 | tf_op jit(solution)/shard_map/ppermute | solution.py:355
  254.2 8.3 %collective-permute-done.7 = f32[4,18,576]{2,1,0:T(8,128)S(1)} collective-permute-done((f32[4,18,576]{2,1,0:T(8,128)S(1)}, f32[4,18,576]{2,1,0:T(8,128)S(1)}, u32[]{:S(2)}, u32[]{:S(2)}) %collective-permute-start.7) | collective-permute-done | bytes 165920 | tf_op jit(solution)/shard_map/ppermute | solution.py:355
  263.9 9.5 %collective-permute-start.10 = (f32[18,576]{1,0:T(8,128)S(1)}, f32[18,576]{1,0:T(8,128)S(1)}, u32[]{:S(2)}, u32[]{:S(2)}) collective-permute-start(f32[18,576]{1,0:T(8,128)S(1)} %get-tuple-element.38), channel_id=1, source_target_pairs={{0,32},{16,48},{32,0},{48,16},{1,33},{17,49},{33,1},{49,17},{2,34}... | collective-permute-start | bytes 124424 | tf_op jit(solution)/shard_map/ppermute | solution.py:355
  274.0 12.6 %collective-permute-done.10 = f32[18,576]{1,0:T(8,128)S(1)} collective-permute-done((f32[18,576]{1,0:T(8,128)S(1)}, f32[18,576]{1,0:T(8,128)S(1)}, u32[]{:S(2)}, u32[]{:S(2)}) %collective-permute-start.10) | collective-permute-done | bytes 41504 | tf_op jit(solution)/shard_map/ppermute | solution.py:355
  286.8 4.6 %collective-permute-start.12 = (f32[18,288]{1,0:T(8,128)S(1)}, f32[18,288]{1,0:T(8,128)S(1)}, u32[]{:S(2)}, u32[]{:S(2)}) collective-permute-start(f32[18,288]{1,0:T(8,128)S(1)} %bitcast.53), channel_id=1, source_target_pairs={{0,2},{2,0},{1,3},{3,1},{4,6},{6,4},{5,7},{7,5},{8,10},{10,8},{9,1... | collective-permute-start | bytes 62216 | tf_op jit(solution)/shard_map/ppermute | solution.py:355
  291.4 3.7 %collective-permute-done.12 = f32[18,288]{1,0:T(8,128)S(1)} collective-permute-done((f32[18,288]{1,0:T(8,128)S(1)}, f32[18,288]{1,0:T(8,128)S(1)}, u32[]{:S(2)}, u32[]{:S(2)}) %collective-permute-start.12) | collective-permute-done | bytes 20768 | tf_op jit(solution)/shard_map/ppermute | solution.py:355
  295.7 6.3 %unpack.1 = (bf16[1,2,256,1152]{3,2,1,0:T(8,128)(2,1)}, bf16[1,2,256,1152]{3,2,1,0:T(8,128)(2,1)}, bf16[1,2,256,1152]{3,2,1,0:T(8,128)(2,1)}, bf16[1,2,256,1152]{3,2,1,0:T(8,128)(2,1)}) custom-call(bf16[256,256]{1,0:T(8,128)(2,1)} %constant.70.clone.order_ref, bf16[64,32,1152]{2,1,0:T(8,128)(2,1)} %all-to-all-done.1.slabs_ref), custom_call_target="tpu_custom_call" | custom-call | flops 1207959552 | bytes 9437184 | tf_op jit(solution)/shard_map/unpack/pallas_call | solution.py:282
  (52 shorter events, 24.8 us)
Async XLA Ops:
  8.1 11.7 %collective-permute-start = (bf16[18,1152]{1,0:T(8,128)(2,1)S(1)}, bf16[18,1152]{1,0:T(8,128)(2,1)S(1)}, u32[]{:S(2)}, u32[]{:S(2)}) collective-permute-start(bf16[18,1152]{1,0:T(8,128)(2,1)S(1)} %constant_dynamic-slice_fusion.2), channel_id=1, source_target_pairs={{0,2},{2,0},{1,3},{3,1},{4,6},{6,4},{5,7},{7,5},{8,10},{10,8},{9,1... | collective-permute-start | bytes 124424 | tf_op jit(solution)/shard_map/ppermute | solution.py:355
  25.8 114.6 %all-to-all-start = ((bf16[64,32,1152]{2,1,0:T(8,128)(2,1)}), bf16[64,32,1152]{2,1,0:T(8,128)(2,1)}, u32[]{:S(2)}, u32[]{:S(2)}) async-start(bf16[64,32,1152]{2,1,0:T(8,128)(2,1)} %pack.3), calls=%async_computation | async-start | bytes 9437184 | tf_op jit(solution)/shard_map/all_to_all | solution.py:398
  35.3 84.5 %all-gather.3.cloned.1.call-start = ((), (), s32[]{:S(2)}) async-start(), calls=%async_computation.2 | async-start | bytes 1880064 | tf_op jit(solution)/shard_map/all_gather | solution.py:391
  122.3 3.3 %collective-permute-start.1 = (bf16[2,288,1152]{2,0,1:T(2,128)(2,1)S(1)}, bf16[2,288,1152]{2,0,1:T(2,128)(2,1)S(1)}, u32[]{:S(2)}, u32[]{:S(2)}) collective-permute-start(bf16[2,288,1152]{2,0,1:T(2,128)(2,1)S(1)} %bitcast.51), channel_id=1, source_target_pairs={{0,1},{1,0},{2,3},{3,2},{4,5},{5,4},{6,7},{7,6},{8,9},{9,8},{10,11... | collective-permute-start | bytes 3981320 | tf_op jit(solution)/shard_map/ppermute | solution.py:355
  131.8 8.6 %copy-start.3 = (bf16[256,256]{1,0:T(8,128)(2,1)S(1)}, bf16[256,256]{1,0:T(8,128)(2,1)}, u32[]{:S(2)}) copy-start(bf16[256,256]{1,0:T(8,128)(2,1)} %constant.68.clone.refs_0_) | copy-start | bytes 393220
  131.8 8.6 %copy-start.4 = (bf16[256,256]{1,0:T(8,128)(2,1)S(1)}, bf16[256,256]{1,0:T(8,128)(2,1)}, u32[]{:S(2)}) copy-start(bf16[256,256]{1,0:T(8,128)(2,1)} %constant.69.clone.refs_1_) | copy-start | bytes 393220
  164.5 2.2 copy-start
  166.6 1.0 copy-start.5
  168.7 9.4 %copy-start.6 = (bf16[512,1152]{1,0:T(8,128)(2,1)S(1)}, bf16[512,1152]{1,0:T(8,128)(2,1)}, u32[]{:S(2)}) copy-start(bf16[512,1152]{1,0:T(8,128)(2,1)} %copy-done.5) | copy-start | bytes 3538948
  168.7 127.0 %all-to-all-start.1 = ((bf16[64,32,1152]{2,1,0:T(8,128)(2,1)}), bf16[64,32,1152]{2,1,0:T(8,128)(2,1)}, u32[]{:S(2)}, u32[]{:S(2)}) async-start(bf16[64,32,1152]{2,1,0:T(8,128)(2,1)} %copy-done), calls=%async_computation.1 | async-start | bytes 9437184 | tf_op jit(solution)/shard_map/all_to_all | solution.py:398
  178.1 1.3 copy-start.8
  181.5 1.6 copy-start.1
  185.0 3.3 %collective-permute-start.2 = (bf16[1152,576]{0,1:T(8,128)(2,1)}, bf16[1152,576]{0,1:T(8,128)(2,1)S(1)}, u32[]{:S(2)}, u32[]{:S(2)}) collective-permute-start(bf16[1152,576]{0,1:T(8,128)(2,1)} %copy.22), channel_id=1, source_target_pairs={{0,1},{1,0},{2,3},{3,2},{4,5},{5,4},{6,7},{7,6},{8,9},{9,8},{10,11... | collective-permute-start | bytes 3981320 | tf_op jit(solution)/shard_map/ppermute | solution.py:355
  189.4 1.8 copy-start.2
  191.5 33.7 %collective-permute-start.3 = (bf16[288,576]{1,0:T(8,128)(2,1)S(1)}, bf16[288,576]{1,0:T(8,128)(2,1)S(1)}, u32[]{:S(2)}, u32[]{:S(2)}) collective-permute-start(bf16[288,576]{1,0:T(8,128)(2,1)S(1)} %get-tuple-element.28), channel_id=1, source_target_pairs={{0,64},{64,0},{128,192},{192,128},{1,65},{65,1},{129,193},{193,129... | collective-permute-start | bytes 995336 | tf_op jit(solution)/shard_map/ppermute | solution.py:355
  193.0 47.5 %collective-permute-start.4 = (bf16[288,576]{1,0:T(8,128)(2,1)S(1)}, bf16[288,576]{1,0:T(8,128)(2,1)S(1)}, u32[]{:S(2)}, u32[]{:S(2)}) collective-permute-start(bf16[288,576]{1,0:T(8,128)(2,1)S(1)} %get-tuple-element.29), channel_id=1, source_target_pairs={{0,128},{64,192},{128,0},{192,64},{1,129},{65,193},{129,1},{193,65... | collective-permute-start | bytes 995336 | tf_op jit(solution)/shard_map/ppermute | solution.py:355
  195.9 44.6 %collective-permute-start.5 = (bf16[288,576]{1,0:T(8,128)(2,1)S(1)}, bf16[288,576]{1,0:T(8,128)(2,1)S(1)}, u32[]{:S(2)}, u32[]{:S(2)}) collective-permute-start(bf16[288,576]{1,0:T(8,128)(2,1)S(1)} %get-tuple-element.30), channel_id=1, source_target_pairs={{0,192},{64,128},{128,64},{192,0},{1,193},{65,129},{129,65},{193,1... | collective-permute-start | bytes 995336 | tf_op jit(solution)/shard_map/ppermute | solution.py:355
  240.9 13.3 %collective-permute-start.6 = (f32[4,18,576]{2,1,0:T(8,128)S(1)}, f32[4,18,576]{2,1,0:T(8,128)S(1)}, u32[]{:S(2)}, u32[]{:S(2)}) collective-permute-start(f32[4,18,576]{2,1,0:T(8,128)S(1)} %get-tuple-element.33), channel_id=1, source_target_pairs={{0,4},{4,0},{8,12},{12,8},{1,5},{5,1},{9,13},{13,9},{2,6},{6,2},{1... | collective-permute-start | bytes 497672 | tf_op jit(solution)/shard_map/ppermute | solution.py:355
  244.3 18.1 %collective-permute-start.7 = (f32[4,18,576]{2,1,0:T(8,128)S(1)}, f32[4,18,576]{2,1,0:T(8,128)S(1)}, u32[]{:S(2)}, u32[]{:S(2)}) collective-permute-start(f32[4,18,576]{2,1,0:T(8,128)S(1)} %get-tuple-element.35), channel_id=1, source_target_pairs={{0,8},{4,12},{8,0},{12,4},{1,9},{5,13},{9,1},{13,5},{2,10},{6,14},... | collective-permute-start | bytes 497672 | tf_op jit(solution)/shard_map/ppermute | solution.py:355
  245.1 18.7 %collective-permute-start.8 = (f32[4,18,576]{2,1,0:T(8,128)S(1)}, f32[4,18,576]{2,1,0:T(8,128)S(1)}, u32[]{:S(2)}, u32[]{:S(2)}) collective-permute-start(f32[4,18,576]{2,1,0:T(8,128)S(1)} %get-tuple-element.34), channel_id=1, source_target_pairs={{0,12},{4,8},{8,4},{12,0},{1,13},{5,9},{9,5},{13,1},{2,14},{6,10},... | collective-permute-start | bytes 497672 | tf_op jit(solution)/shard_map/ppermute | solution.py:355
  263.9 22.7 %collective-permute-start.10 = (f32[18,576]{1,0:T(8,128)S(1)}, f32[18,576]{1,0:T(8,128)S(1)}, u32[]{:S(2)}, u32[]{:S(2)}) collective-permute-start(f32[18,576]{1,0:T(8,128)S(1)} %get-tuple-element.38), channel_id=1, source_target_pairs={{0,32},{16,48},{32,0},{48,16},{1,33},{17,49},{33,1},{49,17},{2,34}... | collective-permute-start | bytes 124424 | tf_op jit(solution)/shard_map/ppermute | solution.py:355
  273.4 13.2 %collective-permute-start.11 = (f32[18,576]{1,0:T(8,128)S(1)}, f32[18,576]{1,0:T(8,128)S(1)}, u32[]{:S(2)}, u32[]{:S(2)}) collective-permute-start(f32[18,576]{1,0:T(8,128)S(1)} %get-tuple-element.37), channel_id=1, source_target_pairs={{0,48},{16,32},{32,16},{48,0},{1,49},{17,33},{33,17},{49,1},{2,50}... | collective-permute-start | bytes 124424 | tf_op jit(solution)/shard_map/ppermute | solution.py:355
  273.4 13.2 %collective-permute-start.9 = (f32[18,576]{1,0:T(8,128)S(1)}, f32[18,576]{1,0:T(8,128)S(1)}, u32[]{:S(2)}, u32[]{:S(2)}) collective-permute-start(f32[18,576]{1,0:T(8,128)S(1)} %get-tuple-element.36), channel_id=1, source_target_pairs={{0,16},{16,0},{32,48},{48,32},{1,17},{17,1},{33,49},{49,33},{2,18}... | collective-permute-start | bytes 124424 | tf_op jit(solution)/shard_map/ppermute | solution.py:355
  286.8 8.3 %collective-permute-start.12 = (f32[18,288]{1,0:T(8,128)S(1)}, f32[18,288]{1,0:T(8,128)S(1)}, u32[]{:S(2)}, u32[]{:S(2)}) collective-permute-start(f32[18,288]{1,0:T(8,128)S(1)} %bitcast.53), channel_id=1, source_target_pairs={{0,2},{2,0},{1,3},{3,1},{4,6},{6,4},{5,7},{7,5},{8,10},{10,8},{9,1... | collective-permute-start | bytes 62216 | tf_op jit(solution)/shard_map/ppermute | solution.py:355
  (1 other events, 1.0 us)
Sparse Core Ops, SparseCore 0:
  39.2 80.5 all-gather.2

commit v2 on v1

v2 whole, which is shorter than its diff:
```python
import functools

import jax
import jax.numpy as jnp
import numpy as np
from jax import lax
from jax.experimental import pallas as pl
from jax.experimental.pallas import tpu as pltpu
from jax.sharding import Mesh
from jax.sharding import PartitionSpec as P

HEADS = 16
HEAD_DIM = 72
D = 1152
SCALE = HEAD_DIM ** (-0.5)
LOG2E = 1.4426950408889634
MIB = 1024 * 1024
F32 = jnp.float32
BF16 = jnp.bfloat16
SEQ = ("y", "zl", "x")
ROWS = ("zh", "c")


def order_to_slabs(np_):
    size = 128 * np_
    out = np.zeros((size, size), np.float32)
    for s in range(16):
        for a in range(4):
            for f in range(2):
                for p in range(np_):
                    out[((s * 4 + a) * 2 + f) * np_ + p, ((a * 2 + f) * 16 + s) * np_ + p] = 1
    return out


def order_to_patches(np_):
    size = 128 * np_
    out = np.zeros((size, size), np.float32)
    for s in range(16):
        for a in range(4):
            for f in range(2):
                for p in range(np_):
                    out[((a * np_ + p) * 16 + s) * 2 + f, ((s * 4 + a) * 2 + f) * np_ + p] = 1
    return out


def const(matrix):
    return jnp.asarray(matrix, BF16)


def move(order, rows):
    return jnp.dot(order, rows, preferred_element_type=F32).astype(BF16)


def whole(shape):
    return pl.BlockSpec(shape, lambda i: (0,) * len(shape))


def params(mib):
    return pltpu.CompilerParams(vmem_limit_bytes=mib * MIB)


def in_hbm(count):
    return [pl.BlockSpec(memory_space=pltpu.HBM)] * count


def in_vmem(count):
    return [pl.BlockSpec(memory_space=pltpu.VMEM)] * count


def pack_kernel(order_ref, q_ref, k_ref, v_ref, c_ref, out_ref, rows_ref, slabs_ref, in_sem, out_sem):
    arrays = (q_ref, k_ref, v_ref, c_ref)
    coming, going = [], []
    for part in range(2):
        for a in range(4):
            coming.append(
                pltpu.make_async_copy(
                    arrays[a].at[0, :, pl.ds(part * 128, 128), :],
                    rows_ref.at[part, a],
                    in_sem.at[part, a],
                )
            )
            coming[-1].start()
    for part in range(2):
        for a in range(4):
            coming[4 * part + a].wait()
        for g in range(4):
            rows = [rows_ref[part, a, f, pl.ds(g * 32, 32), :] for a in range(4) for f in range(2)]
            slabs_ref[part, g] = move(order_ref[...], jnp.concatenate(rows, axis=0)).reshape(16, 16, D)
            going.append(
                pltpu.make_async_copy(
                    slabs_ref.at[part, g],
                    out_ref.at[pl.ds(g * 16, 16), pl.ds(part * 16, 16), :],
                    out_sem.at[part, g],
                )
            )
            going[-1].start()
    for copy in going:
        copy.wait()


def pack(arrays):
    return pl.pallas_call(
        pack_kernel,
        in_specs=in_vmem(1) + in_hbm(4),
        out_specs=pl.BlockSpec(memory_space=pltpu.HBM),
        out_shape=jax.ShapeDtypeStruct((64, 32, D), BF16),
        scratch_shapes=[
            pltpu.VMEM((2, 4, 2, 128, D), BF16),
            pltpu.VMEM((2, 4, 16, 16, D), BF16),
            pltpu.SemaphoreType.DMA((2, 4)),
            pltpu.SemaphoreType.DMA((2, 4)),
        ],
        compiler_params=params(60),
        cost_estimate=pl.CostEstimate(
            flops=2 * 2048 * 256 * D, bytes_accessed=8192 * D, transcendentals=0
        ),
        name="pack",
    )(const(order_to_slabs(2)), *arrays)


def masks(j):
    lane = lax.broadcasted_iota(jnp.int32, (1, 256), 1)
    first = (lane >= 16 * j) & (lane < 16 * j + 72)
    second = (lane >= 16 * j + 72) & (lane < 16 * j + 144)
    return first.astype(F32).astype(BF16), second.astype(F32).astype(BF16)


def both(t, pair):
    return jnp.concatenate([t * pair[0], t * pair[1]], axis=0)


def beside(t):
    return jnp.concatenate([t[:128], t[128:]], axis=1)


def by_last(left, right):
    return lax.dot_general(left, right, (((1,), (1,)), ((), ())), preferred_element_type=F32)


def by_first(left, right):
    return lax.dot_general(left, right, (((0,), (0,)), ((), ())), preferred_element_type=F32)


def forward_part(part, order_ref, r_ref, x_hbm, in_ref, x_ref, att_ref, stat_ref, in_sem, x_sem):
    slots = pl.ds(pl.multiple_of(part * 16, 16), 16)
    for b in range(4):
        n = part * 4 + b
        pltpu.make_async_copy(r_ref.at[pl.ds(b * 16, 16), slots, :], in_ref.at[n], in_sem.at[n]).wait()
        t = move(order_ref[...], in_ref[n].reshape(256, D))
        for a in range(4):
            for p in range(2):
                x_ref[part, a, pl.ds(p * 128 + b * 32, 32), :] = t[(a * 2 + p) * 32 : (a * 2 + p + 1) * 32]
    pltpu.make_async_copy(x_ref.at[part], x_hbm.at[part], x_sem.at[part]).start()
    att_ref[part] = jnp.zeros((256, D), BF16)
    for j in range(8):
        pair = masks(j)
        win = pl.ds(128 * j, 256)
        for p in range(2):
            rows = pl.ds(p * 128, 128)
            kk = both(x_ref[part, 1, rows, win], pair)
            vv = both(x_ref[part, 2, rows, win], pair)
            scores = by_last(kk, x_ref[part, 0, rows, win]).reshape(2, 128, 128)
            top = jnp.max(scores, axis=1, keepdims=True)
            raised = jnp.exp2((scores - top) * (SCALE * LOG2E))
            scale = 1.0 / jnp.sum(raised, axis=1, keepdims=True)
            low = (raised * scale).astype(BF16).reshape(256, 128)
            att_ref[part, rows, win] += by_first(low, vv).astype(BF16)
            stat_ref[part, 2 * j + p, pl.ds(0, 2), :] = top.reshape(2, 128)
            stat_ref[part, 2 * j + p, pl.ds(2, 2), :] = scale.reshape(2, 128)


def forward_kernel(
    order_ref, r_ref, x_hbm, att_hbm, stat_hbm, mine_hbm, theirs_hbm,
    in_ref, x_ref, att_ref, stat_ref, mine_ref, theirs_ref, in_sem, x_sem, end_sem,
):
    for n in range(8):
        part, b = divmod(n, 4)
        pltpu.make_async_copy(
            r_ref.at[pl.ds(b * 16, 16), pl.ds(part * 16, 16), :], in_ref.at[n], in_sem.at[n]
        ).start()

    @pl.loop(0, 2)
    def _(part):
        forward_part(part, order_ref, r_ref, x_hbm, in_ref, x_ref, att_ref, stat_ref, in_sem, x_sem)

    ending = [
        pltpu.make_async_copy(att_ref, att_hbm, end_sem.at[0]),
        pltpu.make_async_copy(stat_ref, stat_hbm, end_sem.at[1]),
        pltpu.make_async_copy(theirs_ref, theirs_hbm, end_sem.at[2]),
        pltpu.make_async_copy(mine_ref, mine_hbm, end_sem.at[3]),
    ]
    ending[0].start()
    ending[1].start()
    att = jnp.concatenate([att_ref[0], att_ref[1]], axis=0)
    cot = jnp.concatenate([x_ref[0, 3], x_ref[1, 3]], axis=0)
    parts = [att[:, 288 * b : 288 * b + 288] for b in range(4)]
    even = jnp.concatenate([parts[0], parts[2]], axis=1)
    odd = jnp.concatenate([parts[1], parts[3]], axis=1)
    core = lax.axis_index("c")
    theirs_ref[...] = by_first(cot, jnp.where(core == 0, odd, even)).astype(BF16)
    ending[2].start()
    mine_ref[...] = by_first(cot, jnp.where(core == 0, even, odd))
    ending[3].start()
    for part in range(2):
        pltpu.make_async_copy(x_ref.at[part], x_hbm.at[part], x_sem.at[part]).wait()
    for copy in ending:
        copy.wait()


def forward(received):
    return pl.pallas_call(
        forward_kernel,
        in_specs=in_vmem(1) + in_hbm(1),
        out_specs=in_hbm(5),
        out_shape=[
            jax.ShapeDtypeStruct((2, 4, 256, D), BF16),
            jax.ShapeDtypeStruct((2, 256, D), BF16),
            jax.ShapeDtypeStruct((2, 16, 4, 128), F32),
            jax.ShapeDtypeStruct((D, 576), F32),
            jax.ShapeDtypeStruct((D, 576), BF16),
        ],
        scratch_shapes=[
            pltpu.VMEM((8, 16, 16, D), BF16),
            pltpu.VMEM((2, 4, 256, D), BF16),
            pltpu.VMEM((2, 256, D), BF16),
            pltpu.VMEM((2, 16, 4, 128), F32),
            pltpu.VMEM((D, 576), F32),
            pltpu.VMEM((D, 576), BF16),
            pltpu.SemaphoreType.DMA((8,)),
            pltpu.SemaphoreType.DMA((2,)),
            pltpu.SemaphoreType.DMA((4,)),
        ],
        compiler_params=params(58),
        cost_estimate=pl.CostEstimate(
            flops=5_000_000_000, bytes_accessed=40 * 256 * D, transcendentals=1048576
        ),
        name="forward",
    )(const(order_to_patches(2)), received)


def backward_part(part, back_ref, x_hbm, s_ref, x_ref, w_ref, att_ref, stat_ref, u_ref, y_ref, out_ref, x_sem, out_sem):
    slots = pl.ds(pl.multiple_of(part * 16, 16), 16)
    pltpu.make_async_copy(x_hbm.at[part], x_ref.at[part], x_sem.at[part]).wait()
    u_ref[...] = by_last(x_ref[part, 3], w_ref[...]).astype(BF16)
    y_ref[...] = jnp.zeros_like(y_ref)
    for j in range(8):
        pair = masks(j)
        win = pl.ds(128 * j, 256)
        for p in range(2):
            rows = pl.ds(p * 128, 128)
            q = x_ref[part, 0, rows, win]
            u = u_ref[rows, win]
            kk = both(x_ref[part, 1, rows, win], pair)
            vv = both(x_ref[part, 2, rows, win], pair)
            top = stat_ref[part, 2 * j + p, pl.ds(0, 2), :].reshape(2, 1, 128)
            scale = stat_ref[part, 2 * j + p, pl.ds(2, 2), :].reshape(2, 1, 128)
            scores = by_last(kk, q).reshape(2, 128, 128)
            prob = jnp.exp2((scores - top) * (SCALE * LOG2E)) * scale
            low = prob.astype(BF16).reshape(256, 128)
            grad = by_last(vv, u).reshape(2, 128, 128)
            centre = jnp.sum(prob * grad, axis=1, keepdims=True)
            sg = (prob * (grad - centre) * SCALE).astype(BF16).reshape(256, 128)
            y_ref[1, rows, win] += by_first(sg, kk).astype(BF16)
            y_ref[2, rows, win] += jnp.dot(
                beside(sg), both(q, pair), preferred_element_type=F32
            ).astype(BF16)
            y_ref[3, rows, win] += jnp.dot(
                beside(low), both(u, pair), preferred_element_type=F32
            ).astype(BF16)
    y_ref[0] = jnp.dot(att_ref[part], w_ref[...], preferred_element_type=F32).astype(BF16)
    for b in range(4):
        n = part * 4 + b
        t = jnp.concatenate(
            [y_ref[a, pl.ds(p * 128 + b * 32, 32), :] for a in range(4) for p in range(2)], axis=0
        )
        out_ref[n] = move(back_ref[...], t).reshape(16, 16, D)
        pltpu.make_async_copy(out_ref.at[n], s_ref.at[pl.ds(b * 16, 16), slots, :], out_sem.at[n]).start()


def backward_kernel(
    back_ref, x_hbm, att_hbm, stat_hbm, w_hbm, s_ref,
    x_ref, w_ref, att_ref, stat_ref, u_ref, y_ref, out_ref, x_sem, w_sem, in_sem, out_sem,
):
    coming = [pltpu.make_async_copy(stat_hbm, stat_ref, in_sem.at[0])]
    coming += [
        pltpu.make_async_copy(w_hbm.at[pl.ds(288 * b, 288), :], w_ref.at[pl.ds(288 * b, 288), :], w_sem.at[b])
        for b in range(4)
    ]
    coming.append(pltpu.make_async_copy(att_hbm, att_ref, in_sem.at[1]))
    pltpu.make_async_copy(x_hbm.at[0], x_ref.at[0], x_sem.at[0]).start()
    for copy in coming:
        copy.start()
    pltpu.make_async_copy(x_hbm.at[1], x_ref.at[1], x_sem.at[1]).start()
    for copy in coming:
        copy.wait()

    @pl.loop(0, 2)
    def _(part):
        backward_part(
            part, back_ref, x_hbm, s_ref, x_ref, w_ref, att_ref, stat_ref, u_ref, y_ref, out_ref, x_sem, out_sem
        )

    for n in range(8):
        part, b = divmod(n, 4)
        pltpu.make_async_copy(
            out_ref.at[n], s_ref.at[pl.ds(b * 16, 16), pl.ds(part * 16, 16), :], out_sem.at[n]
        ).wait()


def backward(arrays, att, stats, weight):
    return pl.pallas_call(
        backward_kernel,
        in_specs=in_vmem(1) + in_hbm(4),
        out_specs=pl.BlockSpec(memory_space=pltpu.HBM),
        out_shape=jax.ShapeDtypeStruct((64, 32, D), BF16),
        scratch_shapes=[
            pltpu.VMEM((2, 4, 256, D), BF16),
            pltpu.VMEM((D, D), BF16),
            pltpu.VMEM((2, 256, D), BF16),
            pltpu.VMEM((2, 16, 4, 128), F32),
            pltpu.VMEM((256, D), BF16),
            pltpu.VMEM((4, 256, D), BF16),
            pltpu.VMEM((8, 16, 16, D), BF16),
            pltpu.SemaphoreType.DMA((2,)),
            pltpu.SemaphoreType.DMA((4,)),
            pltpu.SemaphoreType.DMA((2,)),
            pltpu.SemaphoreType.DMA((8,)),
        ],
        compiler_params=params(58),
        cost_estimate=pl.CostEstimate(
            flops=9_000_000_000, bytes_accessed=40 * 256 * D + 2 * D * D, transcendentals=1048576
        ),
        name="backward",
    )(const(order_to_patches(2).T.copy()), arrays, att, stats, weight)


def unpack_kernel(order_ref, slabs_ref, *refs):
    outs = refs[:4]
    in_ref, rows_ref, in_sem, out_sem = refs[4:]
    coming, going = [], []
    for n in range(8):
        part, g = divmod(n, 4)
        coming.append(
            pltpu.make_async_copy(
                slabs_ref.at[pl.ds(g * 16, 16), pl.ds(part * 16, 16), :], in_ref.at[n], in_sem.at[n]
            )
        )
        coming[-1].start()
    for n in range(8):
        part, g = divmod(n, 4)
        coming[n].wait()
        t = move(order_ref[...], in_ref[n].reshape(256, D))
        for a in range(4):
            for f in range(2):
                at = (a * 2 + f) * 32
                rows_ref[part, a, f, pl.ds(g * 32, 32), :] = t[at : at + 32]
            if g % 2 == 1:
                begin = (g - 1) * 32
                going.append(
                    pltpu.make_async_copy(
                        rows_ref.at[part, a, :, pl.ds(begin, 64), :],
                        outs[a].at[0, :, pl.ds(part * 128 + begin, 64), :],
                        out_sem.at[n, a],
                    )
                )
                going[-1].start()
    for copy in going:
        copy.wait()


def unpack(slabs):
    return pl.pallas_call(
        unpack_kernel,
        in_specs=in_vmem(1) + in_hbm(1),
        out_specs=in_hbm(4),
        out_shape=[jax.ShapeDtypeStruct((1, 2, 256, D), BF16)] * 4,
        scratch_shapes=[
            pltpu.VMEM((8, 16, 16, D), BF16),
            pltpu.VMEM((2, 4, 2, 128, D), BF16),
            pltpu.SemaphoreType.DMA((8,)),
            pltpu.SemaphoreType.DMA((8, 4)),
        ],
        compiler_params=params(60),
        cost_estimate=pl.CostEstimate(
            flops=2 * 2048 * 256 * D, bytes_accessed=8192 * D, transcendentals=0
        ),
        name="unpack",
    )(const(order_to_slabs(2).T.copy()), slabs)


def halves_kernel(mine_hbm, other_hbm, own_hbm, s1, s2, s3, mine_ref, other_ref, send_ref, in_sem, out_sem):
    y = lax.axis_index("y")
    outs = (own_hbm, s1, s2, s3)
    coming, going = [], []
    for k in (1, 2, 3, 0):
        rows = pl.ds(pl.multiple_of((y ^ k) * 288, 32), 288)
        coming.append((
            pltpu.make_async_copy(mine_hbm.at[rows, :], mine_ref.at[k], in_sem.at[k, 0]),
            pltpu.make_async_copy(other_hbm.at[rows, :], other_ref.at[k], in_sem.at[k, 1]),
        ))
        for copy in coming[-1]:
            copy.start()
    for i, k in enumerate((1, 2, 3, 0)):
        for copy in coming[i]:
            copy.wait()
        total = mine_ref[k] + other_ref[k].astype(F32)
        if k == 0:
            mine_ref[k] = total
            source = mine_ref.at[k]
        else:
            send_ref[k - 1] = total.astype(BF16)
            source = send_ref.at[k - 1]
        going.append(pltpu.make_async_copy(source, outs[k], out_sem.at[k]))
        going[-1].start()
    for copy in going:
        copy.wait()


def halves(mine, other):
    return pl.pallas_call(
        halves_kernel,
        in_specs=in_hbm(2),
        out_specs=in_hbm(4),
        out_shape=[jax.ShapeDtypeStruct((288, 576), F32)] + [jax.ShapeDtypeStruct((288, 576), BF16)] * 3,
        scratch_shapes=[
            pltpu.VMEM((4, 288, 576), F32),
            pltpu.VMEM((4, 288, 576), BF16),
            pltpu.VMEM((3, 288, 576), BF16),
            pltpu.SemaphoreType.DMA((4, 2)),
            pltpu.SemaphoreType.DMA((4,)),
        ],
        compiler_params=params(60),
        cost_estimate=pl.CostEstimate(flops=D * 576, bytes_accessed=10 * D * 576, transcendentals=0),
        name="halves",
    )(mine, other)


SIZES = {"y": 4, "x": 4, "zl": 4, "zh": 2, "c": 2, ("zl", "zh"): 8}


def swap(value, axis, k):
    return lax.ppermute(value, axis, [(i, i ^ k) for i in range(SIZES[axis])])


def sum_over(blocks, axis):
    at = lax.axis_index(axis)
    total = lax.dynamic_index_in_dim(blocks, at, 0, keepdims=False)
    for k in range(1, SIZES[axis]):
        total = total + swap(lax.dynamic_index_in_dim(blocks, at ^ k, 0, keepdims=False), axis, k)
    return total


def weight_total(mine, theirs):
    own, *sent = halves(mine, swap(theirs, "c", 1))
    total = own
    for k in range(1, 4):
        total = total + swap(sent[k - 1], "y", k).astype(F32)
    blocks = total.reshape(4, 4, 18, 576).transpose(1, 0, 2, 3)
    blocks = sum_over(blocks, "x")
    blocks = blocks.reshape(4, 18, 2, 288).transpose(0, 2, 1, 3).reshape(8, 18, 288)
    return sum_over(blocks, ("zl", "zh")).T


def by_rank(axis, own, other):
    first = lax.axis_index(axis) == 0
    return jnp.stack([jnp.where(first, own, other), jnp.where(first, other, own)])


def whole_weight(out_weight):
    place = lax.axis_index("y") * 4 + lax.axis_index("x")
    piece = lax.dynamic_slice_in_dim(out_weight, place * 18, 18, 0)
    rows = lax.all_gather(piece, ("zh", "y", "x"), axis=0, tiled=False).reshape(2, 288, D)
    both = by_rank("c", rows, swap(rows, "c", 1))
    return both.transpose(1, 0, 2, 3).reshape(D, D)


def exchange(t):
    return lax.all_to_all(t, SEQ, split_axis=0, concat_axis=0, tiled=True)


def on_device(queries, keys, values, cotangent, out_weight):
    arrays = (queries, keys, values, cotangent)
    weight = whole_weight(out_weight)
    received = exchange(pack(arrays))
    by_patch, att, stats, mine, theirs = forward(received)
    weight_grad = weight_total(mine, theirs)
    sent = backward(by_patch, att, stats, weight)
    return (*unpack(exchange(sent)), weight_grad)


def solution(mesh):
    fine = Mesh(mesh.devices.reshape(4, 4, 4, 2, 2), ("y", "zl", "x", "zh", "c"))
    frames = P(ROWS, SEQ, None, None)
    return jax.shard_map(
        on_device,
        mesh=fine,
        in_specs=(frames, frames, frames, frames, P(ROWS, None)),
        out_specs=(frames, frames, frames, frames, P(ROWS, SEQ)),
        check_vma=False,
    )
```

time: 309 us -> 328 us (1.061)
  waiting for transfers between devices: 177 us -> 196 us
  Pallas kernels: 41.6 us -> 54.6 us
  local copies, waits for them, and re-layouts: 15.9 us -> 7.82 us
  other arithmetic: 8.61 us -> 2.53 us
    all_gather x1, waiting for transfers between devices: 83.7 us -> 113 us  [whole_weight(): lax.all_gather(piece, ('zh', 'y', 'x'), axis=0, tiled=False)]
    pallas_call x6 -> x5, Pallas kernels: 41.6 us -> 54.6 us  [the longest x1 20.6 us: backward(): pl.pallas_call(backward_kernel, in_specs=in_vmem(1) + in_hbm(4), out_spec...]
    unnamed x19 -> x5, local copies, waits for them, and re-layouts: 8.91 us -> 0.66 us
    all_to_all x2, waiting for transfers between devices: 8.23 us -> 0.21 us  [exchange(): return lax.all_to_all(t, SEQ, split_axis=0, concat_axis=0, tiled=True)]
    all_to_all x2, starting transfers between devices: 18.9 us -> 23.1 us  [exchange(): return lax.all_to_all(t, SEQ, split_axis=0, concat_axis=0, tiled=True)]
    another operation x3 -> x1, other arithmetic: 3.99 us -> 0.24 us  [by_rank(): jnp.stack([jnp.where(first, own, other), jnp.where(first, other, own)])]
    ppermute x13 -> x15, starting transfers between devices: 32 us -> 28.5 us  [swap(): return lax.ppermute(value, axis, [(i, i ^ k) for i in range(SIZES[axis])])]
    transpose x1, other arithmetic: 3.75 us -> 0.27 us  [whole_weight(): return both.transpose(1, 0, 2, 3).reshape(D, D)]
  transfers between devices with their start and end apart: 16 -> 18, of which waited for: 11 -> 11; matrix products, arithmetic and copies ran while one was open for 4% -> 3% of each run, Pallas kernels for 2% -> 1%
where the time goes in v2:
time: 328 us; the launch traced here: 327 us
  waiting for transfers between devices  196 us (60%)
  Pallas kernels  54.6 us (17%)
  starting transfers between devices  51.6 us (16%)
  between operations  14.3 us (4%)
  local copies, waits for them, and re-layouts  7.82 us (2%)
    all_gather x1, waiting for transfers between devices, whole_weight(): lax.all_gather(piece, ('zh', 'y', 'x'), axis=0, tiled=False)  113 us
    ppermute x15, waiting for transfers between devices, swap(): return lax.ppermute(value, axis, [(i, i ^ k) for i in range(SIZES[axis])])  82.7 us
    ppermute x15, starting transfers between devices, swap(): return lax.ppermute(value, axis, [(i, i ^ k) for i in range(SIZES[axis])])  28.5 us
    all_to_all x2, starting transfers between devices, exchange(): return lax.all_to_all(t, SEQ, split_axis=0, concat_axis=0, tiled=True)  23.1 us
    pallas_call x1, Pallas kernels, backward(): pl.pallas_call(backward_kernel, in_specs=in_vmem(1) + in_hbm(4), out_spec...  20.6 us
    pallas_call x1, Pallas kernels, forward(): pl.pallas_call(forward_kernel, in_specs=in_vmem(1) + in_hbm(1), out_specs...  19 us
  transfers between devices with their start and end apart: 18, of which 11 were waited for; matrix products, arithmetic and copies ran while one was open for 3% of the time, Pallas kernels for 1%

profile of v2, /device:TPU:2, one launch (start us, length us, event | category | flops | bytes accessed | tf_op | source)
XLA Modules:
  0.0 326.9 jit_solution(9033775663139364395)
XLA Ops:
  7.2 5.5 %pack.1 = bf16[64,32,1152]{2,1,0:T(8,128)(2,1)} custom-call(bf16[256,256]{1,0:T(8,128)(2,1)} %constant.76.clone.order_ref, bf16[1,2,256,1152]{3,2,1,0:T(8,128)(2,1)} %q_ref.1, bf16[1,2,256,1152]{3,2,1,0:T(8,128)(2,1)} %k_ref.1, bf16[1,2,256,1152]{3,2,1,0:T(8,128)(2,1)} %v_ref.1, bf16[1,2,256,1152]{3,2,1,0:T(8,128)(2,1)} %c_ref.1), custom_call_target="tpu_custom_call" | custom-call | flops 1207959552 | bytes 9437184 | tf_op jit(solution)/shard_map/pack/pallas_call | solution.py:102
  12.6 12.3 %all-to-all-start = ((bf16[64,32,1152]{2,1,0:T(8,128)(2,1)}), bf16[64,32,1152]{2,1,0:T(8,128)(2,1)}, u32[]{:S(2)}, u32[]{:S(2)}) async-start(bf16[64,32,1152]{2,1,0:T(8,128)(2,1)} %pack.1), calls=%async_computation | async-start | bytes 9437184 | tf_op jit(solution)/shard_map/all_to_all | solution.py:478
  25.6 113.1 %all-gather.4.cloned.1.call-done = bf16[32,18,1152]{2,1,0:T(8,128)(2,1)} async-done(((bf16[1,18,1152]{2,1,0:T(8,128)(2,1)}), bf16[32,18,1152]{2,1,0:T(8,128)(2,1)}) %all-gather.4.cloned.1.call-update) | async-done | bytes 1327120 | tf_op jit(solution)/shard_map/all_gather | solution.py:472
  138.8 2.4 reshape.31
  141.3 3.0 collective-permute-done
  144.9 1.7 copy.16
  146.8 19.0 %forward.1 = (bf16[2,4,256,1152]{3,2,1,0:T(8,128)(2,1)}, bf16[2,256,1152]{2,1,0:T(8,128)(2,1)}, f32[2,16,4,128]{3,2,1,0:T(4,128)}, f32[1152,576]{1,0:T(8,128)}, bf16[1152,576]{1,0:T(8,128)(2,1)}) custom-call(bf16[256,256]{1,0:T(8,128)(2,1)} %constant.77.clone.order_ref, bf16[64,32,1152]{2,1,0:T(8,128)(2,1)} %all-to-all-done.r_ref), custom_call_target="tpu_custom_call" | custom-call | flops 5000000000 | bytes 11796480 | tf_op jit(solution)/shard_map/forward/pallas_call | solution.py:211
  165.8 20.6 %backward.1 = bf16[64,32,1152]{2,1,0:T(8,128)(2,1)} custom-call(bf16[256,256]{1,0:T(8,128)(2,1)} %constant.78.clone.back_ref, bf16[2,4,256,1152]{3,2,1,0:T(8,128)(2,1)} %get-tuple-element.18.x_hbm, bf16[2,256,1152]{2,1,0:T(8,128)(2,1)} %get-tuple-element.19.att_hbm, f32[2,16,4,128]{3,2,1,0:T(4,128)} %get-tuple-element.20.stat_hbm, bf16[1152,1152]{1,0:T(8,128)(2,1)} %bitcast.53), custom_call_target="tpu_custom_call" | custom-call | flops 8999999488 | bytes 14450688 | tf_op jit(solution)/shard_map/backward/pallas_call | solution.py:311
  186.4 10.8 %all-to-all-start.1 = ((bf16[64,32,1152]{2,1,0:T(8,128)(2,1)}), bf16[64,32,1152]{2,1,0:T(8,128)(2,1)}, u32[]{:S(2)}, u32[]{:S(2)}) async-start(bf16[64,32,1152]{2,1,0:T(8,128)(2,1)} %backward.1), calls=%async_computation.1 | async-start | bytes 9437184 | tf_op jit(solution)/shard_map/all_to_all | solution.py:478
  198.4 3.0 collective-permute-done.1
  203.1 3.3 %halves.1 = (f32[288,576]{1,0:T(8,128)}, bf16[288,576]{1,0:T(8,128)(2,1)}, bf16[288,576]{1,0:T(8,128)(2,1)}, bf16[288,576]{1,0:T(8,128)(2,1)}) custom-call(f32[1152,576]{1,0:T(8,128)} %get-tuple-element.25.mine_hbm, bf16[1152,576]{1,0:T(8,128)(2,1)} %copy.18.other_hbm), custom_call_target="tpu_custom_call" | custom-call | flops 663552 | bytes 6635520 | tf_op jit(solution)/shard_map/halves/pallas_call | solution.py:420
  208.0 2.9 collective-permute-start.3
  211.2 33.2 %collective-permute-done.2 = bf16[288,576]{1,0:T(8,128)(2,1)S(1)} collective-permute-done((bf16[288,576]{1,0:T(8,128)(2,1)}, bf16[288,576]{1,0:T(8,128)(2,1)S(1)}, u32[]{:S(2)}, u32[]{:S(2)}) %collective-permute-start.2) | collective-permute-done | bytes 331808 | tf_op jit(solution)/shard_map/ppermute | solution.py:442
  244.4 15.2 %collective-permute-done.3 = bf16[288,576]{1,0:T(8,128)(2,1)S(1)} collective-permute-done((bf16[288,576]{1,0:T(8,128)(2,1)}, bf16[288,576]{1,0:T(8,128)(2,1)S(1)}, u32[]{:S(2)}, u32[]{:S(2)}) %collective-permute-start.3) | collective-permute-done | bytes 331808 | tf_op jit(solution)/shard_map/ppermute | solution.py:442
  261.1 2.0 collective-permute-start.5
  264.9 8.3 %collective-permute-done.5 = f32[4,18,576]{2,1,0:T(8,128)S(1)} collective-permute-done((f32[4,18,576]{2,1,0:T(8,128)S(1)}, f32[4,18,576]{2,1,0:T(8,128)S(1)}, u32[]{:S(2)}, u32[]{:S(2)}) %collective-permute-start.5) | collective-permute-done | bytes 165920 | tf_op jit(solution)/shard_map/ppermute | solution.py:442
  273.2 7.4 %collective-permute-done.6 = f32[4,18,576]{2,1,0:T(8,128)S(1)} collective-permute-done((f32[4,18,576]{2,1,0:T(8,128)S(1)}, f32[4,18,576]{2,1,0:T(8,128)S(1)}, u32[]{:S(2)}, u32[]{:S(2)}) %collective-permute-start.6) | collective-permute-done | bytes 165920 | tf_op jit(solution)/shard_map/ppermute | solution.py:442
  280.5 1.7 collective-permute-done.7
  282.7 9.9 %collective-permute-start.11 = (f32[18,288]{1,0:T(8,128)S(1)}, f32[18,288]{1,0:T(8,128)S(1)}, u32[]{:S(2)}, u32[]{:S(2)}) collective-permute-start(f32[18,288]{1,0:T(8,128)S(1)} %get-tuple-element.40), channel_id=1, source_target_pairs={{0,32},{2,34},{16,48},{18,50},{32,0},{34,2},{48,16},{50,18},{1,33}... | collective-permute-start | bytes 62216 | tf_op jit(solution)/shard_map/ppermute | solution.py:442
  292.9 6.0 %collective-permute-start.13 = (f32[18,288]{1,0:T(8,128)S(1)}, f32[18,288]{1,0:T(8,128)S(1)}, u32[]{:S(2)}, u32[]{:S(2)}) collective-permute-start(f32[18,288]{1,0:T(8,128)S(1)} %get-tuple-element.38), channel_id=1, source_target_pairs={{0,48},{2,50},{16,32},{18,34},{32,16},{34,18},{48,0},{50,2},{1,49}... | collective-permute-start | bytes 62216 | tf_op jit(solution)/shard_map/ppermute | solution.py:442
  298.9 6.0 %collective-permute-done.10 = f32[18,288]{1,0:T(8,128)S(1)} collective-permute-done((f32[18,288]{1,0:T(8,128)S(1)}, f32[18,288]{1,0:T(8,128)S(1)}, u32[]{:S(2)}, u32[]{:S(2)}) %collective-permute-start.10) | collective-permute-done | bytes 20768 | tf_op jit(solution)/shard_map/ppermute | solution.py:442
  305.0 3.3 %collective-permute-start.8 = (f32[18,288]{1,0:T(8,128)S(1)}, f32[18,288]{1,0:T(8,128)S(1)}, u32[]{:S(2)}, u32[]{:S(2)}) collective-permute-start(f32[18,288]{1,0:T(8,128)S(1)} %get-tuple-element.36), channel_id=1, source_target_pairs={{0,2},{2,0},{16,18},{18,16},{32,34},{34,32},{48,50},{50,48},{1,3},... | collective-permute-start | bytes 62216 | tf_op jit(solution)/shard_map/ppermute | solution.py:442
  308.3 4.8 %collective-permute-done.8 = f32[18,288]{1,0:T(8,128)S(1)} collective-permute-done((f32[18,288]{1,0:T(8,128)S(1)}, f32[18,288]{1,0:T(8,128)S(1)}, u32[]{:S(2)}, u32[]{:S(2)}) %collective-permute-start.8) | collective-permute-done | bytes 20768 | tf_op jit(solution)/shard_map/ppermute | solution.py:442
  313.7 6.3 %unpack.1 = (bf16[1,2,256,1152]{3,2,1,0:T(8,128)(2,1)}, bf16[1,2,256,1152]{3,2,1,0:T(8,128)(2,1)}, bf16[1,2,256,1152]{3,2,1,0:T(8,128)(2,1)}, bf16[1,2,256,1152]{3,2,1,0:T(8,128)(2,1)}) custom-call(bf16[256,256]{1,0:T(8,128)(2,1)} %constant.79.clone.order_ref, bf16[64,32,1152]{2,1,0:T(8,128)(2,1)} %all-to-all-done.1.slabs_ref), custom_call_target="tpu_custom_call" | custom-call | flops 1207959552 | bytes 9437184 | tf_op jit(solution)/shard_map/unpack/pallas_call | solution.py:372
  (38 shorter events, 10.9 us)
Async XLA Ops:
  7.2 17.8 %copy-start = (bf16[288,1152]{1,0:T(8,128)(2,1)S(1)}, bf16[288,1152]{1,0:T(8,128)(2,1)}, u32[]{:S(2)}) copy-start(bf16[288,1152]{1,0:T(8,128)(2,1)} %param.13) | copy-start | bytes 1990660
  12.6 134.1 %all-to-all-start = ((bf16[64,32,1152]{2,1,0:T(8,128)(2,1)}), bf16[64,32,1152]{2,1,0:T(8,128)(2,1)}, u32[]{:S(2)}, u32[]{:S(2)}) async-start(bf16[64,32,1152]{2,1,0:T(8,128)(2,1)} %pack.1), calls=%async_computation | async-start | bytes 9437184 | tf_op jit(solution)/shard_map/all_to_all | solution.py:478
  24.9 113.9 %all-gather.4.cloned.1.call-start = ((), (), s32[]{:S(2)}) async-start(), calls=%async_computation.2 | async-start | bytes 1824768 | tf_op jit(solution)/shard_map/all_gather | solution.py:472
  141.2 3.1 collective-permute-start
  186.4 10.8 %copy-start.1 = (bf16[1152,576]{1,0:T(8,128)(2,1)S(1)}, bf16[1152,576]{1,0:T(8,128)(2,1)}, u32[]{:S(2)}) copy-start(bf16[1152,576]{1,0:T(8,128)(2,1)} %get-tuple-element.26) | copy-start | bytes 3981316
  186.4 127.3 %all-to-all-start.1 = ((bf16[64,32,1152]{2,1,0:T(8,128)(2,1)}), bf16[64,32,1152]{2,1,0:T(8,128)(2,1)}, u32[]{:S(2)}, u32[]{:S(2)}) async-start(bf16[64,32,1152]{2,1,0:T(8,128)(2,1)} %backward.1), calls=%async_computation.1 | async-start | bytes 9437184 | tf_op jit(solution)/shard_map/all_to_all | solution.py:478
  198.3 3.1 collective-permute-start.1
  206.4 37.9 %collective-permute-start.2 = (bf16[288,576]{1,0:T(8,128)(2,1)}, bf16[288,576]{1,0:T(8,128)(2,1)S(1)}, u32[]{:S(2)}, u32[]{:S(2)}) collective-permute-start(bf16[288,576]{1,0:T(8,128)(2,1)} %get-tuple-element.28), channel_id=1, source_target_pairs={{0,64},{64,0},{128,192},{192,128},{1,65},{65,1},{129,193},{193,129... | collective-permute-start | bytes 995336 | tf_op jit(solution)/shard_map/ppermute | solution.py:442
  208.0 51.6 %collective-permute-start.3 = (bf16[288,576]{1,0:T(8,128)(2,1)}, bf16[288,576]{1,0:T(8,128)(2,1)S(1)}, u32[]{:S(2)}, u32[]{:S(2)}) collective-permute-start(bf16[288,576]{1,0:T(8,128)(2,1)} %get-tuple-element.29), channel_id=1, source_target_pairs={{0,128},{64,192},{128,0},{192,64},{1,129},{65,193},{129,1},{193,65... | collective-permute-start | bytes 995336 | tf_op jit(solution)/shard_map/ppermute | solution.py:442
  210.9 48.7 %collective-permute-start.4 = (bf16[288,576]{1,0:T(8,128)(2,1)}, bf16[288,576]{1,0:T(8,128)(2,1)S(1)}, u32[]{:S(2)}, u32[]{:S(2)}) collective-permute-start(bf16[288,576]{1,0:T(8,128)(2,1)} %get-tuple-element.30), channel_id=1, source_target_pairs={{0,192},{64,128},{128,64},{192,0},{1,193},{65,129},{129,65},{193,1... | collective-permute-start | bytes 995336 | tf_op jit(solution)/shard_map/ppermute | solution.py:442
  261.1 12.1 %collective-permute-start.5 = (f32[4,18,576]{2,1,0:T(8,128)S(1)}, f32[4,18,576]{2,1,0:T(8,128)S(1)}, u32[]{:S(2)}, u32[]{:S(2)}) collective-permute-start(f32[4,18,576]{2,1,0:T(8,128)S(1)} %get-tuple-element.33), channel_id=1, source_target_pairs={{0,4},{4,0},{8,12},{12,8},{1,5},{5,1},{9,13},{13,9},{2,6},{6,2},{1... | collective-permute-start | bytes 497672 | tf_op jit(solution)/shard_map/ppermute | solution.py:442
  263.1 17.4 %collective-permute-start.6 = (f32[4,18,576]{2,1,0:T(8,128)S(1)}, f32[4,18,576]{2,1,0:T(8,128)S(1)}, u32[]{:S(2)}, u32[]{:S(2)}) collective-permute-start(f32[4,18,576]{2,1,0:T(8,128)S(1)} %get-tuple-element.35), channel_id=1, source_target_pairs={{0,8},{4,12},{8,0},{12,4},{1,9},{5,13},{9,1},{13,5},{2,10},{6,14},... | collective-permute-start | bytes 497672 | tf_op jit(solution)/shard_map/ppermute | solution.py:442
  263.3 19.0 %collective-permute-start.7 = (f32[4,18,576]{2,1,0:T(8,128)S(1)}, f32[4,18,576]{2,1,0:T(8,128)S(1)}, u32[]{:S(2)}, u32[]{:S(2)}) collective-permute-start(f32[4,18,576]{2,1,0:T(8,128)S(1)} %get-tuple-element.34), channel_id=1, source_target_pairs={{0,12},{4,8},{8,4},{12,0},{1,13},{5,9},{9,5},{13,1},{2,14},{6,10},... | collective-permute-start | bytes 497672 | tf_op jit(solution)/shard_map/ppermute | solution.py:442
  282.6 22.4 %collective-permute-start.10 = (f32[18,288]{1,0:T(8,128)S(1)}, f32[18,288]{1,0:T(8,128)S(1)}, u32[]{:S(2)}, u32[]{:S(2)}) collective-permute-start(f32[18,288]{1,0:T(8,128)S(1)} %get-tuple-element.41), channel_id=1, source_target_pairs={{0,18},{2,16},{16,2},{18,0},{32,50},{34,48},{48,34},{50,32},{1,19}... | collective-permute-start | bytes 62216 | tf_op jit(solution)/shard_map/ppermute | solution.py:442
  282.7 25.6 %collective-permute-start.11 = (f32[18,288]{1,0:T(8,128)S(1)}, f32[18,288]{1,0:T(8,128)S(1)}, u32[]{:S(2)}, u32[]{:S(2)}) collective-permute-start(f32[18,288]{1,0:T(8,128)S(1)} %get-tuple-element.40), channel_id=1, source_target_pairs={{0,32},{2,34},{16,48},{18,50},{32,0},{34,2},{48,16},{50,18},{1,33}... | collective-permute-start | bytes 62216 | tf_op jit(solution)/shard_map/ppermute | solution.py:442
  292.5 15.8 %collective-permute-start.12 = (f32[18,288]{1,0:T(8,128)S(1)}, f32[18,288]{1,0:T(8,128)S(1)}, u32[]{:S(2)}, u32[]{:S(2)}) collective-permute-start(f32[18,288]{1,0:T(8,128)S(1)} %get-tuple-element.39), channel_id=1, source_target_pairs={{0,34},{2,32},{16,50},{18,48},{32,2},{34,0},{48,18},{50,16},{1,35}... | collective-permute-start | bytes 62216 | tf_op jit(solution)/shard_map/ppermute | solution.py:442
  292.9 15.4 %collective-permute-start.13 = (f32[18,288]{1,0:T(8,128)S(1)}, f32[18,288]{1,0:T(8,128)S(1)}, u32[]{:S(2)}, u32[]{:S(2)}) collective-permute-start(f32[18,288]{1,0:T(8,128)S(1)} %get-tuple-element.38), channel_id=1, source_target_pairs={{0,48},{2,50},{16,32},{18,34},{32,16},{34,18},{48,0},{50,2},{1,49}... | collective-permute-start | bytes 62216 | tf_op jit(solution)/shard_map/ppermute | solution.py:442
  298.9 9.4 %collective-permute-start.14 = (f32[18,288]{1,0:T(8,128)S(1)}, f32[18,288]{1,0:T(8,128)S(1)}, u32[]{:S(2)}, u32[]{:S(2)}) collective-permute-start(f32[18,288]{1,0:T(8,128)S(1)} %get-tuple-element.37), channel_id=1, source_target_pairs={{0,50},{2,48},{16,34},{18,32},{32,18},{34,16},{48,2},{50,0},{1,51}... | collective-permute-start | bytes 62216 | tf_op jit(solution)/shard_map/ppermute | solution.py:442
  305.0 8.1 %collective-permute-start.8 = (f32[18,288]{1,0:T(8,128)S(1)}, f32[18,288]{1,0:T(8,128)S(1)}, u32[]{:S(2)}, u32[]{:S(2)}) collective-permute-start(f32[18,288]{1,0:T(8,128)S(1)} %get-tuple-element.36), channel_id=1, source_target_pairs={{0,2},{2,0},{16,18},{18,16},{32,34},{34,32},{48,50},{50,48},{1,3},... | collective-permute-start | bytes 62216 | tf_op jit(solution)/shard_map/ppermute | solution.py:442
  308.3 4.8 %collective-permute-start.9 = (f32[18,288]{1,0:T(8,128)S(1)}, f32[18,288]{1,0:T(8,128)S(1)}, u32[]{:S(2)}, u32[]{:S(2)}) collective-permute-start(f32[18,288]{1,0:T(8,128)S(1)} %get-tuple-element.42), channel_id=1, source_target_pairs={{0,16},{2,18},{16,0},{18,2},{32,48},{34,50},{48,32},{50,34},{1,17}... | collective-permute-start | bytes 62216 | tf_op jit(solution)/shard_map/ppermute | solution.py:442
Sparse Core Ops, SparseCore 0:
  29.7 109.0 all-gather.3

commit v3 on v1

--- a/solution.py
+++ b/solution.py
@@ -59,61 +59,63 @@
     return pltpu.CompilerParams(vmem_limit_bytes=mib * MIB)
 
 
-def anywhere(count):
-    return [pl.BlockSpec(memory_space=pl.ANY)] * count
+def in_hbm(count):
+    return [pl.BlockSpec(memory_space=pltpu.HBM)] * count
 
 
 def in_vmem(count):
     return [pl.BlockSpec(memory_space=pltpu.VMEM)] * count
 
 
-def pack_kernel(part, order_ref, q_ref, k_ref, v_ref, c_ref, *refs):
-    out_ref, rows_ref, slabs_ref, in_sem, out_sem = refs[-5:]
+def pack_kernel(order_ref, q_ref, k_ref, v_ref, c_ref, token, out_ref, rows_ref, slabs_ref, in_sem, out_sem):
     arrays = (q_ref, k_ref, v_ref, c_ref)
     coming, going = [], []
-    for a in range(4):
-        coming.append(
-            pltpu.make_async_copy(
-                arrays[a].at[0, :, pl.ds(part * 128, 128), :], rows_ref.at[a], in_sem.at[a]
+    for part in range(2):
+        for a in range(4):
+            coming.append(
+                pltpu.make_async_copy(
+                    arrays[a].at[0, :, pl.ds(part * 128, 128), :],
+                    rows_ref.at[part, a],
+                    in_sem.at[part, a],
+                )
             )
-        )
-        coming[-1].start()
-    for copy in coming:
-        copy.wait()
-    for g in range(4):
-        rows = [rows_ref[a, f, pl.ds(g * 32, 32), :] for a in range(4) for f in range(2)]
-        slabs_ref[g] = move(order_ref[...], jnp.concatenate(rows, axis=0)).reshape(16, 16, D)
-        going.append(
-            pltpu.make_async_copy(
-                slabs_ref.at[g],
-                out_ref.at[pl.ds(g * 16, 16), pl.ds(part * 16, 16), :],
-                out_sem.at[g],
+            coming[-1].start()
+    for part in range(2):
+        for a in range(4):
+            coming[4 * part + a].wait()
+        for g in range(4):
+            rows = [rows_ref[part, a, f, pl.ds(g * 32, 32), :] for a in range(4) for f in range(2)]
+            slabs_ref[part, g] = move(order_ref[...], jnp.concatenate(rows, axis=0)).reshape(16, 16, D)
+            going.append(
+                pltpu.make_async_copy(
+                    slabs_ref.at[part, g],
+                    out_ref.at[pl.ds(g * 16, 16), pl.ds(part * 16, 16), :],
+                    out_sem.at[part, g],
+                )
             )
-        )
-        going[-1].start()
+            going[-1].start()
     for copy in going:
         copy.wait()
 
 
-def pack(part, arrays, before):
-    return pl.pallas_call(
-        functools.partial(pack_kernel, part),
-        in_specs=in_vmem(1) + anywhere(4 + len(before)),
-        out_specs=pl.BlockSpec(memory_space=pl.ANY),
+def pack(arrays, token):
+    return pl.pallas_call(
+        pack_kernel,
+        in_specs=in_vmem(1) + in_hbm(4) + [pl.BlockSpec(memory_space=pl.ANY)],
+        out_specs=pl.BlockSpec(memory_space=pltpu.HBM),
         out_shape=jax.ShapeDtypeStruct((64, 32, D), BF16),
         scratch_shapes=[
-            pltpu.VMEM((4, 2, 128, D), BF16),
-            pltpu.VMEM((4, 16, 16, D), BF16),
-            pltpu.SemaphoreType.DMA((4,)),
-            pltpu.SemaphoreType.DMA((4,)),
+            pltpu.VMEM((2, 4, 2, 128, D), BF16),
+            pltpu.VMEM((2, 4, 16, 16, D), BF16),
+            pltpu.SemaphoreType.DMA((2, 4)),
+            pltpu.SemaphoreType.DMA((2, 4)),
         ],
-        input_output_aliases={5: 0} if before else {},
         compiler_params=params(60),
         cost_estimate=pl.CostEstimate(
-            flops=2 * 1024 * 256 * D, bytes_accessed=4096 * D, transcendentals=0
+            flops=2 * 2048 * 256 * D, bytes_accessed=8192 * D, transcendentals=0
         ),
         name="pack",
-    )(const(order_to_slabs(2)), *arrays, *before)
+    )(const(order_to_slabs(2)), *arrays, token)
 
 
 def attend_part(part, order_ref, back_ref, r_ref, w_ref, s_ref, att_ref, cot_ref, *refs):
@@ -218,8 +220,8 @@
     order = order_to_patches(2)
     return pl.pallas_call(
         attend_kernel,
-        in_specs=in_vmem(2) + anywhere(1) + in_vmem(1),
-        out_specs=anywhere(3),
+        in_specs=in_vmem(2) + in_hbm(1) + in_vmem(1),
+        out_specs=in_hbm(3),
         out_shape=[
             jax.ShapeDtypeStruct((64, 32, D), BF16),
             jax.ShapeDtypeStruct((512, D), BF16),
@@ -236,7 +238,7 @@
             pltpu.SemaphoreType.DMA((8,)),
             pltpu.SemaphoreType.DMA((2, 2)),
         ],
-        compiler_params=params(40),
+        compiler_params=params(58),
         cost_estimate=pl.CostEstimate(
             flops=12_000_000_000, bytes_accessed=40 * 256 * D + 2 * D * D, transcendentals=1048576
         ),
@@ -281,8 +283,8 @@
 def unpack(slabs):
     return pl.pallas_call(
         unpack_kernel,
-        in_specs=in_vmem(1) + anywhere(1),
-        out_specs=anywhere(4),
+        in_specs=in_vmem(1) + in_hbm(1),
+        out_specs=in_hbm(4),
         out_shape=[jax.ShapeDtypeStruct((1, 2, 256, D), BF16)] * 4,
         scratch_shapes=[
             pltpu.VMEM((8, 16, 16, D), BF16),
@@ -298,25 +300,34 @@
     )(const(order_to_slabs(2).T.copy()), slabs)
 
 
-def outer_kernel(att_ref, cot_ref, mine_ref, theirs_ref):
+def outer_kernel(turn_ref, att_ref, cot_ref, mine_ref, theirs_ref):
     att = att_ref[...]
     cot = cot_ref[...]
+    turned = move(cot, turn_ref[...])
     parts = [att[:, 288 * b : 288 * b + 288] for b in range(4)]
-    even = jnp.concatenate([parts[0], parts[2]], axis=1)
-    odd = jnp.concatenate([parts[1], parts[3]], axis=1)
     core = lax.axis_index("c")
 
-    def product(t):
-        return lax.dot_general(cot, t, (((0,), (0,)), ((), ())), preferred_element_type=F32)
-
-    mine_ref[...] = product(jnp.where(core == 0, even, odd))
-    theirs_ref[...] = product(jnp.where(core == 0, odd, even)).astype(theirs_ref.dtype)
+    def product(left, even, odd):
+        chosen = jnp.where(core == 0, even, odd)
+        return lax.dot_general(left, chosen, (((0,), (0,)), ((), ())), preferred_element_type=F32)
+
+    theirs_ref[:, :288] = product(cot, parts[1], parts[0]).astype(BF16)
+    theirs_ref[:, 288:] = product(turned, parts[3], parts[2]).astype(BF16)
+    mine_ref[:, :288] = product(cot, parts[0], parts[1])
+    mine_ref[:, 288:] = product(turned, parts[2], parts[3])
+
+
+def turn():
+    order = np.arange(D).reshape(4, 4, 4, 18).transpose(2, 0, 1, 3).reshape(-1)
+    out = np.zeros((D, D), np.float32)
+    out[order, np.arange(D)] = 1
+    return const(out)
 
 
 def outer(att, cot):
     return pl.pallas_call(
         outer_kernel,
-        in_specs=in_vmem(2),
+        in_specs=in_vmem(3),
         out_specs=in_vmem(2),
         out_shape=[jax.ShapeDtypeStruct((D, 576), F32), jax.ShapeDtypeStruct((D, 576), BF16)],
         compiler_params=params(24),
@@ -324,56 +335,78 @@
             flops=2 * 512 * D * D, bytes_accessed=4 * 512 * D + 6 * D * 576, transcendentals=0
         ),
         name="outer",
-    )(att, cot)
+    )(turn(), att, cot)
 
 
 def halves_kernel(mine_ref, other_ref, own_ref, *out_refs):
-    y = lax.axis_index("y")
-    for k in range(4):
-        rows = pl.ds(pl.multiple_of((y ^ k) * 288, 32), 288)
-        total = mine_ref[rows, :] + other_ref[rows, :].astype(F32)
-        if k == 0:
-            own_ref[...] = total
-        else:
-            out_refs[k - 1][...] = total.astype(BF16)
+    for i, axis in enumerate(("y", "x")):
+        columns = slice(288 * i, 288 * i + 288)
+        at = lax.axis_index(axis)
+        for k in range(4):
+            rows = pl.ds(pl.multiple_of((at ^ k) * 288, 32), 288)
+            total = mine_ref[rows, columns] + other_ref[rows, columns].astype(F32)
+            if k == 0:
+                own_ref[i] = total
+            else:
+                out_refs[3 * i + k - 1][...] = total.astype(BF16)
 
 
 def halves(mine, other):
     return pl.pallas_call(
         halves_kernel,
         in_specs=in_vmem(2),
-        out_specs=in_vmem(4),
-        out_shape=[jax.ShapeDtypeStruct((288, 576), F32)] + [jax.ShapeDtypeStruct((288, 576), BF16)] * 3,
+        out_specs=in_vmem(7),
+        out_shape=[jax.ShapeDtypeStruct((2, 288, 288), F32)] + [jax.ShapeDtypeStruct((288, 288), BF16)] * 6,
         compiler_params=params(24),
         cost_estimate=pl.CostEstimate(flops=D * 576, bytes_accessed=10 * D * 576, transcendentals=0),
         name="halves",
     )(mine, other)
 
 
+SIZES = {"y": 4, "x": 4, "zl": 4, "zh": 2, "c": 2, ("zl", "zh"): 8}
+
+
 def swap(value, axis, k):
-    size = 2 if axis in ("zh", "c") else 4
-    return lax.ppermute(value, axis, [(i, i ^ k) for i in range(size)])
-
-
-def sum_over(blocks, axis, size):
+    return lax.ppermute(value, axis, [(i, i ^ k) for i in range(SIZES[axis])])
+
+
+def terms_over(blocks, axis):
     at = lax.axis_index(axis)
-    total = lax.dynamic_index_in_dim(blocks, at, 0, keepdims=False)
-    for k in range(1, size):
-        total = total + swap(lax.dynamic_index_in_dim(blocks, at ^ k, 0, keepdims=False), axis, k)
-    return total
-
-
-def weight_total(att, cot):
+    own = lax.dynamic_index_in_dim(blocks, at, 0, keepdims=False)
+    return [own] + [
+        swap(lax.dynamic_index_in_dim(blocks, at ^ k, 0, keepdims=False), axis, k)
+        for k in range(1, SIZES[axis])
+    ]
+
+
+def weight_terms(att, cot):
     mine, theirs = outer(att, cot)
     own, *sent = halves(mine, swap(theirs, "c", 1))
-    total = own
+    here, there = own[0], own[1]
     for k in range(1, 4):
-        total = total + swap(sent[k - 1], "y", k).astype(F32)
-    blocks = total.reshape(4, 4, 18, 576).transpose(1, 0, 2, 3)
-    blocks = sum_over(blocks, "x", 4)
-    blocks = sum_over(blocks, "zl", 4)
-    blocks = blocks.reshape(18, 2, 288).transpose(1, 0, 2)
-    return sum_over(blocks, "zh", 2).T
+        here = here + swap(sent[k - 1], "y", k).astype(F32)
+        there = there + swap(sent[k + 2], "x", k).astype(F32)
+    here = sum(terms_over(here.reshape(4, 4, 18, 288).transpose(1, 0, 2, 3), "x"))
+    there = sum(terms_over(there.reshape(4, 4, 18, 288), "y"))
+    return terms_over(jnp.stack([here, there], axis=1).reshape(8, 18, 288), ("zl", "zh"))
+
+
+def add_up_kernel(*refs):
+    total = refs[0][...]
+    for ref in refs[1:8]:
+        total = total + ref[...]
+    refs[-1][...] = total
+
+
+def add_up(terms, token):
+    return pl.pallas_call(
+        add_up_kernel,
+        in_specs=in_vmem(8) + [pl.BlockSpec(memory_space=pl.ANY)],
+        out_specs=pl.BlockSpec(memory_space=pltpu.VMEM),
+        out_shape=jax.ShapeDtypeStruct((18, 288), F32),
+        compiler_params=params(8),
+        name="add_up",
+    )(*terms, token)
 
 
 def by_rank(axis, own, other):
@@ -381,13 +414,8 @@
     return jnp.stack([jnp.where(first, own, other), jnp.where(first, other, own)])
 
 
-def weight_piece(out_weight):
-    place = lax.axis_index("y") * 4 + lax.axis_index("x")
-    piece = lax.dynamic_slice_in_dim(out_weight, place * 18, 18, 0)
-    return by_rank("zh", piece, swap(piece, "zh", 1))
-
-
-def whole_weight(pair):
+def whole_weight(piece, other):
+    pair = by_rank("zh", piece, other)
     rows = lax.all_gather(pair, ("y", "x"), axis=0, tiled=False)
     rows = rows.transpose(1, 0, 2, 3).reshape(2, 288, D)
     both = by_rank("c", rows, swap(rows, "c", 1))
@@ -400,13 +428,14 @@
 
 def on_device(queries, keys, values, cotangent, out_weight):
     arrays = (queries, keys, values, cotangent)
-    pair = weight_piece(out_weight)
-    packed = pack(0, arrays, ())
-    packed = pack(1, arrays, (packed, pair))
-    received = exchange(packed)
-    sent, att, cot = attend(received, whole_weight(pair))
-    weight_grad = weight_total(att, cot)
-    return (*unpack(exchange(sent)), weight_grad)
+    place = lax.axis_index("y") * 4 + lax.axis_index("x")
+    piece = lax.dynamic_slice_in_dim(out_weight, place * 18, 18, 0)
+    other = swap(piece, "zh", 1)
+    received = exchange(pack(arrays, other))
+    sent, att, cot = attend(received, whole_weight(piece, other))
+    terms = weight_terms(att, cot)
+    outs = unpack(exchange(sent))
+    return (*outs, add_up(terms, outs[0]).T)
 
 
 def solution(mesh):

time: 309 us -> 304 us (0.984); the launches traced: 309 us -> 300 us
  waiting for transfers between devices: 177 us -> 136 us
  starting transfers between devices: 51 us -> 83.1 us
    ppermute x13 -> x22, waiting for transfers between devices: 84.7 us -> 38.5 us  [swap(): return lax.ppermute(value, axis, [(i, i ^ k) for i in range(SIZES[axis])])]
    ppermute x13 -> x22, starting transfers between devices: 32 us -> 59.7 us  [swap(): return lax.ppermute(value, axis, [(i, i ^ k) for i in range(SIZES[axis])])]
    all_to_all x2, waiting for transfers between devices: 8.23 us -> 14.4 us  [exchange(): return lax.all_to_all(t, SEQ, split_axis=0, concat_axis=0, tiled=True)]
    all_to_all x2, starting transfers between devices: 18.9 us -> 23.3 us  [exchange(): return lax.all_to_all(t, SEQ, split_axis=0, concat_axis=0, tiled=True)]
    unnamed x19 -> x16, local copies, waits for them, and re-layouts: 8.91 us -> 8.36 us
  transfers between devices with their start and end apart: 16 -> 25, of which waited for: 11 -> 14; matrix products, arithmetic and copies ran while one was open for 4% -> 5% of each run, Pallas kernels for 2% -> 4%
where the time goes in v3:
time: 304 us; the launch traced here: 300 us
  waiting for transfers between devices  136 us (45%)
  starting transfers between devices  83.1 us (27%)
  Pallas kernels  41.6 us (14%)
  local copies, waits for them, and re-layouts  16.8 us (6%)
  between operations  14.6 us (5%)
  other arithmetic  8.04 us (3%)
    all_gather x1, waiting for transfers between devices, whole_weight(): rows = lax.all_gather(pair, ('y', 'x'), axis=0, tiled=False)  82.8 us
    ppermute x22, starting transfers between devices, swap(): return lax.ppermute(value, axis, [(i, i ^ k) for i in range(SIZES[axis])])  59.7 us
    ppermute x22, waiting for transfers between devices, swap(): return lax.ppermute(value, axis, [(i, i ^ k) for i in range(SIZES[axis])])  38.5 us
    pallas_call x1, Pallas kernels, attend(): pl.pallas_call(attend_kernel, in_specs=in_vmem(2) + in_hbm(1) + in_vmem(1...  24.1 us
    all_to_all x2, starting transfers between devices, exchange(): return lax.all_to_all(t, SEQ, split_axis=0, concat_axis=0, tiled=True)  23.3 us
    all_to_all x2, waiting for transfers between devices, exchange(): return lax.all_to_all(t, SEQ, split_axis=0, concat_axis=0, tiled=True)  14.4 us
    unnamed x16, local copies, waits for them, and re-layouts  8.36 us
    pallas_call x1, Pallas kernels, unpack(): pl.pallas_call(unpack_kernel, in_specs=in_vmem(1) + in_hbm(1), out_specs=...  6.28 us
  transfers between devices with their start and end apart: 25, of which 14 were waited for; matrix products, arithmetic and copies ran while one was open for 5% of the time, Pallas kernels for 4%

profile of v3, /device:TPU:2, one launch (start us, length us, event | category | flops | bytes accessed | tf_op | source)
XLA Modules:
  0.0 299.7 jit_solution(18219681276044324955)
XLA Ops:
  8.1 7.3 %collective-permute-start = (bf16[18,1152]{1,0:T(8,128)(2,1)S(1)}, bf16[18,1152]{1,0:T(8,128)(2,1)S(1)}, u32[]{:S(2)}, u32[]{:S(2)}) collective-permute-start(bf16[18,1152]{1,0:T(8,128)(2,1)S(1)} %constant_dynamic-slice_fusion), channel_id=1, source_target_pairs={{0,2},{2,0},{1,3},{3,1},{4,6},{6,4},{5,7},{7,5},{8,10},{10,8},{9,1... | collective-permute-start | bytes 124424 | tf_op jit(solution)/shard_map/ppermute | solution.py:370
  18.1 5.4 %pack.1 = bf16[64,32,1152]{2,1,0:T(8,128)(2,1)} custom-call(bf16[256,256]{1,0:T(8,128)(2,1)} %constant.86.clone.order_ref, bf16[1,2,256,1152]{3,2,1,0:T(8,128)(2,1)} %q_ref.1, bf16[1,2,256,1152]{3,2,1,0:T(8,128)(2,1)} %k_ref.1, bf16[1,2,256,1152]{3,2,1,0:T(8,128)(2,1)} %v_ref.1, bf16[1,2,256,1152]{3,2,1,0:T(8,128)(2,1)} %c_ref.1, bf16[18,1152]{1,0:T(8,128)(2,1)} %copy-done.6), custom_call_target="tpu_custom_call" | custom-call | flops 1207959552 | bytes 9437184 | tf_op jit(solution)/shard_map/pack/pallas_call | solution.py:102
  23.5 11.1 %all-to-all-start = ((bf16[64,32,1152]{2,1,0:T(8,128)(2,1)}), bf16[64,32,1152]{2,1,0:T(8,128)(2,1)}, u32[]{:S(2)}, u32[]{:S(2)}) async-start(bf16[64,32,1152]{2,1,0:T(8,128)(2,1)} %pack.1), calls=%async_computation | async-start | bytes 9437184 | tf_op jit(solution)/shard_map/all_to_all | solution.py:426
  36.3 82.8 %all-gather.3.cloned.1.call-done = bf16[32,18,1152]{2,1,0:T(8,128)(2,1)} async-done(((bf16[2,18,1152]{2,1,0:T(8,128)(2,1)}), bf16[32,18,1152]{2,1,0:T(8,128)(2,1)}) %all-gather.3.cloned.1.call-update) | async-done | bytes 1327120 | tf_op jit(solution)/shard_map/all_gather | solution.py:419
  119.1 2.5 copy.20
  122.2 3.0 %collective-permute-done.1 = bf16[2,288,1152]{2,0,1:T(2,128)(2,1)S(1)} collective-permute-done((bf16[2,288,1152]{2,0,1:T(2,128)(2,1)S(1)}, bf16[2,288,1152]{2,0,1:T(2,128)(2,1)S(1)}, u32[]{:S(2)}, u32[]{:S(2)}) %collective-permute-start.1) | collective-permute-done | bytes 1327136 | tf_op jit(solution)/shard_map/ppermute | solution.py:370
  127.7 3.8 %maximum_bitcast_fusion = bf16[2,2,288,1152]{3,0,2,1:T(2,128)(2,1)S(1)} fusion(bf16[1,2,288,1152]{3,1,2,0:T(2,128)(2,1)S(1)} %get-tuple-element.38, bf16[1,2,288,1152]{3,1,2,0:T(2,128)(2,1)S(1)} %get-tuple-element.37), kind=kLoop, calls=%fused_computation | loop fusion | flops 1327104 | bytes 5308416 | tf_op jit(solution)/shard_map/transpose | solution.py:422
  133.3 5.5 %all-to-all-done.refs_2_ = bf16[64,32,1152]{2,1,0:T(8,128)(2,1)} async-done(((bf16[64,32,1152]{2,1,0:T(8,128)(2,1)}), bf16[64,32,1152]{2,1,0:T(8,128)(2,1)}, u32[]{:S(2)}, u32[]{:S(2)}) %all-to-all-start) | async-done | bytes 4718624 | tf_op jit(solution)/shard_map/all_to_all | solution.py:426
  138.7 24.1 %attend.1 = (bf16[64,32,1152]{2,1,0:T(8,128)(2,1)}, bf16[512,1152]{1,0:T(8,128)(2,1)}, bf16[512,1152]{1,0:T(8,128)(2,1)}) custom-call(bf16[256,256]{1,0:T(8,128)(2,1)} %constant.87.clone.refs_0_, bf16[256,256]{1,0:T(8,128)(2,1)} %constant.88.clone.refs_1_, bf16[64,32,1152]{2,1,0:T(8,128)(2,1)} %all-to-all-done.refs_2_, bf16[1152,1152]{1,0:T(8,128)(2,1)} %bitcast.82), custom_call_target="tpu_custom_call" | custom-call | flops 12000000000 | bytes 14450688 | tf_op jit(solution)/shard_map/attend/pallas_call | solution.py:221
  162.8 12.2 %all-to-all-start.1 = ((bf16[64,32,1152]{2,1,0:T(8,128)(2,1)}), bf16[64,32,1152]{2,1,0:T(8,128)(2,1)}, u32[]{:S(2)}, u32[]{:S(2)}) async-start(bf16[64,32,1152]{2,1,0:T(8,128)(2,1)} %get-tuple-element.21), calls=%async_computation.1 | async-start | bytes 9437184 | tf_op jit(solution)/shard_map/all_to_all | solution.py:426
  178.0 4.5 %outer.1 = (f32[1152,576]{1,0:T(8,128)S(1)}, bf16[1152,576]{1,0:T(8,128)(2,1)S(1)}) custom-call(bf16[1152,1152]{1,0:T(8,128)(2,1)S(1)} %copy-done.3, bf16[512,1152]{1,0:T(8,128)(2,1)S(1)} %copy-done.4, bf16[512,1152]{1,0:T(8,128)(2,1)S(1)} %copy-done.5), custom_call_target="tpu_custom_call" | custom-call | flops 1358954496 | bytes 6340608 | tf_op jit(solution)/shard_map/outer/pallas_call | solution.py:328
  186.0 3.3 %collective-permute-done.2 = bf16[1152,576]{0,1:T(8,128)(2,1)S(1)} collective-permute-done((bf16[1152,576]{0,1:T(8,128)(2,1)}, bf16[1152,576]{0,1:T(8,128)(2,1)S(1)}, u32[]{:S(2)}, u32[]{:S(2)}) %collective-permute-start.2) | collective-permute-done | bytes 1327136 | tf_op jit(solution)/shard_map/ppermute | solution.py:370
  196.6 2.9 collective-permute-start.4
  199.8 10.8 %collective-permute-done.10 = bf16[288,288]{1,0:T(8,128)(2,1)S(1)} collective-permute-done((bf16[288,288]{1,0:T(8,128)(2,1)S(1)}, bf16[288,288]{1,0:T(8,128)(2,1)S(1)}, u32[]{:S(2)}, u32[]{:S(2)}) %collective-permute-start.10) | collective-permute-done | bytes 165920 | tf_op jit(solution)/shard_map/ppermute | solution.py:370
  210.6 8.8 %collective-permute-start.9 = (bf16[288,288]{1,0:T(8,128)(2,1)S(1)}, bf16[288,288]{1,0:T(8,128)(2,1)S(1)}, u32[]{:S(2)}, u32[]{:S(2)}) collective-permute-start(bf16[288,288]{1,0:T(8,128)(2,1)S(1)} %get-tuple-element.34), channel_id=1, source_target_pairs={{0,4},{4,0},{8,12},{12,8},{1,5},{5,1},{9,13},{13,9},{2,6},{6,2},{1... | collective-permute-start | bytes 497672 | tf_op jit(solution)/shard_map/ppermute | solution.py:370
  221.6 5.7 %collective-permute-done.4 = bf16[288,288]{1,0:T(8,128)(2,1)S(1)} collective-permute-done((bf16[288,288]{1,0:T(8,128)(2,1)S(1)}, bf16[288,288]{1,0:T(8,128)(2,1)S(1)}, u32[]{:S(2)}, u32[]{:S(2)}) %collective-permute-start.4) | collective-permute-done | bytes 165920 | tf_op jit(solution)/shard_map/ppermute | solution.py:370
  227.9 4.9 %collective-permute-start.6 = (f32[4,18,288]{2,1,0:T(8,128)S(1)}, f32[4,18,288]{2,1,0:T(8,128)S(1)}, u32[]{:S(2)}, u32[]{:S(2)}) collective-permute-start(f32[4,18,288]{2,1,0:T(8,128)S(1)} %get-tuple-element.41), channel_id=1, source_target_pairs={{0,4},{4,0},{8,12},{12,8},{1,5},{5,1},{9,13},{13,9},{2,6},{6,2},{1... | collective-permute-start | bytes 248840 | tf_op jit(solution)/shard_map/ppermute | solution.py:370
  232.8 3.6 %collective-permute-start.7 = (f32[4,18,288]{2,1,0:T(8,128)S(1)}, f32[4,18,288]{2,1,0:T(8,128)S(1)}, u32[]{:S(2)}, u32[]{:S(2)}) collective-permute-start(f32[4,18,288]{2,1,0:T(8,128)S(1)} %get-tuple-element.43), channel_id=1, source_target_pairs={{0,8},{4,12},{8,0},{12,4},{1,9},{5,13},{9,1},{13,5},{2,10},{6,14},... | collective-permute-start | bytes 248840 | tf_op jit(solution)/shard_map/ppermute | solution.py:370
  245.2 5.9 %collective-permute-done.13 = f32[4,18,288]{2,1,0:T(8,128)S(1)} collective-permute-done((f32[4,18,288]{2,1,0:T(8,128)S(1)}, f32[4,18,288]{2,1,0:T(8,128)S(1)}, u32[]{:S(2)}, u32[]{:S(2)}) %collective-permute-start.13) | collective-permute-done | bytes 82976 | tf_op jit(solution)/shard_map/ppermute | solution.py:370
  253.2 3.5 %collective-permute-start.15 = (f32[18,288]{1,0:T(8,128)S(1)}, f32[18,288]{1,0:T(8,128)S(1)}, u32[]{:S(2)}, u32[]{:S(2)}) collective-permute-start(f32[18,288]{1,0:T(8,128)S(1)} %get-tuple-element.53), channel_id=1, source_target_pairs={{0,2},{2,0},{16,18},{18,16},{32,34},{34,32},{48,50},{50,48},{1,3},... | collective-permute-start | bytes 62216 | tf_op jit(solution)/shard_map/ppermute | solution.py:370
  256.7 3.1 %collective-permute-start.17 = (f32[18,288]{1,0:T(8,128)S(1)}, f32[18,288]{1,0:T(8,128)S(1)}, u32[]{:S(2)}, u32[]{:S(2)}) collective-permute-start(f32[18,288]{1,0:T(8,128)S(1)} %get-tuple-element.51), channel_id=1, source_target_pairs={{0,18},{2,16},{16,2},{18,0},{32,50},{34,48},{48,34},{50,32},{1,19}... | collective-permute-start | bytes 62216 | tf_op jit(solution)/shard_map/ppermute | solution.py:370
  259.8 11.5 %collective-permute-start.18 = (f32[18,288]{1,0:T(8,128)S(1)}, f32[18,288]{1,0:T(8,128)S(1)}, u32[]{:S(2)}, u32[]{:S(2)}) collective-permute-start(f32[18,288]{1,0:T(8,128)S(1)} %get-tuple-element.50), channel_id=1, source_target_pairs={{0,32},{2,34},{16,48},{18,50},{32,0},{34,2},{48,16},{50,18},{1,33}... | collective-permute-start | bytes 62216 | tf_op jit(solution)/shard_map/ppermute | solution.py:370
  275.4 8.9 %all-to-all-done.1.slabs_ref = bf16[64,32,1152]{2,1,0:T(8,128)(2,1)} async-done(((bf16[64,32,1152]{2,1,0:T(8,128)(2,1)}), bf16[64,32,1152]{2,1,0:T(8,128)(2,1)}, u32[]{:S(2)}, u32[]{:S(2)}) %all-to-all-start.1) | async-done | bytes 4718624 | tf_op jit(solution)/shard_map/all_to_all | solution.py:426
  284.4 6.3 %unpack.1 = (bf16[1,2,256,1152]{3,2,1,0:T(8,128)(2,1)}, bf16[1,2,256,1152]{3,2,1,0:T(8,128)(2,1)}, bf16[1,2,256,1152]{3,2,1,0:T(8,128)(2,1)}, bf16[1,2,256,1152]{3,2,1,0:T(8,128)(2,1)}) custom-call(bf16[256,256]{1,0:T(8,128)(2,1)} %constant.90.clone.order_ref, bf16[64,32,1152]{2,1,0:T(8,128)(2,1)} %all-to-all-done.1.slabs_ref), custom_call_target="tpu_custom_call" | custom-call | flops 1207959552 | bytes 9437184 | tf_op jit(solution)/shard_map/unpack/pallas_call | solution.py:284
  (67 shorter events, 44.0 us)
Async XLA Ops:
  8.1 9.4 %collective-permute-start = (bf16[18,1152]{1,0:T(8,128)(2,1)S(1)}, bf16[18,1152]{1,0:T(8,128)(2,1)S(1)}, u32[]{:S(2)}, u32[]{:S(2)}) collective-permute-start(bf16[18,1152]{1,0:T(8,128)(2,1)S(1)} %constant_dynamic-slice_fusion), channel_id=1, source_target_pairs={{0,2},{2,0},{1,3},{3,1},{4,6},{6,4},{5,7},{7,5},{8,10},{10,8},{9,1... | collective-permute-start | bytes 124424 | tf_op jit(solution)/shard_map/ppermute | solution.py:370
  23.5 115.2 %all-to-all-start = ((bf16[64,32,1152]{2,1,0:T(8,128)(2,1)}), bf16[64,32,1152]{2,1,0:T(8,128)(2,1)}, u32[]{:S(2)}, u32[]{:S(2)}) async-start(bf16[64,32,1152]{2,1,0:T(8,128)(2,1)} %pack.1), calls=%async_computation | async-start | bytes 9437184 | tf_op jit(solution)/shard_map/all_to_all | solution.py:426
  34.6 84.5 %all-gather.3.cloned.1.call-start = ((), (), s32[]{:S(2)}) async-start(), calls=%async_computation.2 | async-start | bytes 1880064 | tf_op jit(solution)/shard_map/all_gather | solution.py:419
  121.6 3.7 %collective-permute-start.1 = (bf16[2,288,1152]{2,0,1:T(2,128)(2,1)S(1)}, bf16[2,288,1152]{2,0,1:T(2,128)(2,1)S(1)}, u32[]{:S(2)}, u32[]{:S(2)}) collective-permute-start(bf16[2,288,1152]{2,0,1:T(2,128)(2,1)S(1)} %bitcast.81), channel_id=1, source_target_pairs={{0,1},{1,0},{2,3},{3,2},{4,5},{5,4},{6,7},{7,6},{8,9},{9,8},{10,11... | collective-permute-start | bytes 3981320 | tf_op jit(solution)/shard_map/ppermute | solution.py:370
  162.8 121.6 %all-to-all-start.1 = ((bf16[64,32,1152]{2,1,0:T(8,128)(2,1)}), bf16[64,32,1152]{2,1,0:T(8,128)(2,1)}, u32[]{:S(2)}, u32[]{:S(2)}) async-start(bf16[64,32,1152]{2,1,0:T(8,128)(2,1)} %get-tuple-element.21), calls=%async_computation.1 | async-start | bytes 9437184 | tf_op jit(solution)/shard_map/all_to_all | solution.py:426
  192.9 17.7 %collective-permute-start.10 = (bf16[288,288]{1,0:T(8,128)(2,1)S(1)}, bf16[288,288]{1,0:T(8,128)(2,1)S(1)}, u32[]{:S(2)}, u32[]{:S(2)}) collective-permute-start(bf16[288,288]{1,0:T(8,128)(2,1)S(1)} %get-tuple-element.35), channel_id=1, source_target_pairs={{0,8},{4,12},{8,0},{12,4},{1,9},{5,13},{9,1},{13,5},{2,10},{6,14},... | collective-permute-start | bytes 497672 | tf_op jit(solution)/shard_map/ppermute | solution.py:370
  195.1 26.5 %collective-permute-start.11 = (bf16[288,288]{1,0:T(8,128)(2,1)S(1)}, bf16[288,288]{1,0:T(8,128)(2,1)S(1)}, u32[]{:S(2)}, u32[]{:S(2)}) collective-permute-start(bf16[288,288]{1,0:T(8,128)(2,1)S(1)} %get-tuple-element.36), channel_id=1, source_target_pairs={{0,12},{4,8},{8,4},{12,0},{1,13},{5,9},{9,5},{13,1},{2,14},{6,10},... | collective-permute-start | bytes 497672 | tf_op jit(solution)/shard_map/ppermute | solution.py:370
  195.1 26.5 %collective-permute-start.3 = (bf16[288,288]{1,0:T(8,128)(2,1)S(1)}, bf16[288,288]{1,0:T(8,128)(2,1)S(1)}, u32[]{:S(2)}, u32[]{:S(2)}) collective-permute-start(bf16[288,288]{1,0:T(8,128)(2,1)S(1)} %get-tuple-element.31), channel_id=1, source_target_pairs={{0,64},{64,0},{128,192},{192,128},{1,65},{65,1},{129,193},{193,129... | collective-permute-start | bytes 497672 | tf_op jit(solution)/shard_map/ppermute | solution.py:370
  196.6 30.7 %collective-permute-start.4 = (bf16[288,288]{1,0:T(8,128)(2,1)S(1)}, bf16[288,288]{1,0:T(8,128)(2,1)S(1)}, u32[]{:S(2)}, u32[]{:S(2)}) collective-permute-start(bf16[288,288]{1,0:T(8,128)(2,1)S(1)} %get-tuple-element.32), channel_id=1, source_target_pairs={{0,128},{64,192},{128,0},{192,64},{1,129},{65,193},{129,1},{193,65... | collective-permute-start | bytes 497672 | tf_op jit(solution)/shard_map/ppermute | solution.py:370
  199.5 28.1 %collective-permute-start.5 = (bf16[288,288]{1,0:T(8,128)(2,1)S(1)}, bf16[288,288]{1,0:T(8,128)(2,1)S(1)}, u32[]{:S(2)}, u32[]{:S(2)}) collective-permute-start(bf16[288,288]{1,0:T(8,128)(2,1)S(1)} %get-tuple-element.33), channel_id=1, source_target_pairs={{0,192},{64,128},{128,64},{192,0},{1,193},{65,129},{129,65},{193,1... | collective-permute-start | bytes 497672 | tf_op jit(solution)/shard_map/ppermute | solution.py:370
  210.6 17.0 %collective-permute-start.9 = (bf16[288,288]{1,0:T(8,128)(2,1)S(1)}, bf16[288,288]{1,0:T(8,128)(2,1)S(1)}, u32[]{:S(2)}, u32[]{:S(2)}) collective-permute-start(bf16[288,288]{1,0:T(8,128)(2,1)S(1)} %get-tuple-element.34), channel_id=1, source_target_pairs={{0,4},{4,0},{8,12},{12,8},{1,5},{5,1},{9,13},{13,9},{2,6},{6,2},{1... | collective-permute-start | bytes 497672 | tf_op jit(solution)/shard_map/ppermute | solution.py:370
  227.9 11.8 %collective-permute-start.6 = (f32[4,18,288]{2,1,0:T(8,128)S(1)}, f32[4,18,288]{2,1,0:T(8,128)S(1)}, u32[]{:S(2)}, u32[]{:S(2)}) collective-permute-start(f32[4,18,288]{2,1,0:T(8,128)S(1)} %get-tuple-element.41), channel_id=1, source_target_pairs={{0,4},{4,0},{8,12},{12,8},{1,5},{5,1},{9,13},{13,9},{2,6},{6,2},{1... | collective-permute-start | bytes 248840 | tf_op jit(solution)/shard_map/ppermute | solution.py:370
  232.8 10.8 %collective-permute-start.7 = (f32[4,18,288]{2,1,0:T(8,128)S(1)}, f32[4,18,288]{2,1,0:T(8,128)S(1)}, u32[]{:S(2)}, u32[]{:S(2)}) collective-permute-start(f32[4,18,288]{2,1,0:T(8,128)S(1)} %get-tuple-element.43), channel_id=1, source_target_pairs={{0,8},{4,12},{8,0},{12,4},{1,9},{5,13},{9,1},{13,5},{2,10},{6,14},... | collective-permute-start | bytes 248840 | tf_op jit(solution)/shard_map/ppermute | solution.py:370
  236.4 8.8 %collective-permute-start.8 = (f32[4,18,288]{2,1,0:T(8,128)S(1)}, f32[4,18,288]{2,1,0:T(8,128)S(1)}, u32[]{:S(2)}, u32[]{:S(2)}) collective-permute-start(f32[4,18,288]{2,1,0:T(8,128)S(1)} %get-tuple-element.42), channel_id=1, source_target_pairs={{0,12},{4,8},{8,4},{12,0},{1,13},{5,9},{9,5},{13,1},{2,14},{6,10},... | collective-permute-start | bytes 248840 | tf_op jit(solution)/shard_map/ppermute | solution.py:370
  236.9 8.2 %collective-permute-start.12 = (f32[4,18,288]{2,1,0:T(8,128)S(1)}, f32[4,18,288]{2,1,0:T(8,128)S(1)}, u32[]{:S(2)}, u32[]{:S(2)}) collective-permute-start(f32[4,18,288]{2,1,0:T(8,128)S(1)} %get-tuple-element.44), channel_id=1, source_target_pairs={{0,64},{64,0},{128,192},{192,128},{1,65},{65,1},{129,193},{193,129... | collective-permute-start | bytes 248840 | tf_op jit(solution)/shard_map/ppermute | solution.py:370
  237.3 13.8 %collective-permute-start.13 = (f32[4,18,288]{2,1,0:T(8,128)S(1)}, f32[4,18,288]{2,1,0:T(8,128)S(1)}, u32[]{:S(2)}, u32[]{:S(2)}) collective-permute-start(f32[4,18,288]{2,1,0:T(8,128)S(1)} %get-tuple-element.46), channel_id=1, source_target_pairs={{0,128},{64,192},{128,0},{192,64},{1,129},{65,193},{129,1},{193,65... | collective-permute-start | bytes 248840 | tf_op jit(solution)/shard_map/ppermute | solution.py:370
  239.7 13.4 %collective-permute-start.14 = (f32[4,18,288]{2,1,0:T(8,128)S(1)}, f32[4,18,288]{2,1,0:T(8,128)S(1)}, u32[]{:S(2)}, u32[]{:S(2)}) collective-permute-start(f32[4,18,288]{2,1,0:T(8,128)S(1)} %get-tuple-element.45), channel_id=1, source_target_pairs={{0,192},{64,128},{128,64},{192,0},{1,193},{65,129},{129,65},{193,1... | collective-permute-start | bytes 248840 | tf_op jit(solution)/shard_map/ppermute | solution.py:370
  253.2 19.1 %collective-permute-start.15 = (f32[18,288]{1,0:T(8,128)S(1)}, f32[18,288]{1,0:T(8,128)S(1)}, u32[]{:S(2)}, u32[]{:S(2)}) collective-permute-start(f32[18,288]{1,0:T(8,128)S(1)} %get-tuple-element.53), channel_id=1, source_target_pairs={{0,2},{2,0},{16,18},{18,16},{32,34},{34,32},{48,50},{50,48},{1,3},... | collective-permute-start | bytes 62216 | tf_op jit(solution)/shard_map/ppermute | solution.py:370
  256.7 17.9 %collective-permute-start.16 = (f32[18,288]{1,0:T(8,128)S(1)}, f32[18,288]{1,0:T(8,128)S(1)}, u32[]{:S(2)}, u32[]{:S(2)}) collective-permute-start(f32[18,288]{1,0:T(8,128)S(1)} %get-tuple-element.52), channel_id=1, source_target_pairs={{0,16},{2,18},{16,0},{18,2},{32,48},{34,50},{48,32},{50,34},{1,17}... | collective-permute-start | bytes 62216 | tf_op jit(solution)/shard_map/ppermute | solution.py:370
  256.7 33.9 %collective-permute-start.17 = (f32[18,288]{1,0:T(8,128)S(1)}, f32[18,288]{1,0:T(8,128)S(1)}, u32[]{:S(2)}, u32[]{:S(2)}) collective-permute-start(f32[18,288]{1,0:T(8,128)S(1)} %get-tuple-element.51), channel_id=1, source_target_pairs={{0,18},{2,16},{16,2},{18,0},{32,50},{34,48},{48,34},{50,32},{1,19}... | collective-permute-start | bytes 62216 | tf_op jit(solution)/shard_map/ppermute | solution.py:370
  259.8 30.9 %collective-permute-start.18 = (f32[18,288]{1,0:T(8,128)S(1)}, f32[18,288]{1,0:T(8,128)S(1)}, u32[]{:S(2)}, u32[]{:S(2)}) collective-permute-start(f32[18,288]{1,0:T(8,128)S(1)} %get-tuple-element.50), channel_id=1, source_target_pairs={{0,32},{2,34},{16,48},{18,50},{32,0},{34,2},{48,16},{50,18},{1,33}... | collective-permute-start | bytes 62216 | tf_op jit(solution)/shard_map/ppermute | solution.py:370
  271.3 19.4 %collective-permute-start.19 = (f32[18,288]{1,0:T(8,128)S(1)}, f32[18,288]{1,0:T(8,128)S(1)}, u32[]{:S(2)}, u32[]{:S(2)}) collective-permute-start(f32[18,288]{1,0:T(8,128)S(1)} %get-tuple-element.49), channel_id=1, source_target_pairs={{0,34},{2,32},{16,50},{18,48},{32,2},{34,0},{48,18},{50,16},{1,35}... | collective-permute-start | bytes 62216 | tf_op jit(solution)/shard_map/ppermute | solution.py:370
  272.3 18.4 %collective-permute-start.20 = (f32[18,288]{1,0:T(8,128)S(1)}, f32[18,288]{1,0:T(8,128)S(1)}, u32[]{:S(2)}, u32[]{:S(2)}) collective-permute-start(f32[18,288]{1,0:T(8,128)S(1)} %get-tuple-element.48), channel_id=1, source_target_pairs={{0,48},{2,50},{16,32},{18,34},{32,16},{34,18},{48,0},{50,2},{1,49}... | collective-permute-start | bytes 62216 | tf_op jit(solution)/shard_map/ppermute | solution.py:370
  274.7 16.0 %collective-permute-start.21 = (f32[18,288]{1,0:T(8,128)S(1)}, f32[18,288]{1,0:T(8,128)S(1)}, u32[]{:S(2)}, u32[]{:S(2)}) collective-permute-start(f32[18,288]{1,0:T(8,128)S(1)} %get-tuple-element.47), channel_id=1, source_target_pairs={{0,50},{2,48},{16,34},{18,32},{32,18},{34,16},{48,2},{50,0},{1,51}... | collective-permute-start | bytes 62216 | tf_op jit(solution)/shard_map/ppermute | solution.py:370
  (9 other events, 35.0 us)
Sparse Core Ops, SparseCore 0:
  38.5 80.5 all-gather.2

commit v4 on v3

--- a/solution.py
+++ b/solution.py
@@ -67,71 +67,68 @@
     return [pl.BlockSpec(memory_space=pltpu.VMEM)] * count
 
 
-def pack_kernel(order_ref, q_ref, k_ref, v_ref, c_ref, token, out_ref, rows_ref, slabs_ref, in_sem, out_sem):
+def pack_kernel(part, order_ref, q_ref, k_ref, v_ref, c_ref, *refs):
+    out_ref, rows_ref, slabs_ref, in_sem, out_sem = refs[-5:]
     arrays = (q_ref, k_ref, v_ref, c_ref)
     coming, going = [], []
-    for part in range(2):
-        for a in range(4):
-            coming.append(
-                pltpu.make_async_copy(
-                    arrays[a].at[0, :, pl.ds(part * 128, 128), :],
-                    rows_ref.at[part, a],
-                    in_sem.at[part, a],
-                )
+    for a in range(4):
+        coming.append(
+            pltpu.make_async_copy(
+                arrays[a].at[0, :, pl.ds(part * 128, 128), :], rows_ref.at[a], in_sem.at[a]
             )
-            coming[-1].start()
-    for part in range(2):
-        for a in range(4):
-            coming[4 * part + a].wait()
-        for g in range(4):
-            rows = [rows_ref[part, a, f, pl.ds(g * 32, 32), :] for a in range(4) for f in range(2)]
-            slabs_ref[part, g] = move(order_ref[...], jnp.concatenate(rows, axis=0)).reshape(16, 16, D)
-            going.append(
-                pltpu.make_async_copy(
-                    slabs_ref.at[part, g],
-                    out_ref.at[pl.ds(g * 16, 16), pl.ds(part * 16, 16), :],
-                    out_sem.at[part, g],
-                )
-            )
-            going[-1].start()
+        )
+        coming[-1].start()
+    for copy in coming:
+        copy.wait()
+    for g in range(4):
+        rows = [rows_ref[a, f, pl.ds(g * 32, 32), :] for a in range(4) for f in range(2)]
+        slabs_ref[g] = move(order_ref[...], jnp.concatenate(rows, axis=0)).reshape(16, 16, D)
+        going.append(
+            pltpu.make_async_copy(slabs_ref.at[g], out_ref.at[pl.ds(g * 16, 16)], out_sem.at[g])
+        )
+        going[-1].start()
     for copy in going:
         copy.wait()
 
 
-def pack(arrays, token):
-    return pl.pallas_call(
-        pack_kernel,
-        in_specs=in_vmem(1) + in_hbm(4) + [pl.BlockSpec(memory_space=pl.ANY)],
+def pack(part, arrays, tokens):
+    return pl.pallas_call(
+        functools.partial(pack_kernel, part),
+        in_specs=in_vmem(1) + in_hbm(4) + [pl.BlockSpec(memory_space=pl.ANY)] * len(tokens),
         out_specs=pl.BlockSpec(memory_space=pltpu.HBM),
-        out_shape=jax.ShapeDtypeStruct((64, 32, D), BF16),
+        out_shape=jax.ShapeDtypeStruct((64, 16, D), BF16),
         scratch_shapes=[
-            pltpu.VMEM((2, 4, 2, 128, D), BF16),
-            pltpu.VMEM((2, 4, 16, 16, D), BF16),
-            pltpu.SemaphoreType.DMA((2, 4)),
-            pltpu.SemaphoreType.DMA((2, 4)),
+            pltpu.VMEM((4, 2, 128, D), BF16),
+            pltpu.VMEM((4, 16, 16, D), BF16),
+            pltpu.SemaphoreType.DMA((4,)),
+            pltpu.SemaphoreType.DMA((4,)),
         ],
         compiler_params=params(60),
         cost_estimate=pl.CostEstimate(
-            flops=2 * 2048 * 256 * D, bytes_accessed=8192 * D, transcendentals=0
+            flops=2 * 1024 * 256 * D, bytes_accessed=4096 * D, transcendentals=0
         ),
         name="pack",
-    )(const(order_to_slabs(2)), *arrays, token)
-
-
-def attend_part(part, order_ref, back_ref, r_ref, w_ref, s_ref, att_ref, cot_ref, *refs):
-    in_ref, x_ref, u_ref, y_ref, out_ref, kept_ref, in_sem, out_sem, kept_sem = refs
-    slots = pl.ds(pl.multiple_of(part * 16, 16), 16)
-    mine = pl.ds(pl.multiple_of(part * 256, 256), 256)
+    )(const(order_to_slabs(2)), *arrays, *tokens)
+
+
+def attend_kernel(
+    order_ref, back_ref, r_ref, w_ref, s_ref, att_ref, cot_ref,
+    in_ref, x_ref, u_ref, y_ref, out_ref, kept_ref, in_sem, out_sem, kept_sem,
+):
+    coming = [
+        pltpu.make_async_copy(r_ref.at[pl.ds(b * 16, 16)], in_ref.at[b], in_sem.at[b]) for b in range(4)
+    ]
+    for copy in coming:
+        copy.start()
     for b in range(4):
-        n = part * 4 + b
-        pltpu.make_async_copy(r_ref.at[pl.ds(b * 16, 16), slots, :], in_ref.at[n], in_sem.at[n]).wait()
-        t = move(order_ref[...], in_ref[n].reshape(256, D))
+        coming[b].wait()
+        t = move(order_ref[...], in_ref[b].reshape(256, D))
         for a in range(4):
             for p in range(2):
                 x_ref[a, pl.ds(p * 128 + b * 32, 32), :] = t[(a * 2 + p) * 32 : (a * 2 + p + 1) * 32]
     cot = x_ref[3]
-    kept_ref[part, 1] = cot
-    pltpu.make_async_copy(kept_ref.at[part, 1], cot_ref.at[mine, :], kept_sem.at[part, 1]).start()
+    going = [pltpu.make_async_copy(x_ref.at[3], cot_ref, kept_sem.at[0])]
+    going[-1].start()
     u_ref[...] = lax.dot_general(
         cot, w_ref[...], (((1,), (1,)), ((), ())), preferred_element_type=F32
     ).astype(BF16)
@@ -179,41 +176,19 @@
                 beside(low), both(u), preferred_element_type=F32
             ).astype(BF16)
     att = y_ref[0]
-    kept_ref[part, 0] = att
-    pltpu.make_async_copy(kept_ref.at[part, 0], att_ref.at[mine, :], kept_sem.at[part, 0]).start()
+    kept_ref[...] = att
+    going.append(pltpu.make_async_copy(kept_ref, att_ref, kept_sem.at[1]))
+    going[-1].start()
     y_ref[0] = jnp.dot(att, w_ref[...], preferred_element_type=F32).astype(BF16)
     for b in range(4):
-        n = part * 4 + b
         t = jnp.concatenate(
             [y_ref[a, pl.ds(p * 128 + b * 32, 32), :] for a in range(4) for p in range(2)], axis=0
         )
-        out_ref[n] = move(back_ref[...], t).reshape(16, 16, D)
-        pltpu.make_async_copy(out_ref.at[n], s_ref.at[pl.ds(b * 16, 16), slots, :], out_sem.at[n]).start()
-
-
-def attend_kernel(*refs):
-    r_ref, s_ref, att_ref, cot_ref = refs[2], refs[4], refs[5], refs[6]
-    in_ref, out_ref, kept_ref, in_sem, out_sem, kept_sem = refs[7], *refs[11:]
-    for n in range(8):
-        part, b = divmod(n, 4)
-        pltpu.make_async_copy(
-            r_ref.at[pl.ds(b * 16, 16), pl.ds(part * 16, 16), :], in_ref.at[n], in_sem.at[n]
-        ).start()
-
-    @pl.loop(0, 2)
-    def _(part):
-        attend_part(part, *refs)
-
-    for part in range(2):
-        for i, ref in enumerate((att_ref, cot_ref)):
-            pltpu.make_async_copy(
-                kept_ref.at[part, i], ref.at[pl.ds(part * 256, 256), :], kept_sem.at[part, i]
-            ).wait()
-        for b in range(4):
-            n = part * 4 + b
-            pltpu.make_async_copy(
-                out_ref.at[n], s_ref.at[pl.ds(b * 16, 16), pl.ds(part * 16, 16), :], out_sem.at[n]
-            ).wait()
+        out_ref[b] = move(back_ref[...], t).reshape(16, 16, D)
+        going.append(pltpu.make_async_copy(out_ref.at[b], s_ref.at[pl.ds(b * 16, 16)], out_sem.at[b]))
+        going[-1].start()
+    for copy in going:
+        copy.wait()
 
 
 def attend(received, weight):
@@ -223,86 +198,81 @@
         in_specs=in_vmem(2) + in_hbm(1) + in_vmem(1),
         out_specs=in_hbm(3),
         out_shape=[
-            jax.ShapeDtypeStruct((64, 32, D), BF16),
-            jax.ShapeDtypeStruct((512, D), BF16),
-            jax.ShapeDtypeStruct((512, D), BF16),
+            jax.ShapeDtypeStruct((64, 16, D), BF16),
+            jax.ShapeDtypeStruct((256, D), BF16),
+            jax.ShapeDtypeStruct((256, D), BF16),
         ],
         scratch_shapes=[
-            pltpu.VMEM((8, 16, 16, D), BF16),
+            pltpu.VMEM((4, 16, 16, D), BF16),
             pltpu.VMEM((4, 256, D), BF16),
             pltpu.VMEM((256, D), BF16),
             pltpu.VMEM((4, 256, D), BF16),
-            pltpu.VMEM((8, 16, 16, D), BF16),
-            pltpu.VMEM((2, 2, 256, D), BF16),
-            pltpu.SemaphoreType.DMA((8,)),
-            pltpu.SemaphoreType.DMA((8,)),
-            pltpu.SemaphoreType.DMA((2, 2)),
+            pltpu.VMEM((4, 16, 16, D), BF16),
+            pltpu.VMEM((256, D), BF16),
+            pltpu.SemaphoreType.DMA((4,)),
+            pltpu.SemaphoreType.DMA((4,)),
+            pltpu.SemaphoreType.DMA((2,)),
         ],
         compiler_params=params(58),
         cost_estimate=pl.CostEstimate(
-            flops=12_000_000_000, bytes_accessed=40 * 256 * D + 2 * D * D, transcendentals=1048576
+            flops=6_000_000_000, bytes_accessed=20 * 256 * D + 2 * D * D, transcendentals=524288
         ),
         name="attend",
     )(const(order), const(order.T.copy()), received, weight)
 
 
-def unpack_kernel(order_ref, slabs_ref, *refs):
-    outs = refs[:4]
-    in_ref, rows_ref, in_sem, out_sem = refs[4:]
+def unpack_kernel(part, order_ref, slabs_ref, *refs):
+    outs = refs[-8:-4]
+    in_ref, rows_ref, in_sem, out_sem = refs[-4:]
     coming, going = [], []
-    for n in range(8):
-        part, g = divmod(n, 4)
+    for g in range(4):
         coming.append(
-            pltpu.make_async_copy(
-                slabs_ref.at[pl.ds(g * 16, 16), pl.ds(part * 16, 16), :], in_ref.at[n], in_sem.at[n]
-            )
+            pltpu.make_async_copy(slabs_ref.at[pl.ds(g * 16, 16)], in_ref.at[g], in_sem.at[g])
         )
         coming[-1].start()
-    for n in range(8):
-        part, g = divmod(n, 4)
-        coming[n].wait()
-        t = move(order_ref[...], in_ref[n].reshape(256, D))
+    for g in range(4):
+        coming[g].wait()
+        t = move(order_ref[...], in_ref[g].reshape(256, D))
         for a in range(4):
             for f in range(2):
                 at = (a * 2 + f) * 32
-                rows_ref[part, a, f, pl.ds(g * 32, 32), :] = t[at : at + 32]
-            if g % 2 == 1:
-                begin = (g - 1) * 32
-                going.append(
-                    pltpu.make_async_copy(
-                        rows_ref.at[part, a, :, pl.ds(begin, 64), :],
-                        outs[a].at[0, :, pl.ds(part * 128 + begin, 64), :],
-                        out_sem.at[n, a],
-                    )
+                rows_ref[g, a, f] = t[at : at + 32]
+            going.append(
+                pltpu.make_async_copy(
+                    rows_ref.at[g, a],
+                    outs[a].at[0, :, pl.ds(part * 128 + g * 32, 32), :],
+                    out_sem.at[g, a],
                 )
-                going[-1].start()
+            )
+            going[-1].start()
     for copy in going:
         copy.wait()
 
 
-def unpack(slabs):
-    return pl.pallas_call(
-        unpack_kernel,
-        in_specs=in_vmem(1) + in_hbm(1),
+def unpack(part, slabs, before):
+    return pl.pallas_call(
+        functools.partial(unpack_kernel, part),
+        in_specs=in_vmem(1) + in_hbm(1 + len(before)),
         out_specs=in_hbm(4),
         out_shape=[jax.ShapeDtypeStruct((1, 2, 256, D), BF16)] * 4,
         scratch_shapes=[
-            pltpu.VMEM((8, 16, 16, D), BF16),
-            pltpu.VMEM((2, 4, 2, 128, D), BF16),
-            pltpu.SemaphoreType.DMA((8,)),
-            pltpu.SemaphoreType.DMA((8, 4)),
+            pltpu.VMEM((4, 16, 16, D), BF16),
+            pltpu.VMEM((4, 4, 2, 32, D), BF16),
+            pltpu.SemaphoreType.DMA((4,)),
+            pltpu.SemaphoreType.DMA((4, 4)),
         ],
+        input_output_aliases={2 + a: a for a in range(len(before))},
         compiler_params=params(60),
         cost_estimate=pl.CostEstimate(
-            flops=2 * 2048 * 256 * D, bytes_accessed=8192 * D, transcendentals=0
+            flops=2 * 1024 * 256 * D, bytes_accessed=4096 * D, transcendentals=0
         ),
         name="unpack",
-    )(const(order_to_slabs(2).T.copy()), slabs)
-
-
-def outer_kernel(turn_ref, att_ref, cot_ref, mine_ref, theirs_ref):
-    att = att_ref[...]
-    cot = cot_ref[...]
+    )(const(order_to_slabs(2).T.copy()), slabs, *before)
+
+
+def outer_kernel(turn_ref, att0_ref, att1_ref, cot0_ref, cot1_ref, mine_ref, theirs_ref):
+    att = jnp.concatenate([att0_ref[...], att1_ref[...]], axis=0)
+    cot = jnp.concatenate([cot0_ref[...], cot1_ref[...]], axis=0)
     turned = move(cot, turn_ref[...])
     parts = [att[:, 288 * b : 288 * b + 288] for b in range(4)]
     core = lax.axis_index("c")
@@ -324,10 +294,10 @@
     return const(out)
 
 
-def outer(att, cot):
+def outer(atts, cots):
     return pl.pallas_call(
         outer_kernel,
-        in_specs=in_vmem(3),
+        in_specs=in_vmem(5),
         out_specs=in_vmem(2),
         out_shape=[jax.ShapeDtypeStruct((D, 576), F32), jax.ShapeDtypeStruct((D, 576), BF16)],
         compiler_params=params(24),
@@ -335,7 +305,7 @@
             flops=2 * 512 * D * D, bytes_accessed=4 * 512 * D + 6 * D * 576, transcendentals=0
         ),
         name="outer",
-    )(turn(), att, cot)
+    )(turn(), *atts, *cots)
 
 
 def halves_kernel(mine_ref, other_ref, own_ref, *out_refs):
@@ -379,16 +349,17 @@
     ]
 
 
-def weight_terms(att, cot):
-    mine, theirs = outer(att, cot)
+def weight_terms(atts, cots):
+    mine, theirs = outer(atts, cots)
     own, *sent = halves(mine, swap(theirs, "c", 1))
     here, there = own[0], own[1]
     for k in range(1, 4):
         here = here + swap(sent[k - 1], "y", k).astype(F32)
         there = there + swap(sent[k + 2], "x", k).astype(F32)
+    first = [here, there]
     here = sum(terms_over(here.reshape(4, 4, 18, 288).transpose(1, 0, 2, 3), "x"))
     there = sum(terms_over(there.reshape(4, 4, 18, 288), "y"))
-    return terms_over(jnp.stack([here, there], axis=1).reshape(8, 18, 288), ("zl", "zh"))
+    return first, terms_over(jnp.stack([here, there], axis=1).reshape(8, 18, 288), ("zl", "zh"))
 
 
 def add_up_kernel(*refs):
@@ -422,6 +393,21 @@
     return both.transpose(1, 0, 2, 3).reshape(D, D)
 
 
+def hold_kernel(*refs):
+    pass
+
+
+def hold(value, tokens):
+    return pl.pallas_call(
+        hold_kernel,
+        in_specs=[pl.BlockSpec(memory_space=pl.ANY)] * (1 + len(tokens)),
+        out_specs=pl.BlockSpec(memory_space=pl.ANY),
+        out_shape=jax.ShapeDtypeStruct(value.shape, value.dtype),
+        input_output_aliases={0: 0},
+        name="hold",
+    )(value, *tokens)
+
+
 def exchange(t):
     return lax.all_to_all(t, SEQ, split_axis=0, concat_axis=0, tiled=True)
 
@@ -431,10 +417,12 @@
     place = lax.axis_index("y") * 4 + lax.axis_index("x")
     piece = lax.dynamic_slice_in_dim(out_weight, place * 18, 18, 0)
     other = swap(piece, "zh", 1)
-    received = exchange(pack(arrays, other))
-    sent, att, cot = attend(received, whole_weight(piece, other))
-    terms = weight_terms(att, cot)
-    outs = unpack(exchange(sent))
+    received = [exchange(hold(pack(0, arrays, []), [other])), exchange(pack(1, arrays, []))]
+    weight = whole_weight(piece, other)
+    sent, atts, cots = zip(*[attend(t, weight) for t in received])
+    begun, terms = weight_terms(atts, cots)
+    outs = unpack(0, exchange(sent[0]), ())
+    outs = unpack(1, exchange(hold(sent[1], begun)), outs)
     return (*outs, add_up(terms, outs[0]).T)
 
 

time: 304 us -> 303 us (level)
  waiting for transfers between devices: 136 us -> 118 us
  Pallas kernels: 41.6 us -> 52 us
  local copies, waits for them, and re-layouts: 16.8 us -> 22.5 us
  starting transfers between devices: 83.1 us -> 79.8 us
    all_gather x1, waiting for transfers between devices: 82.8 us -> 0.02 us  [whole_weight(): rows = lax.all_gather(pair, ('y', 'x'), axis=0, tiled=False)]
    all_to_all x2 -> x4, waiting for transfers between devices: 14.4 us -> 81.5 us  [exchange(): return lax.all_to_all(t, SEQ, split_axis=0, concat_axis=0, tiled=True)]
    ppermute x22, starting transfers between devices: 59.7 us -> 46.5 us  [swap(): return lax.ppermute(value, axis, [(i, i ^ k) for i in range(SIZES[axis])])]
    all_to_all x2 -> x4, starting transfers between devices: 23.3 us -> 33.3 us  [exchange(): return lax.all_to_all(t, SEQ, split_axis=0, concat_axis=0, tiled=True)]
    pallas_call x3 -> x7, Pallas kernels: 16.1 us -> 22.2 us  [the longest x2 8.8 us: unpack(): pl.pallas_call(functools.partial(unpack_kernel, part), in_specs=in_vmem(1...]
    pallas_call x1 -> x2, Pallas kernels: 24.1 us -> 28.4 us  [attend(): pl.pallas_call(attend_kernel, in_specs=in_vmem(2) + in_hbm(1) + in_vmem(1...]
    unnamed x16 -> x28, local copies, waits for them, and re-layouts: 8.36 us -> 10.4 us
  transfers between devices with their start and end apart: 25 -> 27, of which waited for: 14 -> 14; matrix products, arithmetic and copies ran while one was open for 5% -> 7% of each run, Pallas kernels for 4% -> 17%
where the time goes in v4:
time: 303 us; the launch traced here: 298 us
  waiting for transfers between devices  118 us (39%)
  starting transfers between devices  79.8 us (26%)
  Pallas kernels  52 us (17%)
  local copies, waits for them, and re-layouts  22.5 us (7%)
  between operations  14.7 us (5%)
  other arithmetic  10.8 us (4%)
    all_to_all x4, waiting for transfers between devices, exchange(): return lax.all_to_all(t, SEQ, split_axis=0, concat_axis=0, tiled=True)  81.5 us
    ppermute x22, starting transfers between devices, swap(): return lax.ppermute(value, axis, [(i, i ^ k) for i in range(SIZES[axis])])  46.5 us
    ppermute x22, waiting for transfers between devices, swap(): return lax.ppermute(value, axis, [(i, i ^ k) for i in range(SIZES[axis])])  36.1 us
    all_to_all x4, starting transfers between devices, exchange(): return lax.all_to_all(t, SEQ, split_axis=0, concat_axis=0, tiled=True)  33.3 us
    pallas_call x2, Pallas kernels, attend(): pl.pallas_call(attend_kernel, in_specs=in_vmem(2) + in_hbm(1) + in_vmem(1...  28.4 us
    unnamed x28, local copies, waits for them, and re-layouts  10.4 us
    pallas_call x2, Pallas kernels, unpack(): pl.pallas_call(functools.partial(unpack_kernel, part), in_specs=in_vmem(1...  8.8 us
    pallas_call x2, Pallas kernels, pack(): pl.pallas_call(functools.partial(pack_kernel, part), in_specs=in_vmem(1)...  8.76 us
  transfers between devices with their start and end apart: 27, of which 14 were waited for; matrix products, arithmetic and copies ran while one was open for 7% of the time, Pallas kernels for 17%

profile of v4, /device:TPU:2, one launch (start us, length us, event | category | flops | bytes accessed | tf_op | source)
XLA Modules:
  0.0 297.5 jit_solution(17048519111389333633)
XLA Ops:
  8.1 7.3 %collective-permute-start = (bf16[18,1152]{1,0:T(8,128)(2,1)S(1)}, bf16[18,1152]{1,0:T(8,128)(2,1)S(1)}, u32[]{:S(2)}, u32[]{:S(2)}) collective-permute-start(bf16[18,1152]{1,0:T(8,128)(2,1)S(1)} %constant_dynamic-slice_fusion), channel_id=1, source_target_pairs={{0,2},{2,0},{1,3},{3,1},{4,6},{6,4},{5,7},{7,5},{8,10},{10,8},{9,1... | collective-permute-start | bytes 124424 | tf_op jit(solution)/shard_map/ppermute | solution.py:340
  15.4 4.3 %pack.3.refs_0_ = bf16[64,16,1152]{2,1,0:T(8,128)(2,1)} custom-call(bf16[256,256]{1,0:T(8,128)(2,1)} %constant.86.clone.order_ref, bf16[1,2,256,1152]{3,2,1,0:T(8,128)(2,1)} %q_ref.3, bf16[1,2,256,1152]{3,2,1,0:T(8,128)(2,1)} %k_ref.3, bf16[1,2,256,1152]{3,2,1,0:T(8,128)(2,1)} %v_ref.3, bf16[1,2,256,1152]{3,2,1,0:T(8,128)(2,1)} %c_ref.3), custom_call_target="tpu_custom_call" | custom-call | flops 603979776 | bytes 4718592 | tf_op jit(solution)/shard_map/pack/pallas_call | solution.py:95
  20.3 9.5 %all-to-all-start.1 = ((bf16[64,16,1152]{2,1,0:T(8,128)(2,1)}), bf16[64,16,1152]{2,1,0:T(8,128)(2,1)S(1)}, u32[]{:S(2)}, u32[]{:S(2)}) async-start(bf16[64,16,1152]{2,1,0:T(8,128)(2,1)} %hold.2), calls=%async_computation.1 | async-start | bytes 4718592 | tf_op jit(solution)/shard_map/all_to_all | solution.py:412
  31.6 4.4 %pack.2 = bf16[64,16,1152]{2,1,0:T(8,128)(2,1)} custom-call(bf16[256,256]{1,0:T(8,128)(2,1)} %constant.86.clone.order_ref, bf16[1,2,256,1152]{3,2,1,0:T(8,128)(2,1)} %q_ref.3, bf16[1,2,256,1152]{3,2,1,0:T(8,128)(2,1)} %k_ref.3, bf16[1,2,256,1152]{3,2,1,0:T(8,128)(2,1)} %v_ref.3, bf16[1,2,256,1152]{3,2,1,0:T(8,128)(2,1)} %c_ref.3), custom_call_target="tpu_custom_call" | custom-call | flops 603979776 | bytes 4718592 | tf_op jit(solution)/shard_map/pack/pallas_call | solution.py:95
  36.0 49.6 %all-to-all-done.1.r_ref = bf16[64,16,1152]{2,1,0:T(8,128)(2,1)S(1)} async-done(((bf16[64,16,1152]{2,1,0:T(8,128)(2,1)}), bf16[64,16,1152]{2,1,0:T(8,128)(2,1)S(1)}, u32[]{:S(2)}, u32[]{:S(2)}) %all-to-all-start.1) | async-done | bytes 2359328 | tf_op jit(solution)/shard_map/all_to_all | solution.py:412
  87.0 6.7 %all-to-all-start = ((bf16[64,16,1152]{2,1,0:T(8,128)(2,1)}), bf16[64,16,1152]{2,1,0:T(8,128)(2,1)}, u32[]{:S(2)}, u32[]{:S(2)}) async-start(bf16[64,16,1152]{2,1,0:T(8,128)(2,1)} %pack.2), calls=%async_computation | async-start | bytes 4718592 | tf_op jit(solution)/shard_map/all_to_all | solution.py:412
  96.6 3.0 %collective-permute-done.1 = bf16[2,288,1152]{2,0,1:T(2,128)(2,1)S(1)} collective-permute-done((bf16[2,288,1152]{2,0,1:T(2,128)(2,1)S(1)}, bf16[2,288,1152]{2,0,1:T(2,128)(2,1)S(1)}, u32[]{:S(2)}, u32[]{:S(2)}) %collective-permute-start.1) | collective-permute-done | bytes 1327136 | tf_op jit(solution)/shard_map/ppermute | solution.py:340
  102.0 3.8 %maximum_bitcast_fusion = bf16[2,2,288,1152]{3,0,2,1:T(2,128)(2,1)S(1)} fusion(bf16[1,2,288,1152]{3,1,2,0:T(2,128)(2,1)S(1)} %get-tuple-element.52, bf16[1,2,288,1152]{3,1,2,0:T(2,128)(2,1)S(1)} %get-tuple-element.51), kind=kLoop, calls=%fused_computation | loop fusion | flops 1327104 | bytes 5308416 | tf_op jit(solution)/shard_map/transpose | solution.py:393
  107.6 14.4 %attend.3 = (bf16[64,16,1152]{2,1,0:T(8,128)(2,1)}, bf16[256,1152]{1,0:T(8,128)(2,1)}, bf16[256,1152]{1,0:T(8,128)(2,1)}) custom-call(bf16[256,256]{1,0:T(8,128)(2,1)} %constant.87.clone.order_ref, bf16[256,256]{1,0:T(8,128)(2,1)} %constant.88.clone.back_ref, bf16[64,16,1152]{2,1,0:T(8,128)(2,1)} %copy-done.11, bf16[1152,1152]{1,0:T(8,128)(2,1)} %bitcast.82), custom_call_target="tpu_custom_call" | custom-call | flops 6000000000 | bytes 8552448 | tf_op jit(solution)/shard_map/attend/pallas_call | solution.py:196
  122.0 27.1 %all-to-all-done.r_ref = bf16[64,16,1152]{2,1,0:T(8,128)(2,1)} async-done(((bf16[64,16,1152]{2,1,0:T(8,128)(2,1)}), bf16[64,16,1152]{2,1,0:T(8,128)(2,1)}, u32[]{:S(2)}, u32[]{:S(2)}) %all-to-all-start) | async-done | bytes 2359328 | tf_op jit(solution)/shard_map/all_to_all | solution.py:412
  149.1 6.5 %all-to-all-start.3 = ((bf16[64,16,1152]{2,1,0:T(8,128)(2,1)}), bf16[64,16,1152]{2,1,0:T(8,128)(2,1)}, u32[]{:S(2)}, u32[]{:S(2)}) async-start(bf16[64,16,1152]{2,1,0:T(8,128)(2,1)} %get-tuple-element.42), calls=%async_computation.3 | async-start | bytes 4718592 | tf_op jit(solution)/shard_map/all_to_all | solution.py:412
  155.6 14.1 %attend.2 = (bf16[64,16,1152]{2,1,0:T(8,128)(2,1)}, bf16[256,1152]{1,0:T(8,128)(2,1)}, bf16[256,1152]{1,0:T(8,128)(2,1)}) custom-call(bf16[256,256]{1,0:T(8,128)(2,1)} %constant.87.clone.order_ref, bf16[256,256]{1,0:T(8,128)(2,1)} %constant.88.clone.back_ref, bf16[64,16,1152]{2,1,0:T(8,128)(2,1)} %all-to-all-done.r_ref, bf16[1152,1152]{1,0:T(8,128)(2,1)} %bitcast.83), custom_call_target="tpu_custom_call" | custom-call | flops 6000000000 | bytes 8552448 | tf_op jit(solution)/shard_map/attend/pallas_call | solution.py:196
  171.9 4.7 %outer.1 = (f32[1152,576]{1,0:T(8,128)S(1)}, bf16[1152,576]{1,0:T(8,128)(2,1)S(1)}) custom-call(bf16[1152,1152]{1,0:T(8,128)(2,1)S(1)} %copy-done.3, bf16[256,1152]{1,0:T(8,128)(2,1)S(1)} %copy-done.4, bf16[256,1152]{1,0:T(8,128)(2,1)S(1)} %copy-done.6, bf16[256,1152]{1,0:T(8,128)(2,1)S(1)} %copy-done.5, bf16[256,1152]{1,0:T(8,128)(2,1)S(1)} %copy-done.7), custom_call_target="tpu_custom_call" | custom-call | flops 1358954496 | bytes 6340608 | tf_op jit(solution)/shard_map/outer/pallas_call | solution.py:298
  180.1 3.3 %collective-permute-done.2 = bf16[1152,576]{0,1:T(8,128)(2,1)S(1)} collective-permute-done((bf16[1152,576]{0,1:T(8,128)(2,1)}, bf16[1152,576]{0,1:T(8,128)(2,1)S(1)}, u32[]{:S(2)}, u32[]{:S(2)}) %collective-permute-start.2) | collective-permute-done | bytes 1327136 | tf_op jit(solution)/shard_map/ppermute | solution.py:340
  194.7 3.4 %collective-permute-done.3 = bf16[288,288]{1,0:T(8,128)(2,1)S(1)} collective-permute-done((bf16[288,288]{1,0:T(8,128)(2,1)S(1)}, bf16[288,288]{1,0:T(8,128)(2,1)S(1)}, u32[]{:S(2)}, u32[]{:S(2)}) %collective-permute-start.3) | collective-permute-done | bytes 165920 | tf_op jit(solution)/shard_map/ppermute | solution.py:340
  198.7 5.6 %collective-permute-done.4 = bf16[288,288]{1,0:T(8,128)(2,1)S(1)} collective-permute-done((bf16[288,288]{1,0:T(8,128)(2,1)S(1)}, bf16[288,288]{1,0:T(8,128)(2,1)S(1)}, u32[]{:S(2)}, u32[]{:S(2)}) %collective-permute-start.4) | collective-permute-done | bytes 165920 | tf_op jit(solution)/shard_map/ppermute | solution.py:340
  211.8 10.6 %all-to-all-start.2 = ((bf16[64,16,1152]{2,1,0:T(8,128)(2,1)}), bf16[64,16,1152]{2,1,0:T(8,128)(2,1)S(1)}, u32[]{:S(2)}, u32[]{:S(2)}) async-start(bf16[64,16,1152]{2,1,0:T(8,128)(2,1)} %hold.3), calls=%async_computation.2 | async-start | bytes 4718592 | tf_op jit(solution)/shard_map/all_to_all | solution.py:412
  235.6 9.7 %collective-permute-done.10 = f32[4,18,288]{2,1,0:T(8,128)S(1)} collective-permute-done((f32[4,18,288]{2,1,0:T(8,128)S(1)}, f32[4,18,288]{2,1,0:T(8,128)S(1)}, u32[]{:S(2)}, u32[]{:S(2)}) %collective-permute-start.10) | collective-permute-done | bytes 82976 | tf_op jit(solution)/shard_map/ppermute | solution.py:340
  255.0 3.1 %collective-permute-start.15 = (f32[18,288]{1,0:T(8,128)S(1)}, f32[18,288]{1,0:T(8,128)S(1)}, u32[]{:S(2)}, u32[]{:S(2)}) collective-permute-start(f32[18,288]{1,0:T(8,128)S(1)} %get-tuple-element.67), channel_id=1, source_target_pairs={{0,2},{2,0},{16,18},{18,16},{32,34},{34,32},{48,50},{50,48},{1,3},... | collective-permute-start | bytes 62216 | tf_op jit(solution)/shard_map/ppermute | solution.py:340
  258.4 3.4 %collective-permute-start.17 = (f32[18,288]{1,0:T(8,128)S(1)}, f32[18,288]{1,0:T(8,128)S(1)}, u32[]{:S(2)}, u32[]{:S(2)}) collective-permute-start(f32[18,288]{1,0:T(8,128)S(1)} %get-tuple-element.65), channel_id=1, source_target_pairs={{0,18},{2,16},{16,2},{18,0},{32,50},{34,48},{48,34},{50,32},{1,19}... | collective-permute-start | bytes 62216 | tf_op jit(solution)/shard_map/ppermute | solution.py:340
  261.8 7.4 %collective-permute-start.18 = (f32[18,288]{1,0:T(8,128)S(1)}, f32[18,288]{1,0:T(8,128)S(1)}, u32[]{:S(2)}, u32[]{:S(2)}) collective-permute-start(f32[18,288]{1,0:T(8,128)S(1)} %get-tuple-element.64), channel_id=1, source_target_pairs={{0,32},{2,34},{16,48},{18,50},{32,0},{34,2},{48,16},{50,18},{1,33}... | collective-permute-start | bytes 62216 | tf_op jit(solution)/shard_map/ppermute | solution.py:340
  269.8 4.4 %unpack.2 = (bf16[1,2,256,1152]{3,2,1,0:T(8,128)(2,1)}, bf16[1,2,256,1152]{3,2,1,0:T(8,128)(2,1)}, bf16[1,2,256,1152]{3,2,1,0:T(8,128)(2,1)}, bf16[1,2,256,1152]{3,2,1,0:T(8,128)(2,1)}) custom-call(bf16[256,256]{1,0:T(8,128)(2,1)} %constant.90.clone.order_ref, bf16[64,16,1152]{2,1,0:T(8,128)(2,1)} %all-to-all-done.3.slabs_ref), custom_call_target="tpu_custom_call" | custom-call | flops 603979776 | bytes 4718592 | tf_op jit(solution)/shard_map/unpack/pallas_call | solution.py:253
  277.9 4.8 %all-to-all-done.2.slabs_ref = bf16[64,16,1152]{2,1,0:T(8,128)(2,1)S(1)} async-done(((bf16[64,16,1152]{2,1,0:T(8,128)(2,1)}), bf16[64,16,1152]{2,1,0:T(8,128)(2,1)S(1)}, u32[]{:S(2)}, u32[]{:S(2)}) %all-to-all-start.2) | async-done | bytes 2359328 | tf_op jit(solution)/shard_map/all_to_all | solution.py:412
  284.1 4.4 %unpack.3 = (bf16[1,2,256,1152]{3,2,1,0:T(8,128)(2,1)}, bf16[1,2,256,1152]{3,2,1,0:T(8,128)(2,1)}, bf16[1,2,256,1152]{3,2,1,0:T(8,128)(2,1)}, bf16[1,2,256,1152]{3,2,1,0:T(8,128)(2,1)}) custom-call(bf16[256,256]{1,0:T(8,128)(2,1)} %constant.90.clone.order_ref, ...), custom_call_target="tpu_custom_call", output_to_operand_aliasing={{0}: (2, {}), {1}: (3, {}), {2}: (4, {}), {3}: (5, {})} | custom-call | flops 603979776 | bytes 4718592 | tf_op jit(solution)/shard_map/unpack/pallas_call | solution.py:253
  (88 shorter events, 67.4 us)
Async XLA Ops:
  8.1 11.6 %collective-permute-start = (bf16[18,1152]{1,0:T(8,128)(2,1)S(1)}, bf16[18,1152]{1,0:T(8,128)(2,1)S(1)}, u32[]{:S(2)}, u32[]{:S(2)}) collective-permute-start(bf16[18,1152]{1,0:T(8,128)(2,1)S(1)} %constant_dynamic-slice_fusion), channel_id=1, source_target_pairs={{0,2},{2,0},{1,3},{3,1},{4,6},{6,4},{5,7},{7,5},{8,10},{10,8},{9,1... | collective-permute-start | bytes 124424 | tf_op jit(solution)/shard_map/ppermute | solution.py:340
  20.3 65.3 %all-to-all-start.1 = ((bf16[64,16,1152]{2,1,0:T(8,128)(2,1)}), bf16[64,16,1152]{2,1,0:T(8,128)(2,1)S(1)}, u32[]{:S(2)}, u32[]{:S(2)}) async-start(bf16[64,16,1152]{2,1,0:T(8,128)(2,1)} %hold.2), calls=%async_computation.1 | async-start | bytes 4718592 | tf_op jit(solution)/shard_map/all_to_all | solution.py:412
  29.9 63.9 %all-gather.3.cloned.1.call-start = ((), (), s32[]{:S(2)}) async-start(), calls=%async_computation.4 | async-start | bytes 1880064 | tf_op jit(solution)/shard_map/all_gather | solution.py:390
  87.0 62.1 %all-to-all-start = ((bf16[64,16,1152]{2,1,0:T(8,128)(2,1)}), bf16[64,16,1152]{2,1,0:T(8,128)(2,1)}, u32[]{:S(2)}, u32[]{:S(2)}) async-start(bf16[64,16,1152]{2,1,0:T(8,128)(2,1)} %pack.2), calls=%async_computation | async-start | bytes 4718592 | tf_op jit(solution)/shard_map/all_to_all | solution.py:412
  149.1 62.7 %all-to-all-start.3 = ((bf16[64,16,1152]{2,1,0:T(8,128)(2,1)}), bf16[64,16,1152]{2,1,0:T(8,128)(2,1)}, u32[]{:S(2)}, u32[]{:S(2)}) async-start(bf16[64,16,1152]{2,1,0:T(8,128)(2,1)} %get-tuple-element.42), calls=%async_computation.3 | async-start | bytes 4718592 | tf_op jit(solution)/shard_map/all_to_all | solution.py:412
  187.0 11.1 %collective-permute-start.3 = (bf16[288,288]{1,0:T(8,128)(2,1)S(1)}, bf16[288,288]{1,0:T(8,128)(2,1)S(1)}, u32[]{:S(2)}, u32[]{:S(2)}) collective-permute-start(bf16[288,288]{1,0:T(8,128)(2,1)S(1)} %get-tuple-element.36), channel_id=1, source_target_pairs={{0,64},{64,0},{128,192},{192,128},{1,65},{65,1},{129,193},{193,129... | collective-permute-start | bytes 497672 | tf_op jit(solution)/shard_map/ppermute | solution.py:340
  188.5 15.8 %collective-permute-start.4 = (bf16[288,288]{1,0:T(8,128)(2,1)S(1)}, bf16[288,288]{1,0:T(8,128)(2,1)S(1)}, u32[]{:S(2)}, u32[]{:S(2)}) collective-permute-start(bf16[288,288]{1,0:T(8,128)(2,1)S(1)} %get-tuple-element.37), channel_id=1, source_target_pairs={{0,128},{64,192},{128,0},{192,64},{1,129},{65,193},{129,1},{193,65... | collective-permute-start | bytes 497672 | tf_op jit(solution)/shard_map/ppermute | solution.py:340
  191.4 14.8 %collective-permute-start.5 = (bf16[288,288]{1,0:T(8,128)(2,1)S(1)}, bf16[288,288]{1,0:T(8,128)(2,1)S(1)}, u32[]{:S(2)}, u32[]{:S(2)}) collective-permute-start(bf16[288,288]{1,0:T(8,128)(2,1)S(1)} %get-tuple-element.38), channel_id=1, source_target_pairs={{0,192},{64,128},{128,64},{192,0},{1,193},{65,129},{129,65},{193,1... | collective-permute-start | bytes 497672 | tf_op jit(solution)/shard_map/ppermute | solution.py:340
  191.8 14.5 %collective-permute-start.6 = (bf16[288,288]{1,0:T(8,128)(2,1)S(1)}, bf16[288,288]{1,0:T(8,128)(2,1)S(1)}, u32[]{:S(2)}, u32[]{:S(2)}) collective-permute-start(bf16[288,288]{1,0:T(8,128)(2,1)S(1)} %get-tuple-element.39), channel_id=1, source_target_pairs={{0,4},{4,0},{8,12},{12,8},{1,5},{5,1},{9,13},{13,9},{2,6},{6,2},{1... | collective-permute-start | bytes 497672 | tf_op jit(solution)/shard_map/ppermute | solution.py:340
  192.3 16.1 %collective-permute-start.7 = (bf16[288,288]{1,0:T(8,128)(2,1)S(1)}, bf16[288,288]{1,0:T(8,128)(2,1)S(1)}, u32[]{:S(2)}, u32[]{:S(2)}) collective-permute-start(bf16[288,288]{1,0:T(8,128)(2,1)S(1)} %get-tuple-element.40), channel_id=1, source_target_pairs={{0,8},{4,12},{8,0},{12,4},{1,9},{5,13},{9,1},{13,5},{2,10},{6,14},... | collective-permute-start | bytes 497672 | tf_op jit(solution)/shard_map/ppermute | solution.py:340
  198.1 12.5 %collective-permute-start.8 = (bf16[288,288]{1,0:T(8,128)(2,1)S(1)}, bf16[288,288]{1,0:T(8,128)(2,1)S(1)}, u32[]{:S(2)}, u32[]{:S(2)}) collective-permute-start(bf16[288,288]{1,0:T(8,128)(2,1)S(1)} %get-tuple-element.41), channel_id=1, source_target_pairs={{0,12},{4,8},{8,4},{12,0},{1,13},{5,9},{9,5},{13,1},{2,14},{6,10},... | collective-permute-start | bytes 497672 | tf_op jit(solution)/shard_map/ppermute | solution.py:340
  211.8 70.9 %all-to-all-start.2 = ((bf16[64,16,1152]{2,1,0:T(8,128)(2,1)}), bf16[64,16,1152]{2,1,0:T(8,128)(2,1)S(1)}, u32[]{:S(2)}, u32[]{:S(2)}) async-start(bf16[64,16,1152]{2,1,0:T(8,128)(2,1)} %hold.3), calls=%async_computation.2 | async-start | bytes 4718592 | tf_op jit(solution)/shard_map/all_to_all | solution.py:412
  225.3 20.0 %collective-permute-start.10 = (f32[4,18,288]{2,1,0:T(8,128)S(1)}, f32[4,18,288]{2,1,0:T(8,128)S(1)}, u32[]{:S(2)}, u32[]{:S(2)}) collective-permute-start(f32[4,18,288]{2,1,0:T(8,128)S(1)} %get-tuple-element.57), channel_id=1, source_target_pairs={{0,8},{4,12},{8,0},{12,4},{1,9},{5,13},{9,1},{13,5},{2,10},{6,14},... | collective-permute-start | bytes 248840 | tf_op jit(solution)/shard_map/ppermute | solution.py:340
  227.5 20.8 %collective-permute-start.11 = (f32[4,18,288]{2,1,0:T(8,128)S(1)}, f32[4,18,288]{2,1,0:T(8,128)S(1)}, u32[]{:S(2)}, u32[]{:S(2)}) collective-permute-start(f32[4,18,288]{2,1,0:T(8,128)S(1)} %get-tuple-element.56), channel_id=1, source_target_pairs={{0,12},{4,8},{8,4},{12,0},{1,13},{5,9},{9,5},{13,1},{2,14},{6,10},... | collective-permute-start | bytes 248840 | tf_op jit(solution)/shard_map/ppermute | solution.py:340
  227.5 20.8 %collective-permute-start.9 = (f32[4,18,288]{2,1,0:T(8,128)S(1)}, f32[4,18,288]{2,1,0:T(8,128)S(1)}, u32[]{:S(2)}, u32[]{:S(2)}) collective-permute-start(f32[4,18,288]{2,1,0:T(8,128)S(1)} %get-tuple-element.55), channel_id=1, source_target_pairs={{0,4},{4,0},{8,12},{12,8},{1,5},{5,1},{9,13},{13,9},{2,6},{6,2},{1... | collective-permute-start | bytes 248840 | tf_op jit(solution)/shard_map/ppermute | solution.py:340
  231.2 18.0 %collective-permute-start.12 = (f32[4,18,288]{2,1,0:T(8,128)S(1)}, f32[4,18,288]{2,1,0:T(8,128)S(1)}, u32[]{:S(2)}, u32[]{:S(2)}) collective-permute-start(f32[4,18,288]{2,1,0:T(8,128)S(1)} %get-tuple-element.58), channel_id=1, source_target_pairs={{0,64},{64,0},{128,192},{192,128},{1,65},{65,1},{129,193},{193,129... | collective-permute-start | bytes 248840 | tf_op jit(solution)/shard_map/ppermute | solution.py:340
  232.7 19.5 %collective-permute-start.13 = (f32[4,18,288]{2,1,0:T(8,128)S(1)}, f32[4,18,288]{2,1,0:T(8,128)S(1)}, u32[]{:S(2)}, u32[]{:S(2)}) collective-permute-start(f32[4,18,288]{2,1,0:T(8,128)S(1)} %get-tuple-element.60), channel_id=1, source_target_pairs={{0,128},{64,192},{128,0},{192,64},{1,129},{65,193},{129,1},{193,65... | collective-permute-start | bytes 248840 | tf_op jit(solution)/shard_map/ppermute | solution.py:340
  255.0 19.3 %collective-permute-start.15 = (f32[18,288]{1,0:T(8,128)S(1)}, f32[18,288]{1,0:T(8,128)S(1)}, u32[]{:S(2)}, u32[]{:S(2)}) collective-permute-start(f32[18,288]{1,0:T(8,128)S(1)} %get-tuple-element.67), channel_id=1, source_target_pairs={{0,2},{2,0},{16,18},{18,16},{32,34},{34,32},{48,50},{50,48},{1,3},... | collective-permute-start | bytes 62216 | tf_op jit(solution)/shard_map/ppermute | solution.py:340
  258.1 18.6 %collective-permute-start.16 = (f32[18,288]{1,0:T(8,128)S(1)}, f32[18,288]{1,0:T(8,128)S(1)}, u32[]{:S(2)}, u32[]{:S(2)}) collective-permute-start(f32[18,288]{1,0:T(8,128)S(1)} %get-tuple-element.66), channel_id=1, source_target_pairs={{0,16},{2,18},{16,0},{18,2},{32,48},{34,50},{48,32},{50,34},{1,17}... | collective-permute-start | bytes 62216 | tf_op jit(solution)/shard_map/ppermute | solution.py:340
  258.4 30.1 %collective-permute-start.17 = (f32[18,288]{1,0:T(8,128)S(1)}, f32[18,288]{1,0:T(8,128)S(1)}, u32[]{:S(2)}, u32[]{:S(2)}) collective-permute-start(f32[18,288]{1,0:T(8,128)S(1)} %get-tuple-element.65), channel_id=1, source_target_pairs={{0,18},{2,16},{16,2},{18,0},{32,50},{34,48},{48,34},{50,32},{1,19}... | collective-permute-start | bytes 62216 | tf_op jit(solution)/shard_map/ppermute | solution.py:340
  261.8 26.7 %collective-permute-start.18 = (f32[18,288]{1,0:T(8,128)S(1)}, f32[18,288]{1,0:T(8,128)S(1)}, u32[]{:S(2)}, u32[]{:S(2)}) collective-permute-start(f32[18,288]{1,0:T(8,128)S(1)} %get-tuple-element.64), channel_id=1, source_target_pairs={{0,32},{2,34},{16,48},{18,50},{32,0},{34,2},{48,16},{50,18},{1,33}... | collective-permute-start | bytes 62216 | tf_op jit(solution)/shard_map/ppermute | solution.py:340
  269.2 19.3 %collective-permute-start.19 = (f32[18,288]{1,0:T(8,128)S(1)}, f32[18,288]{1,0:T(8,128)S(1)}, u32[]{:S(2)}, u32[]{:S(2)}) collective-permute-start(f32[18,288]{1,0:T(8,128)S(1)} %get-tuple-element.63), channel_id=1, source_target_pairs={{0,34},{2,32},{16,50},{18,48},{32,2},{34,0},{48,18},{50,16},{1,35}... | collective-permute-start | bytes 62216 | tf_op jit(solution)/shard_map/ppermute | solution.py:340
  274.2 14.3 %collective-permute-start.20 = (f32[18,288]{1,0:T(8,128)S(1)}, f32[18,288]{1,0:T(8,128)S(1)}, u32[]{:S(2)}, u32[]{:S(2)}) collective-permute-start(f32[18,288]{1,0:T(8,128)S(1)} %get-tuple-element.62), channel_id=1, source_target_pairs={{0,48},{2,50},{16,32},{18,34},{32,16},{34,18},{48,0},{50,2},{1,49}... | collective-permute-start | bytes 62216 | tf_op jit(solution)/shard_map/ppermute | solution.py:340
  276.7 11.8 %collective-permute-start.21 = (f32[18,288]{1,0:T(8,128)S(1)}, f32[18,288]{1,0:T(8,128)S(1)}, u32[]{:S(2)}, u32[]{:S(2)}) collective-permute-start(f32[18,288]{1,0:T(8,128)S(1)} %get-tuple-element.61), channel_id=1, source_target_pairs={{0,50},{2,48},{16,34},{18,32},{32,18},{34,16},{48,2},{50,0},{1,51}... | collective-permute-start | bytes 62216 | tf_op jit(solution)/shard_map/ppermute | solution.py:340
  (17 other events, 89.2 us)
Sparse Core Ops, SparseCore 0:
  33.7 53.9 all-gather.2

commit v5 on v4

--- a/solution.py
+++ b/solution.py
@@ -357,27 +357,9 @@
         here = here + swap(sent[k - 1], "y", k).astype(F32)
         there = there + swap(sent[k + 2], "x", k).astype(F32)
     first = [here, there]
-    here = sum(terms_over(here.reshape(4, 4, 18, 288).transpose(1, 0, 2, 3), "x"))
-    there = sum(terms_over(there.reshape(4, 4, 18, 288), "y"))
-    return first, terms_over(jnp.stack([here, there], axis=1).reshape(8, 18, 288), ("zl", "zh"))
-
-
-def add_up_kernel(*refs):
-    total = refs[0][...]
-    for ref in refs[1:8]:
-        total = total + ref[...]
-    refs[-1][...] = total
-
-
-def add_up(terms, token):
-    return pl.pallas_call(
-        add_up_kernel,
-        in_specs=in_vmem(8) + [pl.BlockSpec(memory_space=pl.ANY)],
-        out_specs=pl.BlockSpec(memory_space=pltpu.VMEM),
-        out_shape=jax.ShapeDtypeStruct((18, 288), F32),
-        compiler_params=params(8),
-        name="add_up",
-    )(*terms, token)
+    here = sum(terms_over(here.reshape(4, 4, 18, 288).transpose(1, 0, 2, 3).reshape(4, 72, 288), "x"))
+    there = sum(terms_over(there.reshape(4, 72, 288), "y"))
+    return first, terms_over(jnp.stack([t.reshape(4, 18, 288) for t in (here, there)], axis=1).reshape(8, 18, 288), ("zl", "zh"))
 
 
 def by_rank(axis, own, other):
@@ -423,7 +405,7 @@
     begun, terms = weight_terms(atts, cots)
     outs = unpack(0, exchange(sent[0]), ())
     outs = unpack(1, exchange(hold(sent[1], begun)), outs)
-    return (*outs, add_up(terms, outs[0]).T)
+    return (*outs, sum(terms).T)
 
 
 def solution(mesh):

time: 303 us -> 305 us (level)
  waiting for transfers between devices: 118 us -> 124 us
  local copies, waits for them, and re-layouts: 22.5 us -> 19 us
    ppermute x22, waiting for transfers between devices: 36.1 us -> 47.3 us  [swap(): return lax.ppermute(value, axis, [(i, i ^ k) for i in range(SIZES[axis])])]
    all_to_all x4, waiting for transfers between devices: 81.5 us -> 76.8 us  [exchange(): return lax.all_to_all(t, SEQ, split_axis=0, concat_axis=0, tiled=True)]
    unnamed x28 -> x36, local copies, waits for them, and re-layouts: 10.4 us -> 9.12 us
  transfers between devices with their start and end apart: 27 -> 27, of which waited for: 14 -> 14; matrix products, arithmetic and copies ran while one was open for 7% -> 6% of each run, Pallas kernels for 17% -> 16%
where the time goes in v5:
time: 305 us; the launch traced here: 299 us
  waiting for transfers between devices  124 us (41%)
  starting transfers between devices  80.3 us (26%)
  Pallas kernels  51.3 us (17%)
  local copies, waits for them, and re-layouts  19 us (6%)
  between operations  14.8 us (5%)
  other arithmetic  9.59 us (3%)
    all_to_all x4, waiting for transfers between devices, exchange(): return lax.all_to_all(t, SEQ, split_axis=0, concat_axis=0, tiled=True)  76.8 us
    ppermute x22, waiting for transfers between devices, swap(): return lax.ppermute(value, axis, [(i, i ^ k) for i in range(SIZES[axis])])  47.3 us
    ppermute x22, starting transfers between devices, swap(): return lax.ppermute(value, axis, [(i, i ^ k) for i in range(SIZES[axis])])  47 us
    all_to_all x4, starting transfers between devices, exchange(): return lax.all_to_all(t, SEQ, split_axis=0, concat_axis=0, tiled=True)  33.3 us
    pallas_call x2, Pallas kernels, attend(): pl.pallas_call(attend_kernel, in_specs=in_vmem(2) + in_hbm(1) + in_vmem(1...  28.4 us
    unnamed x36, local copies, waits for them, and re-layouts  9.12 us
    pallas_call x2, Pallas kernels, unpack(): pl.pallas_call(functools.partial(unpack_kernel, part), in_specs=in_vmem(1...  8.8 us
    pallas_call x2, Pallas kernels, pack(): pl.pallas_call(functools.partial(pack_kernel, part), in_specs=in_vmem(1)...  8.77 us
  transfers between devices with their start and end apart: 27, of which 14 were waited for; matrix products, arithmetic and copies ran while one was open for 6% of the time, Pallas kernels for 16%

profile of v5, /device:TPU:2, one launch (start us, length us, event | category | flops | bytes accessed | tf_op | source)
XLA Modules:
  0.0 299.2 jit_solution(14801041536239229178)
XLA Ops:
  8.1 7.3 %collective-permute-start = (bf16[18,1152]{1,0:T(8,128)(2,1)S(1)}, bf16[18,1152]{1,0:T(8,128)(2,1)S(1)}, u32[]{:S(2)}, u32[]{:S(2)}) collective-permute-start(bf16[18,1152]{1,0:T(8,128)(2,1)S(1)} %constant_dynamic-slice_fusion.12), channel_id=1, source_target_pairs={{0,2},{2,0},{1,3},{3,1},{4,6},{6,4},{5,7},{7,5},{8,10},{10,8},{9,1... | collective-permute-start | bytes 124424 | tf_op jit(solution)/shard_map/ppermute | solution.py:340
  15.4 4.3 %pack.3.refs_0_ = bf16[64,16,1152]{2,1,0:T(8,128)(2,1)} custom-call(bf16[256,256]{1,0:T(8,128)(2,1)} %constant.86.clone.order_ref, bf16[1,2,256,1152]{3,2,1,0:T(8,128)(2,1)} %q_ref.3, bf16[1,2,256,1152]{3,2,1,0:T(8,128)(2,1)} %k_ref.3, bf16[1,2,256,1152]{3,2,1,0:T(8,128)(2,1)} %v_ref.3, bf16[1,2,256,1152]{3,2,1,0:T(8,128)(2,1)} %c_ref.3), custom_call_target="tpu_custom_call" | custom-call | flops 603979776 | bytes 4718592 | tf_op jit(solution)/shard_map/pack/pallas_call | solution.py:95
  20.4 9.5 %all-to-all-start.1 = ((bf16[64,16,1152]{2,1,0:T(8,128)(2,1)}), bf16[64,16,1152]{2,1,0:T(8,128)(2,1)S(1)}, u32[]{:S(2)}, u32[]{:S(2)}) async-start(bf16[64,16,1152]{2,1,0:T(8,128)(2,1)} %hold.2), calls=%async_computation.1 | async-start | bytes 4718592 | tf_op jit(solution)/shard_map/all_to_all | solution.py:394
  31.6 4.4 %pack.2 = bf16[64,16,1152]{2,1,0:T(8,128)(2,1)} custom-call(bf16[256,256]{1,0:T(8,128)(2,1)} %constant.86.clone.order_ref, bf16[1,2,256,1152]{3,2,1,0:T(8,128)(2,1)} %q_ref.3, bf16[1,2,256,1152]{3,2,1,0:T(8,128)(2,1)} %k_ref.3, bf16[1,2,256,1152]{3,2,1,0:T(8,128)(2,1)} %v_ref.3, bf16[1,2,256,1152]{3,2,1,0:T(8,128)(2,1)} %c_ref.3), custom_call_target="tpu_custom_call" | custom-call | flops 603979776 | bytes 4718592 | tf_op jit(solution)/shard_map/pack/pallas_call | solution.py:95
  36.0 49.6 %all-to-all-done.1.r_ref = bf16[64,16,1152]{2,1,0:T(8,128)(2,1)S(1)} async-done(((bf16[64,16,1152]{2,1,0:T(8,128)(2,1)}), bf16[64,16,1152]{2,1,0:T(8,128)(2,1)S(1)}, u32[]{:S(2)}, u32[]{:S(2)}) %all-to-all-start.1) | async-done | bytes 2359328 | tf_op jit(solution)/shard_map/all_to_all | solution.py:394
  87.0 6.7 %all-to-all-start = ((bf16[64,16,1152]{2,1,0:T(8,128)(2,1)}), bf16[64,16,1152]{2,1,0:T(8,128)(2,1)}, u32[]{:S(2)}, u32[]{:S(2)}) async-start(bf16[64,16,1152]{2,1,0:T(8,128)(2,1)} %pack.2), calls=%async_computation | async-start | bytes 4718592 | tf_op jit(solution)/shard_map/all_to_all | solution.py:394
  102.0 3.8 %maximum_bitcast_fusion = bf16[2,2,288,1152]{3,0,2,1:T(2,128)(2,1)S(1)} fusion(bf16[1,2,288,1152]{3,1,2,0:T(2,128)(2,1)S(1)} %get-tuple-element.52, bf16[1,2,288,1152]{3,1,2,0:T(2,128)(2,1)S(1)} %get-tuple-element.51), kind=kLoop, calls=%fused_computation | loop fusion | flops 1327104 | bytes 5308416 | tf_op jit(solution)/shard_map/transpose | solution.py:375
  107.6 14.3 %attend.3 = (bf16[64,16,1152]{2,1,0:T(8,128)(2,1)}, bf16[256,1152]{1,0:T(8,128)(2,1)}, bf16[256,1152]{1,0:T(8,128)(2,1)}) custom-call(bf16[256,256]{1,0:T(8,128)(2,1)} %constant.87.clone.order_ref, bf16[256,256]{1,0:T(8,128)(2,1)} %constant.88.clone.back_ref, bf16[64,16,1152]{2,1,0:T(8,128)(2,1)} %copy-done.10, bf16[1152,1152]{1,0:T(8,128)(2,1)} %bitcast.103), custom_call_target="tpu_custom_call" | custom-call | flops 6000000000 | bytes 8552448 | tf_op jit(solution)/shard_map/attend/pallas_call | solution.py:196
  121.9 27.2 %all-to-all-done.r_ref = bf16[64,16,1152]{2,1,0:T(8,128)(2,1)} async-done(((bf16[64,16,1152]{2,1,0:T(8,128)(2,1)}), bf16[64,16,1152]{2,1,0:T(8,128)(2,1)}, u32[]{:S(2)}, u32[]{:S(2)}) %all-to-all-start) | async-done | bytes 2359328 | tf_op jit(solution)/shard_map/all_to_all | solution.py:394
  149.1 6.5 %all-to-all-start.3 = ((bf16[64,16,1152]{2,1,0:T(8,128)(2,1)}), bf16[64,16,1152]{2,1,0:T(8,128)(2,1)}, u32[]{:S(2)}, u32[]{:S(2)}) async-start(bf16[64,16,1152]{2,1,0:T(8,128)(2,1)} %get-tuple-element.42), calls=%async_computation.3 | async-start | bytes 4718592 | tf_op jit(solution)/shard_map/all_to_all | solution.py:394
  155.6 14.0 %attend.2 = (bf16[64,16,1152]{2,1,0:T(8,128)(2,1)}, bf16[256,1152]{1,0:T(8,128)(2,1)}, bf16[256,1152]{1,0:T(8,128)(2,1)}) custom-call(bf16[256,256]{1,0:T(8,128)(2,1)} %constant.87.clone.order_ref, bf16[256,256]{1,0:T(8,128)(2,1)} %constant.88.clone.back_ref, bf16[64,16,1152]{2,1,0:T(8,128)(2,1)} %all-to-all-done.r_ref, bf16[1152,1152]{1,0:T(8,128)(2,1)} %bitcast.104), custom_call_target="tpu_custom_call" | custom-call | flops 6000000000 | bytes 8552448 | tf_op jit(solution)/shard_map/attend/pallas_call | solution.py:196
  171.9 4.7 %outer.1 = (f32[1152,576]{1,0:T(8,128)S(1)}, bf16[1152,576]{1,0:T(8,128)(2,1)S(1)}) custom-call(bf16[1152,1152]{1,0:T(8,128)(2,1)S(1)} %copy-done.2, bf16[256,1152]{1,0:T(8,128)(2,1)S(1)} %copy-done.3, bf16[256,1152]{1,0:T(8,128)(2,1)S(1)} %copy-done.5, bf16[256,1152]{1,0:T(8,128)(2,1)S(1)} %copy-done.4, bf16[256,1152]{1,0:T(8,128)(2,1)S(1)} %copy-done.6), custom_call_target="tpu_custom_call" | custom-call | flops 1358954496 | bytes 6340608 | tf_op jit(solution)/shard_map/outer/pallas_call | solution.py:298
  180.0 3.3 %collective-permute-done.2 = bf16[1152,576]{0,1:T(8,128)(2,1)S(1)} collective-permute-done((bf16[1152,576]{0,1:T(8,128)(2,1)}, bf16[1152,576]{0,1:T(8,128)(2,1)S(1)}, u32[]{:S(2)}, u32[]{:S(2)}) %collective-permute-start.2) | collective-permute-done | bytes 1327136 | tf_op jit(solution)/shard_map/ppermute | solution.py:340
  194.6 3.4 %collective-permute-done.3 = bf16[288,288]{1,0:T(8,128)(2,1)S(1)} collective-permute-done((bf16[288,288]{1,0:T(8,128)(2,1)S(1)}, bf16[288,288]{1,0:T(8,128)(2,1)S(1)}, u32[]{:S(2)}, u32[]{:S(2)}) %collective-permute-start.3) | collective-permute-done | bytes 165920 | tf_op jit(solution)/shard_map/ppermute | solution.py:340
  198.6 5.7 %collective-permute-done.4 = bf16[288,288]{1,0:T(8,128)(2,1)S(1)} collective-permute-done((bf16[288,288]{1,0:T(8,128)(2,1)S(1)}, bf16[288,288]{1,0:T(8,128)(2,1)S(1)}, u32[]{:S(2)}, u32[]{:S(2)}) %collective-permute-start.4) | collective-permute-done | bytes 165920 | tf_op jit(solution)/shard_map/ppermute | solution.py:340
  211.7 10.6 %all-to-all-start.2 = ((bf16[64,16,1152]{2,1,0:T(8,128)(2,1)}), bf16[64,16,1152]{2,1,0:T(8,128)(2,1)S(1)}, u32[]{:S(2)}, u32[]{:S(2)}) async-start(bf16[64,16,1152]{2,1,0:T(8,128)(2,1)} %hold.3), calls=%async_computation.2 | async-start | bytes 4718592 | tf_op jit(solution)/shard_map/all_to_all | solution.py:394
  233.1 9.7 %collective-permute-done.10 = f32[72,288]{1,0:T(8,128)S(1)} collective-permute-done((f32[72,288]{1,0:T(8,128)S(1)}, f32[72,288]{1,0:T(8,128)S(1)}, u32[]{:S(2)}, u32[]{:S(2)}) %collective-permute-start.10) | collective-permute-done | bytes 82976 | tf_op jit(solution)/shard_map/ppermute | solution.py:340
  245.8 3.3 %collective-permute-done.13 = f32[72,288]{1,0:T(8,128)S(1)} collective-permute-done((f32[72,288]{1,0:T(8,128)}, f32[72,288]{1,0:T(8,128)S(1)}, u32[]{:S(2)}, u32[]{:S(2)}) %collective-permute-start.13) | collective-permute-done | bytes 82976 | tf_op jit(solution)/shard_map/ppermute | solution.py:340
  251.8 3.3 %collective-permute-start.15 = (f32[18,288]{1,0:T(8,128)S(1)}, f32[18,288]{1,0:T(8,128)S(1)}, u32[]{:S(2)}, u32[]{:S(2)}) collective-permute-start(f32[18,288]{1,0:T(8,128)S(1)} %bitcast.114), channel_id=1, source_target_pairs={{0,2},{2,0},{16,18},{18,16},{32,34},{34,32},{48,50},{50,48},{1,3},... | collective-permute-start | bytes 62216 | tf_op jit(solution)/shard_map/ppermute | solution.py:340
  255.2 3.5 %collective-permute-start.17 = (f32[18,288]{1,0:T(8,128)S(1)}, f32[18,288]{1,0:T(8,128)S(1)}, u32[]{:S(2)}, u32[]{:S(2)}) collective-permute-start(f32[18,288]{1,0:T(8,128)S(1)} %bitcast.111), channel_id=1, source_target_pairs={{0,18},{2,16},{16,2},{18,0},{32,50},{34,48},{48,34},{50,32},{1,19}... | collective-permute-start | bytes 62216 | tf_op jit(solution)/shard_map/ppermute | solution.py:340
  258.7 7.8 %collective-permute-start.18 = (f32[18,288]{1,0:T(8,128)S(1)}, f32[18,288]{1,0:T(8,128)S(1)}, u32[]{:S(2)}, u32[]{:S(2)}) collective-permute-start(f32[18,288]{1,0:T(8,128)S(1)} %bitcast.113), channel_id=1, source_target_pairs={{0,32},{2,34},{16,48},{18,50},{32,0},{34,2},{48,16},{50,18},{1,33}... | collective-permute-start | bytes 62216 | tf_op jit(solution)/shard_map/ppermute | solution.py:340
  270.8 10.3 %collective-permute-done.17 = f32[18,288]{1,0:T(8,128)S(1)} collective-permute-done((f32[18,288]{1,0:T(8,128)S(1)}, f32[18,288]{1,0:T(8,128)S(1)}, u32[]{:S(2)}, u32[]{:S(2)}) %collective-permute-start.17) | collective-permute-done | bytes 20768 | tf_op jit(solution)/shard_map/ppermute | solution.py:340
  281.9 4.4 %unpack.2 = (bf16[1,2,256,1152]{3,2,1,0:T(8,128)(2,1)}, bf16[1,2,256,1152]{3,2,1,0:T(8,128)(2,1)}, bf16[1,2,256,1152]{3,2,1,0:T(8,128)(2,1)}, bf16[1,2,256,1152]{3,2,1,0:T(8,128)(2,1)}) custom-call(bf16[256,256]{1,0:T(8,128)(2,1)} %constant.90.clone.order_ref, bf16[64,16,1152]{2,1,0:T(8,128)(2,1)} %all-to-all-done.3.slabs_ref), custom_call_target="tpu_custom_call" | custom-call | flops 603979776 | bytes 4718592 | tf_op jit(solution)/shard_map/unpack/pallas_call | solution.py:253
  287.7 4.4 %unpack.3 = (bf16[1,2,256,1152]{3,2,1,0:T(8,128)(2,1)}, bf16[1,2,256,1152]{3,2,1,0:T(8,128)(2,1)}, bf16[1,2,256,1152]{3,2,1,0:T(8,128)(2,1)}, bf16[1,2,256,1152]{3,2,1,0:T(8,128)(2,1)}) custom-call(bf16[256,256]{1,0:T(8,128)(2,1)} %constant.90.clone.order_ref, ...), custom_call_target="tpu_custom_call", output_to_operand_aliasing={{0}: (2, {}), {1}: (3, {}), {2}: (4, {}), {3}: (5, {})} | custom-call | flops 603979776 | bytes 4718592 | tf_op jit(solution)/shard_map/unpack/pallas_call | solution.py:253
  (100 shorter events, 62.3 us)
Async XLA Ops:
  8.1 11.6 %collective-permute-start = (bf16[18,1152]{1,0:T(8,128)(2,1)S(1)}, bf16[18,1152]{1,0:T(8,128)(2,1)S(1)}, u32[]{:S(2)}, u32[]{:S(2)}) collective-permute-start(bf16[18,1152]{1,0:T(8,128)(2,1)S(1)} %constant_dynamic-slice_fusion.12), channel_id=1, source_target_pairs={{0,2},{2,0},{1,3},{3,1},{4,6},{6,4},{5,7},{7,5},{8,10},{10,8},{9,1... | collective-permute-start | bytes 124424 | tf_op jit(solution)/shard_map/ppermute | solution.py:340
  20.4 65.3 %all-to-all-start.1 = ((bf16[64,16,1152]{2,1,0:T(8,128)(2,1)}), bf16[64,16,1152]{2,1,0:T(8,128)(2,1)S(1)}, u32[]{:S(2)}, u32[]{:S(2)}) async-start(bf16[64,16,1152]{2,1,0:T(8,128)(2,1)} %hold.2), calls=%async_computation.1 | async-start | bytes 4718592 | tf_op jit(solution)/shard_map/all_to_all | solution.py:394
  29.9 63.9 %all-gather.3.cloned.1.call-start = ((), (), s32[]{:S(2)}) async-start(), calls=%async_computation.4 | async-start | bytes 1880064 | tf_op jit(solution)/shard_map/all_gather | solution.py:372
  87.0 62.1 %all-to-all-start = ((bf16[64,16,1152]{2,1,0:T(8,128)(2,1)}), bf16[64,16,1152]{2,1,0:T(8,128)(2,1)}, u32[]{:S(2)}, u32[]{:S(2)}) async-start(bf16[64,16,1152]{2,1,0:T(8,128)(2,1)} %pack.2), calls=%async_computation | async-start | bytes 4718592 | tf_op jit(solution)/shard_map/all_to_all | solution.py:394
  149.1 62.6 %all-to-all-start.3 = ((bf16[64,16,1152]{2,1,0:T(8,128)(2,1)}), bf16[64,16,1152]{2,1,0:T(8,128)(2,1)}, u32[]{:S(2)}, u32[]{:S(2)}) async-start(bf16[64,16,1152]{2,1,0:T(8,128)(2,1)} %get-tuple-element.42), calls=%async_computation.3 | async-start | bytes 4718592 | tf_op jit(solution)/shard_map/all_to_all | solution.py:394
  186.9 11.1 %collective-permute-start.3 = (bf16[288,288]{1,0:T(8,128)(2,1)S(1)}, bf16[288,288]{1,0:T(8,128)(2,1)S(1)}, u32[]{:S(2)}, u32[]{:S(2)}) collective-permute-start(bf16[288,288]{1,0:T(8,128)(2,1)S(1)} %get-tuple-element.36), channel_id=1, source_target_pairs={{0,64},{64,0},{128,192},{192,128},{1,65},{65,1},{129,193},{193,129... | collective-permute-start | bytes 497672 | tf_op jit(solution)/shard_map/ppermute | solution.py:340
  188.5 15.9 %collective-permute-start.4 = (bf16[288,288]{1,0:T(8,128)(2,1)S(1)}, bf16[288,288]{1,0:T(8,128)(2,1)S(1)}, u32[]{:S(2)}, u32[]{:S(2)}) collective-permute-start(bf16[288,288]{1,0:T(8,128)(2,1)S(1)} %get-tuple-element.37), channel_id=1, source_target_pairs={{0,128},{64,192},{128,0},{192,64},{1,129},{65,193},{129,1},{193,65... | collective-permute-start | bytes 497672 | tf_op jit(solution)/shard_map/ppermute | solution.py:340
  191.3 14.8 %collective-permute-start.5 = (bf16[288,288]{1,0:T(8,128)(2,1)S(1)}, bf16[288,288]{1,0:T(8,128)(2,1)S(1)}, u32[]{:S(2)}, u32[]{:S(2)}) collective-permute-start(bf16[288,288]{1,0:T(8,128)(2,1)S(1)} %get-tuple-element.38), channel_id=1, source_target_pairs={{0,192},{64,128},{128,64},{192,0},{1,193},{65,129},{129,65},{193,1... | collective-permute-start | bytes 497672 | tf_op jit(solution)/shard_map/ppermute | solution.py:340
  191.7 14.5 %collective-permute-start.6 = (bf16[288,288]{1,0:T(8,128)(2,1)S(1)}, bf16[288,288]{1,0:T(8,128)(2,1)S(1)}, u32[]{:S(2)}, u32[]{:S(2)}) collective-permute-start(bf16[288,288]{1,0:T(8,128)(2,1)S(1)} %get-tuple-element.39), channel_id=1, source_target_pairs={{0,4},{4,0},{8,12},{12,8},{1,5},{5,1},{9,13},{13,9},{2,6},{6,2},{1... | collective-permute-start | bytes 497672 | tf_op jit(solution)/shard_map/ppermute | solution.py:340
  192.2 16.1 %collective-permute-start.7 = (bf16[288,288]{1,0:T(8,128)(2,1)S(1)}, bf16[288,288]{1,0:T(8,128)(2,1)S(1)}, u32[]{:S(2)}, u32[]{:S(2)}) collective-permute-start(bf16[288,288]{1,0:T(8,128)(2,1)S(1)} %get-tuple-element.40), channel_id=1, source_target_pairs={{0,8},{4,12},{8,0},{12,4},{1,9},{5,13},{9,1},{13,5},{2,10},{6,14},... | collective-permute-start | bytes 497672 | tf_op jit(solution)/shard_map/ppermute | solution.py:340
  198.0 12.6 %collective-permute-start.8 = (bf16[288,288]{1,0:T(8,128)(2,1)S(1)}, bf16[288,288]{1,0:T(8,128)(2,1)S(1)}, u32[]{:S(2)}, u32[]{:S(2)}) collective-permute-start(bf16[288,288]{1,0:T(8,128)(2,1)S(1)} %get-tuple-element.41), channel_id=1, source_target_pairs={{0,12},{4,8},{8,4},{12,0},{1,13},{5,9},{9,5},{13,1},{2,14},{6,10},... | collective-permute-start | bytes 497672 | tf_op jit(solution)/shard_map/ppermute | solution.py:340
  211.7 74.5 %all-to-all-start.2 = ((bf16[64,16,1152]{2,1,0:T(8,128)(2,1)}), bf16[64,16,1152]{2,1,0:T(8,128)(2,1)S(1)}, u32[]{:S(2)}, u32[]{:S(2)}) async-start(bf16[64,16,1152]{2,1,0:T(8,128)(2,1)} %hold.3), calls=%async_computation.2 | async-start | bytes 4718592 | tf_op jit(solution)/shard_map/all_to_all | solution.py:394
  223.0 19.8 %collective-permute-start.10 = (f32[72,288]{1,0:T(8,128)S(1)}, f32[72,288]{1,0:T(8,128)S(1)}, u32[]{:S(2)}, u32[]{:S(2)}) collective-permute-start(f32[72,288]{1,0:T(8,128)S(1)} %bitcast.110), channel_id=1, source_target_pairs={{0,8},{4,12},{8,0},{12,4},{1,9},{5,13},{9,1},{13,5},{2,10},{6,14},... | collective-permute-start | bytes 248840 | tf_op jit(solution)/shard_map/ppermute | solution.py:340
  225.2 20.6 %collective-permute-start.11 = (f32[72,288]{1,0:T(8,128)S(1)}, f32[72,288]{1,0:T(8,128)S(1)}, u32[]{:S(2)}, u32[]{:S(2)}) collective-permute-start(f32[72,288]{1,0:T(8,128)S(1)} %bitcast.108), channel_id=1, source_target_pairs={{0,12},{4,8},{8,4},{12,0},{1,13},{5,9},{9,5},{13,1},{2,14},{6,10},... | collective-permute-start | bytes 248840 | tf_op jit(solution)/shard_map/ppermute | solution.py:340
  225.3 20.5 %collective-permute-start.9 = (f32[72,288]{1,0:T(8,128)S(1)}, f32[72,288]{1,0:T(8,128)S(1)}, u32[]{:S(2)}, u32[]{:S(2)}) collective-permute-start(f32[72,288]{1,0:T(8,128)S(1)} %bitcast.109), channel_id=1, source_target_pairs={{0,4},{4,0},{8,12},{12,8},{1,5},{5,1},{9,13},{13,9},{2,6},{6,2},{1... | collective-permute-start | bytes 248840 | tf_op jit(solution)/shard_map/ppermute | solution.py:340
  228.7 17.1 %collective-permute-start.12 = (f32[72,288]{1,0:T(8,128)}, f32[72,288]{1,0:T(8,128)S(1)}, u32[]{:S(2)}, u32[]{:S(2)}) collective-permute-start(f32[72,288]{1,0:T(8,128)} %get-tuple-element.59), channel_id=1, source_target_pairs={{0,64},{64,0},{128,192},{192,128},{1,65},{65,1},{129,193},{193,129... | collective-permute-start | bytes 248840 | tf_op jit(solution)/shard_map/ppermute | solution.py:340
  230.2 19.0 %collective-permute-start.13 = (f32[72,288]{1,0:T(8,128)}, f32[72,288]{1,0:T(8,128)S(1)}, u32[]{:S(2)}, u32[]{:S(2)}) collective-permute-start(f32[72,288]{1,0:T(8,128)} %get-tuple-element.61), channel_id=1, source_target_pairs={{0,128},{64,192},{128,0},{192,64},{1,129},{65,193},{129,1},{193,65... | collective-permute-start | bytes 248840 | tf_op jit(solution)/shard_map/ppermute | solution.py:340
  251.8 15.4 %collective-permute-start.15 = (f32[18,288]{1,0:T(8,128)S(1)}, f32[18,288]{1,0:T(8,128)S(1)}, u32[]{:S(2)}, u32[]{:S(2)}) collective-permute-start(f32[18,288]{1,0:T(8,128)S(1)} %bitcast.114), channel_id=1, source_target_pairs={{0,2},{2,0},{16,18},{18,16},{32,34},{34,32},{48,50},{50,48},{1,3},... | collective-permute-start | bytes 62216 | tf_op jit(solution)/shard_map/ppermute | solution.py:340
  255.2 14.6 %collective-permute-start.16 = (f32[18,288]{1,0:T(8,128)S(1)}, f32[18,288]{1,0:T(8,128)S(1)}, u32[]{:S(2)}, u32[]{:S(2)}) collective-permute-start(f32[18,288]{1,0:T(8,128)S(1)} %bitcast.112), channel_id=1, source_target_pairs={{0,16},{2,18},{16,0},{18,2},{32,48},{34,50},{48,32},{50,34},{1,17}... | collective-permute-start | bytes 62216 | tf_op jit(solution)/shard_map/ppermute | solution.py:340
  255.2 25.9 %collective-permute-start.17 = (f32[18,288]{1,0:T(8,128)S(1)}, f32[18,288]{1,0:T(8,128)S(1)}, u32[]{:S(2)}, u32[]{:S(2)}) collective-permute-start(f32[18,288]{1,0:T(8,128)S(1)} %bitcast.111), channel_id=1, source_target_pairs={{0,18},{2,16},{16,2},{18,0},{32,50},{34,48},{48,34},{50,32},{1,19}... | collective-permute-start | bytes 62216 | tf_op jit(solution)/shard_map/ppermute | solution.py:340
  258.7 22.5 %collective-permute-start.18 = (f32[18,288]{1,0:T(8,128)S(1)}, f32[18,288]{1,0:T(8,128)S(1)}, u32[]{:S(2)}, u32[]{:S(2)}) collective-permute-start(f32[18,288]{1,0:T(8,128)S(1)} %bitcast.113), channel_id=1, source_target_pairs={{0,32},{2,34},{16,48},{18,50},{32,0},{34,2},{48,16},{50,18},{1,33}... | collective-permute-start | bytes 62216 | tf_op jit(solution)/shard_map/ppermute | solution.py:340
  266.4 14.8 %collective-permute-start.19 = (f32[18,288]{1,0:T(8,128)S(1)}, f32[18,288]{1,0:T(8,128)S(1)}, u32[]{:S(2)}, u32[]{:S(2)}) collective-permute-start(f32[18,288]{1,0:T(8,128)S(1)} %bitcast.115), channel_id=1, source_target_pairs={{0,34},{2,32},{16,50},{18,48},{32,2},{34,0},{48,18},{50,16},{1,35}... | collective-permute-start | bytes 62216 | tf_op jit(solution)/shard_map/ppermute | solution.py:340
  267.2 14.0 %collective-permute-start.20 = (f32[18,288]{1,0:T(8,128)S(1)}, f32[18,288]{1,0:T(8,128)S(1)}, u32[]{:S(2)}, u32[]{:S(2)}) collective-permute-start(f32[18,288]{1,0:T(8,128)S(1)} %bitcast.117), channel_id=1, source_target_pairs={{0,48},{2,50},{16,32},{18,34},{32,16},{34,18},{48,0},{50,2},{1,49}... | collective-permute-start | bytes 62216 | tf_op jit(solution)/shard_map/ppermute | solution.py:340
  269.7 11.5 %collective-permute-start.21 = (f32[18,288]{1,0:T(8,128)S(1)}, f32[18,288]{1,0:T(8,128)S(1)}, u32[]{:S(2)}, u32[]{:S(2)}) collective-permute-start(f32[18,288]{1,0:T(8,128)S(1)} %bitcast.116), channel_id=1, source_target_pairs={{0,50},{2,48},{16,34},{18,32},{32,18},{34,16},{48,2},{50,0},{1,51}... | collective-permute-start | bytes 62216 | tf_op jit(solution)/shard_map/ppermute | solution.py:340
  (16 other events, 92.1 us)
Sparse Core Ops, SparseCore 0:
  33.7 53.9 all-gather.2
